TPU v7x, 32 devices: a whole 2x2x4 slice. The times are simulated.
32 devices in a mesh: row: 4 (over y, core), col: 8 (over z, x).
Axes of the slice: x: 2, y: 2, z: 4, core: 2. Of those that a mesh axis runs over, the one named last changes fastest.
Arguments:
- features: bfloat16 [6, 32, 32, 512], P(None, 'row', 'col'), may hold values from -13 to 13
- priors: bfloat16 [2, 6, 32, 32, 512], P(None, None, 'row', 'col'), may hold values from 0 to 13
- domain: int32 [6], replicated, may hold values from 0 to 1, as said below
- shared_w: bfloat16 [3, 3, 3, 512, 512], replicated, may hold values from -0.09375 to 0.09375
- shared_gain: float32 [3, 512], replicated, may hold values from 0.5 to 1.5
- shared_bias: float32 [3, 512], replicated, may hold values from -3 to 3
- first_w: bfloat16 [2, 1024, 512], replicated, may hold values from -0.1875 to 0.1875
- second_w: bfloat16 [2, 512, 512], replicated, may hold values from -0.25 to 0.25
- task_conv: bfloat16 [2, 3, 3, 512, 512], replicated, may hold values from -0.09375 to 0.09375
- task_gain: float32 [2, 3, 512], replicated, may hold values from 0.5 to 1.5
- task_bias: float32 [2, 3, 512], replicated, may hold values from -3 to 3
- shared_cot: bfloat16 [6, 16, 16, 512], P(None, 'row', 'col'), may hold values from -6 to 6
- task_cot: bfloat16 [2, 6, 16, 16, 512], P(None, None, 'row', 'col'), may hold values from -6 to 6
Outputs:
- shared_out: bfloat16 [6, 16, 16, 512], P(None, 'row', 'col')
- task_out: bfloat16 [2, 6, 16, 16, 512], P(None, None, 'row', 'col')
- grad_features: float32 [6, 32, 32, 512], P(None, 'row', 'col')
- grad_priors: float32 [2, 6, 32, 32, 512], P(None, None, 'row', 'col')
- grad_shared_w: float32 [3, 3, 3, 512, 512], replicated
- grad_shared_gain: float32 [3, 512], replicated
- grad_shared_bias: float32 [3, 512], replicated
- grad_first_w: float32 [2, 1024, 512], replicated
- grad_second_w: float32 [2, 512, 512], replicated
- grad_task_conv: float32 [2, 3, 3, 512, 512], replicated
- grad_task_gain: float32 [2, 3, 512], replicated
- grad_task_bias: float32 [2, 3, 512], replicated
Inputs may be any that keep to these rules, and one draw needn't show every extreme that they name: `domain`: every one of the 2 domains names at least one image.
All inputs are finite; a program needn't handle non-finite values.
Results may differ from a plain program's by a relative error of at most 0.015.
Values may be sent and summed in bfloat16 or wider, within the bound.
No kernel may reach another device: no remote copies, remote signals or barrier semaphores. Data moves between devices by JAX's collectives and lax.ppermute only.
A program may use at most 256 MiB of HBM per device.

v0:
```python
import jax
import jax.numpy as jnp
from jax import lax
from jax.sharding import PartitionSpec as P

TASKS = 2
CONVS = 3
DOMAINS = 2


EPSILON = 1e-05
HIGHEST = lax.Precision.HIGHEST


def with_halo(shard, sides, width):
    for axis, dim in sides:
        count, length = (lax.axis_size(axis), shard.shape[dim])
        up = [(i, (i + 1) % count) for i in range(count - 1)]
        down = [(j, i) for i, j in up]
        last = lax.slice_in_dim(shard, length - width, length, axis=dim)
        leading = lax.slice_in_dim(shard, 0, width, axis=dim)
        before = lax.ppermute(last, axis, up)
        after = lax.ppermute(leading, axis, down)
        shard = jnp.concatenate([before, shard, after], axis=dim)
    return shard


def surround(tile):
    return with_halo(tile, (("row", 1), ("col", 2)), 1)


def surround_grads(tile):
    return with_halo(tile, (("row", 1), ("col", 2)), 1)


def convolve(padded, kernel):
    return lax.conv_general_dilated(
        padded,
        kernel,
        (1, 1),
        "VALID",
        dimension_numbers=("NHWC", "HWIO", "NHWC"),
        preferred_element_type=jnp.float32,
    )


def convolve_back(padded_grad, kernel):
    flipped = jnp.flip(kernel, (0, 1))
    return lax.conv_general_dilated(
        padded_grad,
        flipped,
        (1, 1),
        "VALID",
        dimension_numbers=("NHWC", "HWOI", "NHWC"),
        preferred_element_type=jnp.float32,
    )


def kernel_grad(padded, grad_out):
    return lax.conv_general_dilated(
        padded,
        grad_out,
        (1, 1),
        "VALID",
        dimension_numbers=("CHWN", "IHWO", "HWNC"),
        preferred_element_type=jnp.float32,
    )


def project(values, weight):
    return jnp.einsum("bhwc,cd->bhwd", values, weight, preferred_element_type=jnp.float32)


def silu_slope(pre_act):
    logistic = jax.nn.sigmoid(pre_act)
    return logistic * (1.0 + pre_act * (1.0 - logistic))


def domain_totals(member, values):
    return jnp.dot(member.T, jnp.sum(values, axis=(1, 2)), precision=HIGHEST)


def per_image(member, stats):
    return jnp.dot(member, stats, precision=HIGHEST)[:, None, None, :]


def norm_forward(product, norm_gain, norm_bias, member, counts):
    totals = lax.psum(domain_totals(member, product), ("row", "col"))
    average = totals / counts[:, None]
    centered = product - per_image(member, average)
    spread = lax.psum(domain_totals(member, centered * centered), ("row", "col")) / counts[:, None]
    inverse = lax.rsqrt(spread + EPSILON)
    normal_form = centered * per_image(member, inverse)
    return (normal_form, inverse, normal_form * norm_gain + norm_bias)


def norm_backward(grad_out, normal_form, inverse, norm_gain, member, counts):
    scaled = grad_out * norm_gain
    sum_plain, sum_cross, gain_grad, bias_grad = lax.psum(
        (
            domain_totals(member, scaled),
            domain_totals(member, scaled * normal_form),
            jnp.sum(grad_out * normal_form, axis=(0, 1, 2)),
            jnp.sum(grad_out, axis=(0, 1, 2)),
        ),
        ("row", "col"),
    )
    plain_mean = per_image(member, sum_plain / counts[:, None])
    cross_mean = per_image(member, sum_cross / counts[:, None])
    grad_in = per_image(member, inverse) * (scaled - plain_mean - normal_form * cross_mean)
    return (grad_in, gain_grad, bias_grad)


def mean_pool(values):
    images, height, breadth, channels = values.shape
    return jnp.mean(values.reshape(images, height // 2, 2, breadth // 2, 2, channels), axis=(2, 4))


def mean_pool_back(grad_out):
    images, half_h, half_w, channels = grad_out.shape
    spread_out = jnp.broadcast_to(
        0.25 * grad_out[:, :, None, :, None, :], (images, half_h, 2, half_w, 2, channels)
    )
    return spread_out.reshape(images, 2 * half_h, 2 * half_w, channels)


def body(
    features,
    priors,
    domain,
    shared_w,
    shared_gain,
    shared_bias,
    first_w,
    second_w,
    task_conv,
    task_gain,
    task_bias,
    shared_cot,
    task_cot,
):
    images, height, breadth, channels = features.shape
    member = (domain[:, None] == jnp.arange(DOMAINS, dtype=jnp.int32)[None, :]).astype(jnp.float32)
    pixels = height * lax.axis_size("row") * breadth * lax.axis_size("col")
    counts = jnp.sum(member, axis=0) * pixels
    shared_keep = []
    activations = []
    current = features
    for conv_index in range(CONVS):
        padded = surround(current)
        product = convolve(padded, shared_w[conv_index])
        normal_form, inverse, normed = norm_forward(
            product, shared_gain[conv_index], shared_bias[conv_index], member, counts
        )
        current = jax.nn.silu(normed)
        if conv_index + 1 < CONVS:
            current = current.astype(jnp.bfloat16)
        shared_keep.append((padded, normal_form, inverse, normed))
        activations.append(current)
    first_act = activations[0]
    last_act = activations[-1]
    shared_out = mean_pool(last_act).astype(jnp.bfloat16)
    task_keep = []
    task_outs = []
    for task_index in range(TASKS):
        hidden = project(first_act, first_w[task_index, :channels]) + project(
            priors[task_index], first_w[task_index, channels:]
        )
        hidden_form, hidden_inverse, hidden_normed = norm_forward(
            hidden, task_gain[task_index, 0], task_bias[task_index, 0], member, counts
        )
        hidden_act = jax.nn.silu(hidden_normed).astype(jnp.bfloat16)
        gate_pre = project(hidden_act, second_w[task_index])
        gate_form, gate_inverse, gate_normed = norm_forward(
            gate_pre, task_gain[task_index, 1], task_bias[task_index, 1], member, counts
        )
        attention = jax.nn.sigmoid(gate_normed)
        padded_masked = surround((attention * last_act).astype(jnp.bfloat16))
        refined = convolve(padded_masked, task_conv[task_index])
        refined_form, refined_inverse, refined_normed = norm_forward(
            refined, task_gain[task_index, 2], task_bias[task_index, 2], member, counts
        )
        task_outs.append(mean_pool(jax.nn.silu(refined_normed)).astype(jnp.bfloat16))
        task_keep.append(
            (
                (hidden_form, hidden_inverse, hidden_normed),
                hidden_act,
                (gate_form, gate_inverse),
                attention,
                padded_masked,
                (refined_form, refined_inverse, refined_normed),
            )
        )
    grad_last = mean_pool_back(shared_cot.astype(jnp.float32))
    grad_first = jnp.zeros(first_act.shape, jnp.float32)
    first_grads = []
    second_grads = []
    refine_grads = []
    prior_grads = []
    task_gain_grads = []
    task_bias_grads = []
    for task_index in range(TASKS):
        hidden_keep, hidden_act, gate_keep, attention, padded_masked, refined_keep = task_keep[
            task_index
        ]
        grad_refined = mean_pool_back(task_cot[task_index].astype(jnp.float32)) * silu_slope(
            refined_keep[2]
        )
        grad_in, gain_two, bias_two = norm_backward(
            grad_refined, refined_keep[0], refined_keep[1], task_gain[task_index, 2], member, counts
        )
        rounded = grad_in.astype(jnp.bfloat16)
        grad_masked = convolve_back(surround_grads(rounded), task_conv[task_index])
        refine_grads.append(kernel_grad(padded_masked, rounded))
        grad_last = grad_last + grad_masked * attention
        grad_gate = grad_masked * last_act * attention * (1.0 - attention)
        grad_in, gain_one, bias_one = norm_backward(
            grad_gate, gate_keep[0], gate_keep[1], task_gain[task_index, 1], member, counts
        )
        rounded = grad_in.astype(jnp.bfloat16)
        second_grads.append(
            jnp.einsum("bhwc,bhwd->cd", hidden_act, rounded, preferred_element_type=jnp.float32)
        )
        grad_hidden = jnp.einsum(
            "bhwd,cd->bhwc", rounded, second_w[task_index], preferred_element_type=jnp.float32
        )
        grad_hidden = grad_hidden * silu_slope(hidden_keep[2])
        grad_in, gain_zero, bias_zero = norm_backward(
            grad_hidden, hidden_keep[0], hidden_keep[1], task_gain[task_index, 0], member, counts
        )
        rounded = grad_in.astype(jnp.bfloat16)
        first_grads.append(
            jnp.concatenate(
                [
                    jnp.einsum(
                        "bhwc,bhwd->cd", first_act, rounded, preferred_element_type=jnp.float32
                    ),
                    jnp.einsum(
                        "bhwc,bhwd->cd",
                        priors[task_index],
                        rounded,
                        preferred_element_type=jnp.float32,
                    ),
                ],
                axis=0,
            )
        )
        grad_first = grad_first + jnp.einsum(
            "bhwd,cd->bhwc",
            rounded,
            first_w[task_index, :channels],
            preferred_element_type=jnp.float32,
        )
        prior_grads.append(
            jnp.einsum(
                "bhwd,cd->bhwc",
                rounded,
                first_w[task_index, channels:],
                preferred_element_type=jnp.float32,
            )
        )
        task_gain_grads.append(jnp.stack([gain_zero, gain_one, gain_two]))
        task_bias_grads.append(jnp.stack([bias_zero, bias_one, bias_two]))
    task_flat = (
        jnp.stack(first_grads).reshape(-1, channels * channels),
        jnp.stack(second_grads).reshape(-1, channels * channels),
        jnp.stack(refine_grads).reshape(-1, channels * channels),
    )
    shared_kernels = [None] * CONVS
    shared_gain_grads = [None] * CONVS
    shared_bias_grads = [None] * CONVS
    grad_act = grad_last
    for conv_index in reversed(range(CONVS)):
        padded, normal_form, inverse, normed = shared_keep[conv_index]
        if conv_index == 0:
            grad_act = grad_act + grad_first
        grad_act = grad_act * silu_slope(normed)
        grad_in, gain_grad, bias_grad = norm_backward(
            grad_act, normal_form, inverse, shared_gain[conv_index], member, counts
        )
        rounded = grad_in.astype(jnp.bfloat16)
        grad_act = convolve_back(surround_grads(rounded), shared_w[conv_index])
        shared_kernels[conv_index] = kernel_grad(padded, rounded)
        shared_gain_grads[conv_index] = gain_grad
        shared_bias_grads[conv_index] = bias_grad
    shared_flat = jnp.stack(shared_kernels).reshape(-1, channels * channels)
    all_parts = (
        lax.psum_scatter(task_flat[0], ("row", "col"), scatter_dimension=1, tiled=True),
        lax.psum_scatter(task_flat[1], ("row", "col"), scatter_dimension=1, tiled=True),
        lax.psum_scatter(task_flat[2], ("row", "col"), scatter_dimension=1, tiled=True),
        lax.psum_scatter(shared_flat, ("row", "col"), scatter_dimension=1, tiled=True),
    )
    all_whole = (
        lax.all_gather(
            all_parts[0].astype(jnp.bfloat16), ("row", "col"), axis=1, tiled=True
        ).astype(jnp.float32),
        lax.all_gather(
            all_parts[1].astype(jnp.bfloat16), ("row", "col"), axis=1, tiled=True
        ).astype(jnp.float32),
        lax.all_gather(
            all_parts[2].astype(jnp.bfloat16), ("row", "col"), axis=1, tiled=True
        ).astype(jnp.float32),
        lax.all_gather(
            all_parts[3].astype(jnp.bfloat16), ("row", "col"), axis=1, tiled=True
        ).astype(jnp.float32),
    )
    task_whole = (all_whole[0], all_whole[1], all_whole[2])
    shared_whole = all_whole[3]
    return (
        shared_out,
        jnp.stack(task_outs),
        grad_act,
        jnp.stack(prior_grads),
        shared_whole.reshape(shared_w.shape),
        jnp.stack(shared_gain_grads),
        jnp.stack(shared_bias_grads),
        task_whole[0].reshape(first_w.shape),
        task_whole[1].reshape(second_w.shape),
        task_whole[2].reshape(task_conv.shape),
        jnp.stack(task_gain_grads),
        jnp.stack(task_bias_grads),
    )


def solution(mesh):
    return jax.shard_map(
        body,
        mesh=mesh,
        in_specs=(
            P(None, "row", "col", None),
            P(None, None, "row", "col", None),
            P(),
            P(),
            P(),
            P(),
            P(),
            P(),
            P(),
            P(),
            P(),
            P(None, "row", "col", None),
            P(None, None, "row", "col", None),
        ),
        out_specs=(
            P(None, "row", "col", None),
            P(None, None, "row", "col", None),
            P(None, "row", "col", None),
            P(None, None, "row", "col", None),
            P(),
            P(),
            P(),
            P(),
            P(),
            P(),
            P(),
            P(),
        ),
        check_vma=False,
    )
```

profile of v0, /device:TPU:0, one launch (start us, length us, event | category | flops | bytes accessed | tf_op | source)
XLA Modules:
  0.0 2284.0 jit_solution(15634113704539423353)
XLA Ops:
  36.4 43.9 %psum.378 = f32[2,512]{1,0:T(2,128)S(1)} all-reduce(f32[2,512]{1,0:T(2,128)S(1)} %fusion.306), channel_id=1, replica_groups=mesh['row'=4,'col'=8] {'row','col'}, use_global_device_ids=true, to_apply=%region_1.0 | all-reduce | flops 1024 | bytes 8192 | tf_op jit(solution)/shard_map/psum | solution.py:88
  80.7 41.5 %psum.379 = f32[2,512]{1,0:T(2,128)S(1)} all-reduce(f32[2,512]{1,0:T(2,128)S(1)} %fusion.305), channel_id=1, replica_groups=mesh['row'=4,'col'=8] {'row','col'}, use_global_device_ids=true, to_apply=%region_4.0 | all-reduce | flops 1024 | bytes 8192 | tf_op jit(solution)/shard_map/psum | solution.py:91
  142.0 42.3 %all-reduce.11 = (f32[2,512]{1,0:T(2,128)S(1)}, f32[2,512]{1,0:T(2,128)S(1)}, f32[2,512]{1,0:T(2,128)S(1)}) all-reduce(f32[2,512]{1,0:T(2,128)S(1)} %fusion.304, f32[2,512]{1,0:T(2,128)S(1)} %fusion.294, f32[2,512]{1,0:T(2,128)S(1)} %fusion.300), channel_id=1, replica_groups=mesh['row'=4,'col'=8] {'row','col'}, use_global_device_ids=true, to_apply=%region_6.7 | all-reduce | flops 3072 | bytes 24576 | tf_op jit(solution)/shard_map/psum | solution.py:88
  185.5 40.5 %all-reduce.10 = (f32[2,512]{1,0:T(2,128)S(1)}, f32[2,512]{1,0:T(2,128)S(1)}, f32[2,512]{1,0:T(2,128)S(1)}) all-reduce(f32[2,512]{1,0:T(2,128)S(1)} %fusion.303, f32[2,512]{1,0:T(2,128)S(1)} %fusion.293, f32[2,512]{1,0:T(2,128)S(1)} %fusion.299), channel_id=1, replica_groups=mesh['row'=4,'col'=8] {'row','col'}, use_global_device_ids=true, to_apply=%region_8.9 | all-reduce | flops 3072 | bytes 24576 | tf_op jit(solution)/shard_map/psum | solution.py:91
  248.5 41.9 %all-reduce.9 = (f32[2,512]{1,0:T(2,128)S(1)}, f32[2,512]{1,0:T(2,128)S(1)}, f32[2,512]{1,0:T(2,128)S(1)}) all-reduce(f32[2,512]{1,0:T(2,128)S(1)} %fusion.302, f32[2,512]{1,0:T(2,128)S(1)} %fusion.292, f32[2,512]{1,0:T(2,128)S(1)} %fusion.298), channel_id=1, replica_groups=mesh['row'=4,'col'=8] {'row','col'}, use_global_device_ids=true, to_apply=%region_10.11 | all-reduce | flops 3072 | bytes 24576 | tf_op jit(solution)/shard_map/psum | solution.py:88
  292.1 39.2 %all-reduce.8 = (f32[2,512]{1,0:T(2,128)S(1)}, f32[2,512]{1,0:T(2,128)S(1)}, f32[2,512]{1,0:T(2,128)S(1)}) all-reduce(f32[2,512]{1,0:T(2,128)S(1)} %fusion.301, f32[2,512]{1,0:T(2,128)S(1)} %fusion.291, f32[2,512]{1,0:T(2,128)S(1)} %fusion.297), channel_id=1, replica_groups=mesh['row'=4,'col'=8] {'row','col'}, use_global_device_ids=true, to_apply=%region_12.13 | all-reduce | flops 3072 | bytes 24576 | tf_op jit(solution)/shard_map/psum | solution.py:91
  364.7 41.7 %all-reduce.7 = (f32[2,512]{1,0:T(2,128)S(1)}, f32[2,512]{1,0:T(2,128)S(1)}) all-reduce(f32[2,512]{1,0:T(2,128)S(1)} %fusion.290, f32[2,512]{1,0:T(2,128)S(1)} %fusion.296), channel_id=1, replica_groups=mesh['row'=4,'col'=8] {'row','col'}, use_global_device_ids=true, to_apply=%region_36.37 | all-reduce | flops 2048 | bytes 16384 | tf_op jit(solution)/shard_map/psum | solution.py:88
  407.2 39.2 %all-reduce.6 = (f32[2,512]{1,0:T(2,128)S(1)}, f32[2,512]{1,0:T(2,128)S(1)}) all-reduce(f32[2,512]{1,0:T(2,128)S(1)} %fusion.289, f32[2,512]{1,0:T(2,128)S(1)} %fusion.295), channel_id=1, replica_groups=mesh['row'=4,'col'=8] {'row','col'}, use_global_device_ids=true, to_apply=%region_38.39 | all-reduce | flops 2048 | bytes 16384 | tf_op jit(solution)/shard_map/psum | solution.py:91
  450.0 41.1 %all-reduce.5 = (f32[2,512]{1,0:T(2,128)S(1)}, f32[2,512]{1,0:T(2,128)S(1)}, f32[2,512]{1,0:T(2,128)S(1)}, f32[2,512]{1,0:T(2,128)S(1)}) all-reduce(f32[2,512]{1,0:T(2,128)S(1)} %fusion.285, f32[2,512]{1,0:T(2,128)S(1)} %fusion.286, f32[2,512]{1,0:T(2,128)S(1)} %fusion.287, ...), channel_id=1, replica_groups=mesh['row'=4,'col'=8] {'row','col'}, use_global_device_ids=true, to_apply=%region_47.48 | all-reduce | flops 4096 | bytes 32768 | tf_op jit(solution)/shard_map/psum | solution.py:99
  506.8 7.1 pad_maximum_fusion.1
  513.9 9.1 pad.169
  523.0 33.0 %copy.218 = f32[3,8,512,512]{3,1,2,0:T(8,128)} copy(f32[3,8,512,512]{3,2,1,0:T(8,128)S(1)} %bitcast.327) | data formatting | bytes 50331648
  568.6 7.7 collective-permute-done.22
  580.9 7.0 multiply_reduce_fusion.1
  589.9 49.1 %all-reduce.4 = (f32[2,512]{1,0:T(2,128)S(1)}, f32[2,512]{1,0:T(2,128)S(1)}, f32[2,512]{1,0:T(2,128)S(1)}, f32[2,512]{1,0:T(2,128)S(1)}, f32[2,512]{1,0:T(2,128)S(1)}, /*index=5*/f32[2,512]{1,0:T(2,128)S(1)}) all-reduce(f32[2,512]{1,0:T(2,128)S(1)} %fusion.275, ...), channel_id=1, replica_groups=mesh['row'=4,'col'=8] {'row','col'}, use_global_device_ids=true, to_apply=%region_67.68 | all-reduce | flops 6144 | bytes 49152 | tf_op jit(solution)/shard_map/psum | solution.py:99
  687.0 59.7 %all-reduce.3 = (f32[2,512]{1,0:T(2,128)S(1)}, f32[2,512]{1,0:T(2,128)S(1)}, f32[2,512]{1,0:T(2,128)S(1)}, f32[2,512]{1,0:T(2,128)S(1)}, f32[2,512]{1,0:T(2,128)S(1)}, /*index=5*/f32[2,512]{1,0:T(2,128)S(1)}) all-reduce(f32[2,512]{1,0:T(2,128)S(1)} %fusion.273, ...), channel_id=1, replica_groups=mesh['row'=4,'col'=8] {'row','col'}, use_global_device_ids=true, to_apply=%region_71.72 | all-reduce | flops 6144 | bytes 49152 | tf_op jit(solution)/shard_map/psum | solution.py:99
  767.4 7.1 collective-permute-start.34
  777.0 7.2 reshape.195
  790.3 303.8 %all-reduce.13 = (bf16[4,262144]{1,0:T(4,128)(2,1)}, f32[2,512]{1,0:T(2,128)S(1)}, f32[2,512]{1,0:T(2,128)S(1)}, f32[1,512]{1,0:T(1,128)}, f32[1,512]{1,0:T(1,12...) all-reduce(f32[4,262144]{1,0:T(4,128)} %reshape.195, ...), channel_id=3, replica_groups=mesh['row'=4,'col'=8] {'row','col'}, use_global_device_ids=true, to_apply=%region_89.90.clone | all-reduce | flops 1584128 | bytes 9527296
  1099.5 13.7 pad_maximum_fusion
  1113.3 12.2 pad.168
  1125.5 43.3 %copy.213 = f32[4,8,512,512]{3,1,2,0:T(8,128)} copy(f32[4,8,512,512]{3,2,1,0:T(8,128)S(1)} %bitcast.321) | data formatting | bytes 67108864
  1174.3 705.6 %reduce-scatter.5.cloned.1.call-done = f32[27,8192]{1,0:T(8,128)} async-done(((f32[27,262144]{1,0:T(8,128)}), f32[27,8192]{1,0:T(8,128)}) %reduce-scatter.5.cloned.1.call-update) | async-done | bytes 884752 | tf_op jit(solution)/shard_map/reduce_scatter | solution.py:291
  1911.6 25.6 %all-gather.9.cloned.1.call-done = bf16[2,262144]{1,0:T(2,128)(2,1)} async-done(((bf16[2,8192]{1,0:T(2,128)(2,1)}), bf16[2,262144]{1,0:T(2,128)(2,1)}) %all-gather.9.cloned.1.call-update) | async-done | bytes 1048592 | tf_op jit(solution)/shard_map/all_gather | solution.py:297
  1940.0 56.1 %all-gather.7.cloned.1.call-done = bf16[4,262144]{1,0:T(4,128)(2,1)} async-done(((bf16[4,8192]{1,0:T(4,128)(2,1)}), bf16[4,262144]{1,0:T(4,128)(2,1)}) %all-gather.7.cloned.1.call-update) | async-done | bytes 2097168 | tf_op jit(solution)/shard_map/all_gather | solution.py:294
  2000.8 93.7 %all-gather.11.cloned.1.call-done = bf16[18,262144]{1,0:T(8,128)(2,1)} async-done(((bf16[18,8192]{1,0:T(8,128)(2,1)}), bf16[18,262144]{1,0:T(8,128)(2,1)}) %all-gather.11.cloned.1.call-update) | async-done | bytes 9437200 | tf_op jit(solution)/shard_map/all_gather | solution.py:300
  2101.1 27.8 %copy.219 = f32[3,8,512,512]{3,2,1,0:T(8,128)} copy(f32[3,8,512,512]{3,1,2,0:T(8,128)S(1)} %bitcast.328) | data formatting | bytes 50331648
  2128.8 15.0 slice.337
  2143.8 67.0 %all-gather.5.cloned.1.call-done = bf16[27,262144]{1,0:T(8,128)(2,1)} async-done(((bf16[27,8192]{1,0:T(8,128)(2,1)}), bf16[27,262144]{1,0:T(8,128)(2,1)}) %all-gather.5.cloned.1.call-update) | async-done | bytes 14155792 | tf_op jit(solution)/shard_map/all_gather | solution.py:303
  2210.8 8.6 reshape.203
  2219.4 36.3 %copy.214 = f32[4,8,512,512]{3,2,1,0:T(8,128)} copy(f32[4,8,512,512]{3,1,2,0:T(8,128)S(1)} %bitcast.323) | data formatting | bytes 67108864
  2255.7 21.3 slice.336
  (576 shorter events, 278.6 us)
Async XLA Ops:
  7.2 1164.9 %reduce-scatter.7.cloned.1.call-start = ((), (), s32[]{:S(2)}) async-start(), calls=%async_computation.6 | async-start | bytes 25952256 | tf_op jit(solution)/shard_map/reduce_scatter | solution.py:290
  8.0 13.7 collective-permute-start
  10.4 12.4 collective-permute-start.1
  333.2 10.1 collective-permute-start.17
  337.5 11.7 collective-permute-start.13
  338.8 10.4 collective-permute-start.12
  343.4 12.3 collective-permute-start.19
  344.7 11.0 collective-permute-start.18
  349.3 10.9 collective-permute-start.15
  350.6 9.6 collective-permute-start.14
  491.7 64.3 %collective-permute-start.21 = (bf16[6,1,4,512]{3,0,2,1:T(8,128)(2,1)S(1)}, bf16[6,1,4,512]{3,0,2,1:T(8,128)(2,1)S(1)}, u32[]{:S(2)}, u32[]{:S(2)}) collective-permute-start(bf16[6,1,4,512]{3,0,2,1:T(8,128)(2,1)S(1)} %get-tuple-element.195), channel_id=1, source_target_pairs={{8,0},{16,8},{24,16},{9,1},{17,9},{25,17},{10,2},{18,10},{26,18},{... | collective-permute-start | bytes 73736 | tf_op jit(solution)/shard_map/ppermute | solution.py:23
  493.0 63.1 %collective-permute-start.20 = (bf16[6,1,4,512]{3,0,2,1:T(8,128)(2,1)S(1)}, bf16[6,1,4,512]{3,0,2,1:T(8,128)(2,1)S(1)}, u32[]{:S(2)}, u32[]{:S(2)}) collective-permute-start(bf16[6,1,4,512]{3,0,2,1:T(8,128)(2,1)S(1)} %get-tuple-element.194), channel_id=1, source_target_pairs={{0,8},{8,16},{16,24},{1,9},{9,17},{17,25},{2,10},{10,18},{18,26},{... | collective-permute-start | bytes 73736 | tf_op jit(solution)/shard_map/ppermute | solution.py:22
  496.6 65.3 %collective-permute-start.25 = (bf16[6,1,4,512]{3,0,2,1:T(8,128)(2,1)S(1)}, bf16[6,1,4,512]{3,0,2,1:T(8,128)(2,1)S(1)}, u32[]{:S(2)}, u32[]{:S(2)}) collective-permute-start(bf16[6,1,4,512]{3,0,2,1:T(8,128)(2,1)S(1)} %get-tuple-element.193), channel_id=1, source_target_pairs={{8,0},{16,8},{24,16},{9,1},{17,9},{25,17},{10,2},{18,10},{26,18},{... | collective-permute-start | bytes 73736 | tf_op jit(solution)/shard_map/ppermute | solution.py:23
  497.9 64.1 %collective-permute-start.24 = (bf16[6,1,4,512]{3,0,2,1:T(8,128)(2,1)S(1)}, bf16[6,1,4,512]{3,0,2,1:T(8,128)(2,1)S(1)}, u32[]{:S(2)}, u32[]{:S(2)}) collective-permute-start(bf16[6,1,4,512]{3,0,2,1:T(8,128)(2,1)S(1)} %get-tuple-element.192), channel_id=1, source_target_pairs={{0,8},{8,16},{16,24},{1,9},{9,17},{17,25},{2,10},{10,18},{18,26},{... | collective-permute-start | bytes 73736 | tf_op jit(solution)/shard_map/ppermute | solution.py:22
  556.0 1323.9 %reduce-scatter.5.cloned.1.call-start = ((), (), s32[]{:S(2)}) async-start(), calls=%async_computation.2 | async-start | bytes 34603008 | tf_op jit(solution)/shard_map/reduce_scatter | solution.py:291
  556.1 12.4 collective-permute-start.23
  557.4 18.9 collective-permute-start.22
  562.0 18.8 collective-permute-start.27
  563.5 17.4 collective-permute-start.26
  648.7 17.6 collective-permute-start.29
  650.0 16.3 collective-permute-start.28
  666.4 11.0 collective-permute-start.31
  667.7 12.9 collective-permute-start.30
  748.3 17.1 collective-permute-start.33
  749.6 15.8 collective-permute-start.32
  766.1 18.1 collective-permute-start.35
  767.4 16.9 collective-permute-start.34
  1168.8 768.4 %all-gather.9.cloned.1.call-start = ((), (), s32[]{:S(2)}) async-start(), calls=%async_computation.5 | async-start | bytes 1081344 | tf_op jit(solution)/shard_map/all_gather | solution.py:297
  1170.5 825.7 %all-gather.7.cloned.1.call-start = ((), (), s32[]{:S(2)}) async-start(), calls=%async_computation.4 | async-start | bytes 2162688 | tf_op jit(solution)/shard_map/all_gather | solution.py:294
  1172.0 922.5 %all-gather.11.cloned.1.call-start = ((), (), s32[]{:S(2)}) async-start(), calls=%async_computation.7 | async-start | bytes 12976128 | tf_op jit(solution)/shard_map/all_gather | solution.py:300
  1174.1 1036.7 %all-gather.5.cloned.1.call-start = ((), (), s32[]{:S(2)}) async-start(), calls=%async_computation.3 | async-start | bytes 17301504 | tf_op jit(solution)/shard_map/all_gather | solution.py:303
  1887.9 9.7 collective-permute-start.37
  (154 other events, 9129.6 us)
Sparse Core Ops, SparseCore 0:
  556.1 615.4 reduce-scatter.6
  1173.9 705.8 reduce-scatter.4
  1883.4 53.7 all-gather.8
  1940.6 55.4 all-gather.6
  1999.6 94.8 all-gather.10
  2097.4 113.3 all-gather.4
where the time goes:
time: 2300 us; the launch traced here: 2280 us
  waiting for transfers between devices  972 us (42%)
  blocking collectives  784 us (34%)
  local copies, waits for them, and re-layouts  236 us (10%)
  starting transfers between devices  111 us (5%)
  matrix products  93.6 us (4%)
  other arithmetic  69.5 us (3%)
    reduce_scatter x1, waiting for transfers between devices, body(): lax.psum_scatter(shared_flat, ('row', 'col'), scatter_dimension=1, tiled=...  706 us
    unnamed x1, blocking collectives  304 us
    unnamed x301, local copies, waits for them, and re-layouts  212 us
    psum x4, blocking collectives, norm_forward(): totals = lax.psum(domain_totals(member, product), ('row', 'col'))  170 us
    psum x4, blocking collectives, norm_forward(): lax.psum(domain_totals(member, centered * centered), ('row', 'col'))  160 us
    psum x3, blocking collectives, norm_backward(): lax.psum((domain_totals(member, scaled), domain_totals(member, scaled * n...  150 us
    all_gather x1, waiting for transfers between devices, body(): lax.all_gather(all_parts[2].astype(jnp.bfloat16), ('row', 'col'), axis=1,...  93.7 us
    ppermute x20, starting transfers between devices, with_halo(): before = lax.ppermute(last, axis, up)  85 us
  transfers between devices with their start and end apart: 46, of which 15 were waited for; matrix products, arithmetic and copies ran while one was open for 13% of the time, Pallas kernels for 0%

commit v1 on v0

v1 whole, which is shorter than its diff:
```python
import jax
import jax.numpy as jnp
import numpy as np
from jax import lax
from jax.sharding import Mesh, PartitionSpec as P

TASKS = 2
CONVS = 3
DOMAINS = 2
CORES = 2

EPSILON = 1e-05
HIGHEST = lax.Precision.HIGHEST
ALL = ("y", "c", "z", "x")
ROW = ("y", "c")
COL = ("z", "x")
CHIPS = ("y", "z", "x")


def size_of(axes):
    total = 1
    for axis in axes:
        total *= lax.axis_size(axis)
    return total


def exchange(value, axes):
    count = size_of(axes)
    return [value] + [
        lax.ppermute(value, axes, [(i, i ^ k) for i in range(count)]) for k in range(1, count)
    ]


def tree_sum(values):
    while len(values) > 1:
        values = [a + b for a, b in zip(values[::2], values[1::2])]
    return values[0]


STAGES = (("c",), ("y", "x"), ("z",))


def total_stats(average, squares, number):
    for axes in STAGES:
        both = exchange(jnp.stack([average, squares]), axes)
        averages = [b[0] for b in both]
        average = tree_sum(averages) * (1.0 / len(both))
        squares = tree_sum([b[1] for b in both]) + number * tree_sum(
            [(a - average) * (a - average) for a in averages]
        )
        number = number * len(both)
    return average, squares / number


def total_sums(value):
    for axes in STAGES:
        value = tree_sum(exchange(value, axes))
    return value


def halo(tile, pad=1):
    for axes, dim in ((ROW, 0), (COL, 1)):
        count, length = size_of(axes), tile.shape[dim]
        up = [(i, i + 1) for i in range(count - 1)]
        down = [(i + 1, i) for i in range(count - 1)]
        before = lax.ppermute(lax.slice_in_dim(tile, length - pad, length, axis=dim), axes, up)
        after = lax.ppermute(lax.slice_in_dim(tile, 0, pad, axis=dim), axes, down)
        tile = jnp.concatenate([before, tile, after], axis=dim)
    return tile


def inner(tile):
    return tile[1:-1, 1:-1]


def convolve(padded, kernel):
    return lax.conv_general_dilated(
        padded,
        kernel,
        (1, 1),
        "VALID",
        dimension_numbers=("HWNC", "HWIO", "HWNC"),
        preferred_element_type=jnp.float32,
    )


def convolve_back(padded_grad, kernel):
    return lax.conv_general_dilated(
        padded_grad,
        jnp.flip(kernel, (0, 1)),
        (1, 1),
        "VALID",
        dimension_numbers=("HWNC", "HWOI", "HWNC"),
        preferred_element_type=jnp.float32,
    )


def project(values, weight):
    return jnp.einsum("hwnc,cd->hwnd", values, weight, preferred_element_type=jnp.float32)


def project_back(values, weight):
    return jnp.einsum("hwnd,cd->hwnc", values, weight, preferred_element_type=jnp.float32)


def outer(values, grads):
    return jnp.einsum("hwnc,hwnd->cd", values, grads, preferred_element_type=jnp.float32)


def silu_slope(pre_act):
    logistic = jax.nn.sigmoid(pre_act)
    return logistic * (1.0 + pre_act * (1.0 - logistic))


def domain_totals(member, values):
    return jnp.dot(member.T, jnp.sum(values, axis=(0, 1)), precision=HIGHEST)


def per_image(member, stats):
    return jnp.dot(member, stats, precision=HIGHEST)[None, None]


def local_stats(member, tile, number):
    average = domain_totals(member, tile) / number
    centered = tile - per_image(member, average)
    return average, domain_totals(member, centered * centered)


def forward_stats(member, tiles, number):
    local = [local_stats(member, tile, number) for tile in tiles]
    average, variance = total_stats(
        jnp.stack([a for a, _ in local]), jnp.stack([s for _, s in local]), number[None]
    )
    return average, lax.rsqrt(variance + EPSILON)


def backward_sums(member, pairs):
    local = [
        jnp.stack([domain_totals(member, dy), domain_totals(member, dy * form)])
        for dy, form in pairs
    ]
    return total_sums(jnp.stack(local))


def backward_input(member, dy, form, inverse, gain, sums, counts):
    plain = per_image(member, sums[0] / counts[:, None])
    cross = per_image(member, sums[1] / counts[:, None])
    return per_image(member, inverse) * gain * (dy - plain - form * cross)


def mean_pool(values):
    h, w, n, c = values.shape
    return jnp.mean(values.reshape(h // 2, 2, w // 2, 2, n, c), axis=(1, 3))


def mean_pool_back(grad_out):
    h, w, n, c = grad_out.shape
    spread = jnp.broadcast_to(
        0.25 * grad_out[:, None, :, None].astype(jnp.float32), (h, 2, w, 2, n, c)
    )
    return spread.reshape(2 * h, 2 * w, n, c)


def to_blocks(tile, by):
    counts = [lax.axis_size(a) for a in CHIPS]
    blocks = 1
    for axis in by:
        blocks *= lax.axis_size(axis)
    h, w, n, c = tile.shape
    cut = jnp.moveaxis(tile.reshape(h, w, n, blocks, c // blocks), 3, 0)
    shape = [s if a in by else 1 for a, s in zip(CHIPS, counts)]
    cut = jnp.broadcast_to(cut.reshape(*shape, *cut.shape[1:]), (*counts, *cut.shape[1:]))
    cut = cut.reshape(-1, *cut.shape[3:])
    got = lax.all_to_all(cut, CHIPS, 0, 0)
    ny, nz, nx = counts
    got = got.reshape(ny, nz, nx, h, w, n, c // blocks)
    got = got.transpose(0, 5, 3, 1, 2, 4, 6)
    return got.reshape(ny * n, h, nz * nx * w, c // blocks)


def share_act(padded):
    return to_blocks(padded[:, 1:-1], ("z",))


def kernel_chunk(act, grads):
    grads = to_blocks(grads, ("y", "x"))
    act = jnp.pad(act, ((0, 0), (0, 0), (1, 1), (0, 0)))
    part = lax.conv_general_dilated(
        act,
        grads,
        (1, 1),
        "VALID",
        dimension_numbers=("CHWN", "IHWO", "HWNC"),
        preferred_element_type=jnp.float32,
    )
    a, b, rows, cols = part.shape
    part = part.reshape(a * b, CORES, rows // CORES, cols)
    me = lax.axis_index("c")
    mine = lax.dynamic_index_in_dim(part, me, 1, keepdims=False)
    other = lax.dynamic_index_in_dim(part, 1 - me, 1, keepdims=False).astype(jnp.bfloat16)
    other = lax.ppermute(other, "c", [(0, 1), (1, 0)])
    return (mine + other.astype(jnp.float32)).astype(jnp.bfloat16)


def gather_kernel(chunk):
    ny, nc, nz, nx = (lax.axis_size(a) for a in ALL)
    taps, rows, cols = chunk.shape
    whole = lax.all_gather(chunk, ALL, axis=0, tiled=False)
    whole = whole.reshape(ny, nc, nz, nx, taps, rows, cols).transpose(4, 2, 1, 5, 0, 3, 6)
    whole = whole.reshape(taps, nz * nc * rows, ny * nx * cols)
    return whole.astype(jnp.float32)


def scatter_matrices(parts):
    m, r, c = parts.shape
    sizes = {a: lax.axis_size(a) for a in ALL}
    per = r // size_of(ALL)
    left = ["m", *ALL, "r", "k"]
    parts = parts.reshape(m, *(sizes[a] for a in ALL), per, c)
    for axes in STAGES:
        rest = [d for d in left if d not in axes]
        parts = parts.transpose([left.index(d) for d in (*axes, *rest)])
        left = rest
        count = size_of(axes)
        parts = parts.reshape(count, *parts.shape[len(axes):])
        me = lax.axis_index(axes)
        got = [lax.dynamic_index_in_dim(parts, me, 0, keepdims=False)]
        for k in range(1, count):
            send = lax.dynamic_index_in_dim(parts, me ^ k, 0, keepdims=False)
            send = lax.ppermute(
                send.astype(jnp.bfloat16), axes, [(i, i ^ k) for i in range(count)]
            )
            got.append(send.astype(jnp.float32))
        parts = tree_sum(got)
    return parts.astype(jnp.bfloat16)


def body(
    features,
    priors,
    domain,
    shared_w,
    shared_gain,
    shared_bias,
    first_w,
    second_w,
    task_conv,
    task_gain,
    task_bias,
    shared_cot,
    task_cot,
):
    images, height, breadth, channels = features.shape
    member = (domain[:, None] == jnp.arange(DOMAINS, dtype=jnp.int32)[None, :]).astype(jnp.float32)
    named = jnp.sum(member, axis=0)[:, None]
    number = named * (height * breadth)
    counts = named[:, 0] * (height * breadth * size_of(ALL))
    row, col = lax.axis_index(ROW), lax.axis_index(COL)
    rows = row * height + jnp.arange(height + 2) - 1
    cols = col * breadth + jnp.arange(breadth + 2) - 1
    inside = (
        ((rows >= 0) & (rows < height * size_of(ROW)))[:, None]
        & ((cols >= 0) & (cols < breadth * size_of(COL)))[None, :]
    )[:, :, None, None]

    def only_inside(tile):
        return jnp.where(inside, tile, 0.0).astype(jnp.bfloat16)

    features = halo(features.transpose(1, 2, 0, 3))
    priors = [halo(priors[t].transpose(1, 2, 0, 3)) for t in range(TASKS)]
    shared_cot = shared_cot.transpose(1, 2, 0, 3)
    task_cot = [halo(task_cot[t].transpose(1, 2, 0, 3)) for t in range(TASKS)]

    def apply_norm(tile, average, inverse, gain, bias):
        form = (tile - per_image(member, average)) * per_image(member, inverse)
        return form, form * gain + bias

    product = convolve(features, shared_w[0])
    product_halo = halo(product)
    features_blocks = share_act(features)
    average, inverse = forward_stats(member, [product], number)
    inverse1 = inverse[0]
    form1, normed1 = apply_norm(product_halo, average[0], inverse1, shared_gain[0], shared_bias[0])
    act1 = only_inside(jax.nn.silu(normed1))

    product = convolve(act1, shared_w[1])
    product_halo = halo(product)
    hidden = [
        project(act1, first_w[t, :channels]) + project(priors[t], first_w[t, channels:])
        for t in range(TASKS)
    ]
    act1_blocks = share_act(act1)
    average, inverse = forward_stats(member, [product] + [inner(h) for h in hidden], number)
    inverse2, inverse_h = inverse[0], inverse[1:]
    form2, normed2 = apply_norm(product_halo, average[0], inverse2, shared_gain[1], shared_bias[1])
    act2 = only_inside(jax.nn.silu(normed2))
    form_h, normed_h, hidden_act = [], [], []
    for t in range(TASKS):
        form, normed = apply_norm(
            hidden[t], average[1 + t], inverse_h[t], task_gain[t, 0], task_bias[t, 0]
        )
        form_h.append(inner(form))
        normed_h.append(inner(normed))
        hidden_act.append(jax.nn.silu(normed).astype(jnp.bfloat16))

    product = convolve(act2, shared_w[2])
    product_halo = halo(product)
    gate = [project(hidden_act[t], second_w[t]) for t in range(TASKS)]
    act2_blocks = share_act(act2)
    average, inverse = forward_stats(member, [product] + [inner(g) for g in gate], number)
    inverse3, inverse_g = inverse[0], inverse[1:]
    form3, normed3 = apply_norm(product_halo, average[0], inverse3, shared_gain[2], shared_bias[2])
    last = jax.nn.silu(normed3)
    shared_out = mean_pool(inner(last)).astype(jnp.bfloat16)
    form_g, attention, masked = [], [], []
    for t in range(TASKS):
        form, normed = apply_norm(
            gate[t], average[1 + t], inverse_g[t], task_gain[t, 1], task_bias[t, 1]
        )
        form_g.append(inner(form))
        weight = jax.nn.sigmoid(normed)
        attention.append(inner(weight))
        masked.append(only_inside(weight * last))

    refined = [convolve(masked[t], task_conv[t]) for t in range(TASKS)]
    refined_halo = [halo(r) for r in refined]
    masked_blocks = [share_act(m) for m in masked]
    average, inverse_r = forward_stats(member, refined, number)
    form_r, dy_r, task_outs = [], [], []
    for t in range(TASKS):
        form, normed = apply_norm(
            refined_halo[t], average[t], inverse_r[t], task_gain[t, 2], task_bias[t, 2]
        )
        form_r.append(form)
        task_outs.append(mean_pool(inner(jax.nn.silu(normed))).astype(jnp.bfloat16))
        dy_r.append(inner(mean_pool_back(task_cot[t])) * silu_slope(normed))

    sums_r = backward_sums(member, [(inner(dy_r[t]), inner(form_r[t])) for t in range(TASKS)])
    dv_r = [
        only_inside(
            backward_input(
                member, dy_r[t], form_r[t], inverse_r[t], task_gain[t, 2], sums_r[t], counts
            )
        )
        for t in range(TASKS)
    ]
    task_chunks = [kernel_chunk(masked_blocks[t], inner(dv_r[t])) for t in range(TASKS)]
    grad_masked = [convolve_back(dv_r[t], task_conv[t]) for t in range(TASKS)]

    grad_last = mean_pool_back(shared_cot)
    own_last = inner(last)
    dy_g = []
    for t in range(TASKS):
        grad_last = grad_last + grad_masked[t] * attention[t]
        dy_g.append(grad_masked[t] * own_last * attention[t] * (1.0 - attention[t]))
    dy3 = grad_last * silu_slope(inner(normed3))
    dy3_halo = halo(dy3)
    sums = backward_sums(
        member, [(dy3, inner(form3))] + [(dy_g[t], form_g[t]) for t in range(TASKS)]
    )
    sums3, sums_g = sums[0], sums[1:]
    dv3 = only_inside(
        backward_input(member, dy3_halo, form3, inverse3, shared_gain[2], sums3, counts)
    )
    dv_g = [
        backward_input(
            member, dy_g[t], form_g[t], inverse_g[t], task_gain[t, 1], sums_g[t], counts
        ).astype(jnp.bfloat16)
        for t in range(TASKS)
    ]
    chunk3 = kernel_chunk(act2_blocks, inner(dv3))
    grad_act2 = convolve_back(dv3, shared_w[2])

    dy2 = grad_act2 * silu_slope(inner(normed2))
    dy2_halo = halo(dy2)
    dy_h = [project_back(dv_g[t], second_w[t]) * silu_slope(normed_h[t]) for t in range(TASKS)]
    sums = backward_sums(
        member, [(dy2, inner(form2))] + [(dy_h[t], form_h[t]) for t in range(TASKS)]
    )
    sums2, sums_h = sums[0], sums[1:]
    dv2 = only_inside(
        backward_input(member, dy2_halo, form2, inverse2, shared_gain[1], sums2, counts)
    )
    dv_h = [
        backward_input(
            member, dy_h[t], form_h[t], inverse_h[t], task_gain[t, 0], sums_h[t], counts
        ).astype(jnp.bfloat16)
        for t in range(TASKS)
    ]
    chunk2 = kernel_chunk(act1_blocks, inner(dv2))
    grad_act1 = convolve_back(dv2, shared_w[1])
    for t in range(TASKS):
        grad_act1 = grad_act1 + project_back(dv_h[t], first_w[t, :channels])

    dy1 = grad_act1 * silu_slope(inner(normed1))
    dy1_halo = halo(dy1)
    sums1 = backward_sums(member, [(dy1, inner(form1))])[0]
    dv1 = only_inside(
        backward_input(member, dy1_halo, form1, inverse1, shared_gain[0], sums1, counts)
    )
    chunk1 = kernel_chunk(features_blocks, inner(dv1))
    grad_features = convolve_back(dv1, shared_w[0])
    grad_priors = [project_back(dv_h[t], first_w[t, channels:]) for t in range(TASKS)]

    matrices = []
    for t in range(TASKS):
        matrices += [outer(inner(act1), dv_h[t]), outer(inner(priors[t]), dv_h[t])]
    for t in range(TASKS):
        matrices.append(outer(inner(hidden_act[t]), dv_g[t]))
    matrices = scatter_matrices(jnp.stack(matrices))
    matrices = lax.all_gather(matrices, ALL, axis=1, tiled=True).astype(jnp.float32)
    grad_first = matrices[: 2 * TASKS].reshape(TASKS, 2 * channels, channels)
    grad_second = matrices[2 * TASKS :]

    shape = (3, 3, channels, channels)
    grad_task = jnp.stack([gather_kernel(c).reshape(shape) for c in task_chunks])
    grad_shared = jnp.stack([gather_kernel(c).reshape(shape) for c in (chunk1, chunk2, chunk3)])

    shared_sums = jnp.sum(jnp.stack([sums1, sums2, sums3]), axis=2)
    task_sums = jnp.sum(jnp.stack([sums_h, sums_g, sums_r], axis=1), axis=3)

    def images_first(tile):
        return tile.transpose(2, 0, 1, 3)

    return (
        images_first(shared_out),
        jnp.stack([images_first(o) for o in task_outs]),
        images_first(grad_features),
        jnp.stack([images_first(g) for g in grad_priors]),
        grad_shared,
        shared_sums[:, 1],
        shared_sums[:, 0],
        grad_first,
        grad_second,
        grad_task,
        task_sums[:, :, 1],
        task_sums[:, :, 0],
    )


def solution(mesh):
    rows, cols = mesh.shape["row"], mesh.shape["col"]
    along_y = rows // CORES
    along_x = along_y
    grid = np.asarray(mesh.devices).reshape(along_y, CORES, cols // along_x, along_x)
    split = Mesh(grid, ALL)
    return jax.shard_map(
        body,
        mesh=split,
        in_specs=(
            P(None, ROW, COL, None),
            P(None, None, ROW, COL, None),
            P(),
            P(),
            P(),
            P(),
            P(),
            P(),
            P(),
            P(),
            P(),
            P(None, ROW, COL, None),
            P(None, None, ROW, COL, None),
        ),
        out_specs=(
            P(None, ROW, COL, None),
            P(None, None, ROW, COL, None),
            P(None, ROW, COL, None),
            P(None, None, ROW, COL, None),
            P(),
            P(),
            P(),
            P(),
            P(),
            P(),
            P(),
            P(),
        ),
        check_vma=False,
    )
```

time: 2300 us -> 918 us (0.40)
  blocking collectives: 784 us -> 0 us
  waiting for transfers between devices: 972 us -> 351 us
  starting transfers between devices: 111 us -> 265 us
  local copies, waits for them, and re-layouts: 236 us -> 136 us
    reduce_scatter x2 -> x0, waiting for transfers between devices: 706 us -> none  [the longest x1 706 us: body(): lax.psum_scatter(shared_flat, ('row', 'col'), scatter_dimension=1, tiled=...]
    psum x11 -> x0, blocking collectives: 480 us -> none  [the longest x4 170 us: norm_forward(): totals = lax.psum(domain_totals(member, product), ('row', 'col'))]
    unnamed x1 -> x0, blocking collectives: 304 us -> none
    all_gather x4 -> x6, waiting for transfers between devices: 242 us -> 0.01 us  [the longest x5 0.01 us: gather_kernel(): whole = lax.all_gather(chunk, ALL, axis=0, tiled=False)]
    all_to_all x0 -> x10, waiting for transfers between devices: none -> 242 us  [to_blocks(): got = lax.all_to_all(cut, CHIPS, 0, 0)]
    unnamed x301 -> x122, local copies, waits for them, and re-layouts: 212 us -> 12.5 us
    ppermute x40 -> x120, starting transfers between devices: 111 us -> 212 us  [the longest x26 103 us: halo(): lax.ppermute(lax.slice_in_dim(tile, length - pad, length, axis=dim), axes...]
    convert_element_type x2 -> x18, local copies, waits for them, and re-layouts: 3.05 us -> 90 us  [the longest x10 88.5 us: gather_kernel(): return whole.astype(jnp.float32)]
  transfers between devices with their start and end apart: 46 -> 136, of which waited for: 15 -> 67; matrix products, arithmetic and copies ran while one was open for 13% -> 23% of each run, Pallas kernels for 0% -> 0%
where the time goes in v1:
time: 918 us; the launch traced here: 906 us
  waiting for transfers between devices  351 us (38%)
  starting transfers between devices  265 us (29%)
  local copies, waits for them, and re-layouts  136 us (15%)
  matrix products  83 us (9%)
  other arithmetic  53.3 us (6%)
  between operations  17.4 us (2%)
    all_to_all x10, waiting for transfers between devices, to_blocks(): got = lax.all_to_all(cut, CHIPS, 0, 0)  242 us
    ppermute x26, starting transfers between devices, halo(): lax.ppermute(lax.slice_in_dim(tile, length - pad, length, axis=dim), axes...  103 us
    convert_element_type x10, local copies, waits for them, and re-layouts, gather_kernel(): return whole.astype(jnp.float32)  88.5 us
    ppermute x56, starting transfers between devices, exchange(): lax.ppermute(value, axes, [(i, i ^ k) for i in range(count)])  67.3 us
    all_to_all x10, starting transfers between devices, to_blocks(): got = lax.all_to_all(cut, CHIPS, 0, 0)  52.3 us
    ppermute x56, waiting for transfers between devices, exchange(): lax.ppermute(value, axes, [(i, i ^ k) for i in range(count)])  46.1 us
    ppermute x26, starting transfers between devices, halo(): after = lax.ppermute(lax.slice_in_dim(tile, 0, pad, axis=dim), axes, down)  33.5 us
    ppermute x7, waiting for transfers between devices, scatter_matrices(): lax.ppermute(send.astype(jnp.bfloat16), axes, [(i, i ^ k) for i in range(...  26.7 us
  transfers between devices with their start and end apart: 136, of which 67 were waited for; matrix products, arithmetic and copies ran while one was open for 23% of the time, Pallas kernels for 0%

profile of v1, /device:TPU:0, one launch (start us, length us, event | category | flops | bytes accessed | tf_op | source)
XLA Modules:
  0.0 905.5 jit_solution(9868342188357531271)
XLA Ops:
  17.6 5.7 collective-permute-start.60
  81.9 5.2 collective-permute-start.6
  215.8 5.3 collective-permute-start.58
  253.3 5.6 fusion.427
  321.8 9.7 %collective-permute-done.114 = bf16[6,4,16,512]{3,2,0,1:T(8,128)(2,1)} collective-permute-done((bf16[6,4,16,512]{3,2,0,1:T(8,128)(2,1)}, bf16[6,4,16,512]{3,2,0,1:T(8,128)(2,1)}, u32[]{:S(2)}, u32[]{:S(2)}) %collective-permute-start.114) | collective-permute-done | bytes 393248 | tf_op jit(solution)/shard_map/ppermute | solution.py:230
  331.5 7.3 collective-permute-done.113
  360.1 22.3 %all-to-all-done.9 = bf16[16,8,4,6,128]{4,1,3,2,0:T(8,128)(2,1)S(1)} async-done(((bf16[16,8,4,6,128]{4,1,3,2,0:T(8,128)(2,1)}), bf16[16,8,4,6,128]{4,1,3,2,0:T(8,128)(2,1)S(1)}, u32[]{:S(2)}, u32[]{:S(2)}) %all-to-all-start.9) | async-done | bytes 786464 | tf_op jit(solution)/shard_map/all_to_all | solution.py:174
  388.0 33.6 %all-to-all-done.8 = bf16[16,10,4,6,128]{4,2,3,1,0:T(4,128)(2,1)S(1)} async-done(((bf16[16,10,4,6,128]{4,2,3,1,0:T(4,128)(2,1)}), bf16[16,10,4,6,128]{4,2,3,1,0:T(4,128)(2,1)S(1)}, u32[]{:S(2)}, u32[]{:S(2)}) %all-to-all-start.8) | async-done | bytes 983072 | tf_op jit(solution)/shard_map/all_to_all | solution.py:174
  433.0 23.8 %all-to-all-done.7 = bf16[16,8,4,6,128]{4,1,3,2,0:T(8,128)(2,1)S(1)} async-done(((bf16[16,8,4,6,128]{4,1,3,2,0:T(8,128)(2,1)}), bf16[16,8,4,6,128]{4,1,3,2,0:T(8,128)(2,1)S(1)}, u32[]{:S(2)}, u32[]{:S(2)}) %all-to-all-start.7) | async-done | bytes 786464 | tf_op jit(solution)/shard_map/all_to_all | solution.py:174
  461.9 36.3 %all-to-all-done.6 = bf16[16,10,4,6,128]{4,2,3,1,0:T(4,128)(2,1)S(1)} async-done(((bf16[16,10,4,6,128]{4,2,3,1,0:T(4,128)(2,1)}), bf16[16,10,4,6,128]{4,2,3,1,0:T(4,128)(2,1)S(1)}, u32[]{:S(2)}, u32[]{:S(2)}) %all-to-all-start.6) | async-done | bytes 983072 | tf_op jit(solution)/shard_map/all_to_all | solution.py:174
  505.9 5.7 all-to-all-start.4
  511.8 30.7 %all-to-all-done.4 = bf16[16,10,4,6,128]{4,2,3,1,0:T(4,128)(2,1)S(1)} async-done(((bf16[16,10,4,6,128]{4,2,3,1,0:T(4,128)(2,1)}), bf16[16,10,4,6,128]{4,2,3,1,0:T(4,128)(2,1)S(1)}, u32[]{:S(2)}, u32[]{:S(2)}) %all-to-all-start.4) | async-done | bytes 983072 | tf_op jit(solution)/shard_map/all_to_all | solution.py:174
  549.3 31.1 %all-to-all-done.5 = bf16[16,8,4,6,128]{4,1,3,2,0:T(8,128)(2,1)S(1)} async-done(((bf16[16,8,4,6,128]{4,1,3,2,0:T(8,128)(2,1)}), bf16[16,8,4,6,128]{4,1,3,2,0:T(8,128)(2,1)S(1)}, u32[]{:S(2)}, u32[]{:S(2)}) %all-to-all-start.5) | async-done | bytes 786464 | tf_op jit(solution)/shard_map/all_to_all | solution.py:174
  605.6 6.1 collective-permute-done.88
  612.8 9.0 all-to-all-done.2
  622.9 12.1 %all-to-all-start.3 = ((bf16[16,8,4,6,128]{4,1,3,2,0:T(8,128)(2,1)}), bf16[16,8,4,6,128]{4,1,3,2,0:T(8,128)(2,1)S(1)}, u32[]{:S(2)}, u32[]{:S(2)}) async-start(bf16[16,8,4,6,128]{4,1,3,2,0:T(8,128)(2,1)} %bitcast.1237), calls=%async_computation.3 | async-start | bytes 1572864 | tf_op jit(solution)/shard_map/all_to_all | solution.py:174
  636.1 30.7 %all-to-all-done.3 = bf16[16,8,4,6,128]{4,1,3,2,0:T(8,128)(2,1)S(1)} async-done(((bf16[16,8,4,6,128]{4,1,3,2,0:T(8,128)(2,1)}), bf16[16,8,4,6,128]{4,1,3,2,0:T(8,128)(2,1)S(1)}, u32[]{:S(2)}, u32[]{:S(2)}) %all-to-all-start.3) | async-done | bytes 786464 | tf_op jit(solution)/shard_map/all_to_all | solution.py:174
  699.9 9.2 %collective-permute-done.106 = f32[1,2,2,512]{3,2,1,0:T(2,128)S(1)} collective-permute-done((f32[1,2,2,512]{3,2,1,0:T(2,128)S(1)}, f32[1,2,2,512]{3,2,1,0:T(2,128)S(1)}, u32[]{:S(2)}, u32[]{:S(2)}) %collective-permute-start.106) | collective-permute-done | bytes 8224 | tf_op jit(solution)/shard_map/ppermute | solution.py:30
  720.8 7.1 all-to-all-start.1
  729.2 24.6 %all-to-all-done.1 = bf16[16,8,4,6,128]{4,1,3,2,0:T(8,128)(2,1)S(1)} async-done(((bf16[16,8,4,6,128]{4,1,3,2,0:T(8,128)(2,1)}), bf16[16,8,4,6,128]{4,1,3,2,0:T(8,128)(2,1)S(1)}, u32[]{:S(2)}, u32[]{:S(2)}) %all-to-all-start.1) | async-done | bytes 786464 | tf_op jit(solution)/shard_map/all_to_all | solution.py:174
  782.7 9.8 %copy.370 = bf16[9,4,2,64,2,2,128]{6,5,4,3,2,1,0:T(2,128)(2,1)} copy(bf16[9,4,2,64,2,2,128]{6,3,0,5,1,2,4:T(8,128)(2,1)} %bitcast.1217) | data formatting | bytes 9437184 | tf_op jit(solution)/shard_map/convert_element_type | solution.py:211
  792.5 8.0 convert_element_type.392
  800.5 10.0 %copy.359 = bf16[9,4,2,64,2,2,128]{6,5,4,3,2,1,0:T(2,128)(2,1)} copy(bf16[9,4,2,64,2,2,128]{6,3,0,5,1,2,4:T(8,128)(2,1)} %bitcast.1218) | data formatting | bytes 9437184 | tf_op jit(solution)/shard_map/convert_element_type | solution.py:211
  810.5 8.2 convert_element_type.385
  818.8 12.0 %maximum_convert_fusion.1 = f32[2,3,3,512,512]{4,3,2,1,0:T(8,128)} fusion(bf16[1,3,3,512,512]{4,3,2,1,0:T(8,128)(2,1)} %convert_element_type.392, bf16[1,3,3,512,512]{4,3,2,1,0:T(8,128)(2,1)} %convert_element_type.385), kind=kLoop, calls=%fused_computation.1 | loop fusion | flops 9437184 | bytes 28311552 | tf_op jit(solution)/shard_map/stack | solution.py:416
  830.8 9.4 %copy.347 = bf16[9,4,2,64,2,2,128]{6,5,4,3,2,1,0:T(2,128)(2,1)} copy(bf16[9,4,2,64,2,2,128]{6,3,0,5,1,2,4:T(8,128)(2,1)} %bitcast.1219) | data formatting | bytes 9437184 | tf_op jit(solution)/shard_map/convert_element_type | solution.py:211
  840.2 8.0 convert_element_type.355
  848.2 9.4 %copy.336 = bf16[9,4,2,64,2,2,128]{6,5,4,3,2,1,0:T(2,128)(2,1)} copy(bf16[9,4,2,64,2,2,128]{6,3,0,5,1,2,4:T(8,128)(2,1)} %bitcast.1220) | data formatting | bytes 9437184 | tf_op jit(solution)/shard_map/convert_element_type | solution.py:211
  857.6 8.2 convert_element_type.348
  865.8 9.4 %copy.325 = bf16[9,4,2,64,2,2,128]{6,5,4,3,2,1,0:T(2,128)(2,1)} copy(bf16[9,4,2,64,2,2,128]{6,3,0,5,1,2,4:T(8,128)(2,1)} %bitcast.1221) | data formatting | bytes 9437184 | tf_op jit(solution)/shard_map/convert_element_type | solution.py:211
  875.2 8.1 convert_element_type.341
  883.3 15.2 %maximum_convert_fusion = f32[3,3,3,512,512]{4,3,2,1,0:T(8,128)} fusion(bf16[1,3,3,512,512]{4,3,2,1,0:T(8,128)(2,1)} %convert_element_type.355, bf16[1,3,3,512,512]{4,3,2,1,0:T(8,128)(2,1)} %convert_element_type.348, bf16[1,3,3,512,512]{4,3,2,1,0:T(8,128)(2,1)} %convert_element_type.341), kind=kLoop, calls=%fused_computation | loop fusion | flops 21233664 | bytes 42467328 | tf_op jit(solution)/shard_map/stack | solution.py:417
  (723 shorter events, 451.2 us)
Async XLA Ops:
  7.2 769.6 %all-gather.12.cloned.1.call-start = ((), (), s32[]{:S(2)}) async-start(), calls=%async_computation.10 | async-start | bytes 3244032 | tf_op jit(solution)/shard_map/all_gather | solution.py:411
  8.3 24.4 %collective-permute-start.1 = (bf16[1,4,6,512]{3,2,1,0:T(8,128)(2,1)S(1)}, bf16[1,4,6,512]{3,2,1,0:T(8,128)(2,1)S(1)}, u32[]{:S(2)}, u32[]{:S(2)}) collective-permute-start(bf16[1,4,6,512]{3,2,1,0:T(8,128)(2,1)S(1)} %get-tuple-element.196), channel_id=1, source_target_pairs={{8,0},{16,8},{24,16},{9,1},{17,9},{25,17},{10,2},{18,10},{26,18},{... | collective-permute-start | bytes 73736 | tf_op jit(solution)/shard_map/ppermute | solution.py:67
  9.6 24.4 %collective-permute-start = (bf16[1,4,6,512]{3,2,1,0:T(8,128)(2,1)S(1)}, bf16[1,4,6,512]{3,2,1,0:T(8,128)(2,1)S(1)}, u32[]{:S(2)}, u32[]{:S(2)}) collective-permute-start(bf16[1,4,6,512]{3,2,1,0:T(8,128)(2,1)S(1)} %get-tuple-element.195), channel_id=1, source_target_pairs={{0,8},{8,16},{16,24},{1,9},{9,17},{17,25},{2,10},{10,18},{18,26},{... | collective-permute-start | bytes 73736 | tf_op jit(solution)/shard_map/ppermute | solution.py:66
  14.1 39.3 %collective-permute-start.24 = (bf16[1,4,6,512]{3,2,1,0:T(8,128)(2,1)S(1)}, bf16[1,4,6,512]{3,2,1,0:T(8,128)(2,1)S(1)}, u32[]{:S(2)}, u32[]{:S(2)}) collective-permute-start(bf16[1,4,6,512]{3,2,1,0:T(8,128)(2,1)S(1)} %get-tuple-element.194), channel_id=1, source_target_pairs={{8,0},{16,8},{24,16},{9,1},{17,9},{25,17},{10,2},{18,10},{26,18},{... | collective-permute-start | bytes 73736 | tf_op jit(solution)/shard_map/ppermute | solution.py:67
  27.5 31.0 %collective-permute-start.23 = (bf16[1,4,6,512]{3,2,1,0:T(8,128)(2,1)S(1)}, bf16[1,4,6,512]{3,2,1,0:T(8,128)(2,1)S(1)}, u32[]{:S(2)}, u32[]{:S(2)}) collective-permute-start(bf16[1,4,6,512]{3,2,1,0:T(8,128)(2,1)S(1)} %get-tuple-element.193), channel_id=1, source_target_pairs={{0,8},{8,16},{16,24},{1,9},{9,17},{17,25},{2,10},{10,18},{18,26},{... | collective-permute-start | bytes 73736 | tf_op jit(solution)/shard_map/ppermute | solution.py:66
  31.2 32.4 %collective-permute-start.20 = (bf16[1,4,6,512]{3,2,1,0:T(8,128)(2,1)S(1)}, bf16[1,4,6,512]{3,2,1,0:T(8,128)(2,1)S(1)}, u32[]{:S(2)}, u32[]{:S(2)}) collective-permute-start(bf16[1,4,6,512]{3,2,1,0:T(8,128)(2,1)S(1)} %get-tuple-element.192), channel_id=1, source_target_pairs={{8,0},{16,8},{24,16},{9,1},{17,9},{25,17},{10,2},{18,10},{26,18},{... | collective-permute-start | bytes 73736 | tf_op jit(solution)/shard_map/ppermute | solution.py:67
  44.3 20.5 %collective-permute-start.19 = (bf16[1,4,6,512]{3,2,1,0:T(8,128)(2,1)S(1)}, bf16[1,4,6,512]{3,2,1,0:T(8,128)(2,1)S(1)}, u32[]{:S(2)}, u32[]{:S(2)}) collective-permute-start(bf16[1,4,6,512]{3,2,1,0:T(8,128)(2,1)S(1)} %get-tuple-element.191), channel_id=1, source_target_pairs={{0,8},{8,16},{16,24},{1,9},{9,17},{17,25},{2,10},{10,18},{18,26},{... | collective-permute-start | bytes 73736 | tf_op jit(solution)/shard_map/ppermute | solution.py:66
  46.9 100.1 %collective-permute-start.63 = (bf16[6,1,6,512]{3,1,0,2:T(2,128)(2,1)S(1)}, bf16[6,1,6,512]{3,1,0,2:T(2,128)(2,1)S(1)}, u32[]{:S(2)}, u32[]{:S(2)}) collective-permute-start(bf16[6,1,6,512]{3,1,0,2:T(2,128)(2,1)S(1)} %get-tuple-element.200), channel_id=1, source_target_pairs={{1,0},{2,1},{3,2},{4,3},{5,4},{6,5},{7,6},{9,8},{10,9},{11,10},{12... | collective-permute-start | bytes 110600 | tf_op jit(solution)/shard_map/ppermute | solution.py:67
  53.4 93.7 %collective-permute-start.62 = (bf16[6,1,6,512]{3,1,0,2:T(2,128)(2,1)S(1)}, bf16[6,1,6,512]{3,1,0,2:T(2,128)(2,1)S(1)}, u32[]{:S(2)}, u32[]{:S(2)}) collective-permute-start(bf16[6,1,6,512]{3,1,0,2:T(2,128)(2,1)S(1)} %get-tuple-element.199), channel_id=1, source_target_pairs={{0,1},{1,2},{2,3},{3,4},{4,5},{5,6},{6,7},{8,9},{9,10},{10,11},{11... | collective-permute-start | bytes 110600 | tf_op jit(solution)/shard_map/ppermute | solution.py:66
  74.1 26.9 %collective-permute-start.26 = (bf16[10,1,6,512]{3,2,1,0:T(8,128)(2,1)S(1)}, bf16[10,1,6,512]{3,2,1,0:T(8,128)(2,1)S(1)}, u32[]{:S(2)}, u32[]{:S(2)}) collective-permute-start(bf16[10,1,6,512]{3,2,1,0:T(8,128)(2,1)S(1)} %get-tuple-element.188), channel_id=1, source_target_pairs={{1,0},{2,1},{3,2},{4,3},{5,4},{6,5},{7,6},{9,8},{10,9},{11,10},{12... | collective-permute-start | bytes 184328 | tf_op jit(solution)/shard_map/ppermute | solution.py:67
  126.0 60.1 %collective-permute-start.67 = (bf16[6,1,6,512]{3,1,0,2:T(2,128)(2,1)S(1)}, bf16[6,1,6,512]{3,1,0,2:T(2,128)(2,1)S(1)}, u32[]{:S(2)}, u32[]{:S(2)}) collective-permute-start(bf16[6,1,6,512]{3,1,0,2:T(2,128)(2,1)S(1)} %get-tuple-element.202), channel_id=1, source_target_pairs={{1,0},{2,1},{3,2},{4,3},{5,4},{6,5},{7,6},{9,8},{10,9},{11,10},{12... | collective-permute-start | bytes 110600 | tf_op jit(solution)/shard_map/ppermute | solution.py:67
  140.1 46.0 %collective-permute-start.66 = (bf16[6,1,6,512]{3,1,0,2:T(2,128)(2,1)S(1)}, bf16[6,1,6,512]{3,1,0,2:T(2,128)(2,1)S(1)}, u32[]{:S(2)}, u32[]{:S(2)}) collective-permute-start(bf16[6,1,6,512]{3,1,0,2:T(2,128)(2,1)S(1)} %get-tuple-element.201), channel_id=1, source_target_pairs={{0,1},{1,2},{2,3},{3,4},{4,5},{5,6},{6,7},{8,9},{9,10},{10,11},{11... | collective-permute-start | bytes 110600 | tf_op jit(solution)/shard_map/ppermute | solution.py:66
  208.2 21.8 %collective-permute-start.48 = (f32[10,1,6,512]{3,2,1,0:T(8,128)S(1)}, f32[10,1,6,512]{3,2,1,0:T(8,128)S(1)}, u32[]{:S(2)}, u32[]{:S(2)}) collective-permute-start(f32[10,1,6,512]{3,2,1,0:T(8,128)S(1)} %get-tuple-element.158), channel_id=1, source_target_pairs={{1,0},{2,1},{3,2},{4,3},{5,4},{6,5},{7,6},{9,8},{10,9},{11,10},{12... | collective-permute-start | bytes 368648 | tf_op jit(solution)/shard_map/ppermute | solution.py:67
  209.5 20.5 %collective-permute-start.47 = (f32[10,1,6,512]{3,2,1,0:T(8,128)S(1)}, f32[10,1,6,512]{3,2,1,0:T(8,128)S(1)}, u32[]{:S(2)}, u32[]{:S(2)}) collective-permute-start(f32[10,1,6,512]{3,2,1,0:T(8,128)S(1)} %get-tuple-element.157), channel_id=1, source_target_pairs={{0,1},{1,2},{2,3},{3,4},{4,5},{5,6},{6,7},{8,9},{9,10},{10,11},{11... | collective-permute-start | bytes 368648 | tf_op jit(solution)/shard_map/ppermute | solution.py:66
  319.2 19.6 %collective-permute-start.113 = (bf16[6,4,16,512]{3,2,0,1:T(8,128)(2,1)}, bf16[6,4,16,512]{3,2,0,1:T(8,128)(2,1)}, u32[]{:S(2)}, u32[]{:S(2)}) collective-permute-start(bf16[6,4,16,512]{3,2,0,1:T(8,128)(2,1)} %get-tuple-element.139), channel_id=1, source_target_pairs={{0,16},{1,17},{16,0},{17,1},{2,18},{3,19},{18,2},{19,3},{4,20},{5,... | collective-permute-start | bytes 1179656 | tf_op jit(solution)/shard_map/ppermute | solution.py:230
  320.5 18.3 %collective-permute-start.112 = (bf16[6,4,16,512]{3,2,0,1:T(8,128)(2,1)}, bf16[6,4,16,512]{3,2,0,1:T(8,128)(2,1)}, u32[]{:S(2)}, u32[]{:S(2)}) collective-permute-start(bf16[6,4,16,512]{3,2,0,1:T(8,128)(2,1)} %get-tuple-element.137), channel_id=1, source_target_pairs={{0,1},{1,0},{16,17},{17,16},{2,3},{3,2},{18,19},{19,18},{4,5},{5,4... | collective-permute-start | bytes 1179656 | tf_op jit(solution)/shard_map/ppermute | solution.py:230
  355.8 26.6 %all-to-all-start.9 = ((bf16[16,8,4,6,128]{4,1,3,2,0:T(8,128)(2,1)}), bf16[16,8,4,6,128]{4,1,3,2,0:T(8,128)(2,1)S(1)}, u32[]{:S(2)}, u32[]{:S(2)}) async-start(bf16[16,8,4,6,128]{4,1,3,2,0:T(8,128)(2,1)} %bitcast.349), calls=%async_computation.9 | async-start | bytes 1572864 | tf_op jit(solution)/shard_map/all_to_all | solution.py:174
  383.6 38.0 %all-to-all-start.8 = ((bf16[16,10,4,6,128]{4,2,3,1,0:T(4,128)(2,1)}), bf16[16,10,4,6,128]{4,2,3,1,0:T(4,128)(2,1)S(1)}, u32[]{:S(2)}, u32[]{:S(2)}) async-start(bf16[16,10,4,6,128]{4,2,3,1,0:T(4,128)(2,1)} %bitcast.342), calls=%async_computation.8 | async-start | bytes 1966080 | tf_op jit(solution)/shard_map/all_to_all | solution.py:174
  387.2 395.5 %all-gather.22.cloned.1.call-start = ((), (), s32[]{:S(2)}) async-start(), calls=%async_computation.15 | async-start | bytes 4866048 | tf_op jit(solution)/shard_map/all_gather | solution.py:208
  429.0 27.8 %all-to-all-start.7 = ((bf16[16,8,4,6,128]{4,1,3,2,0:T(8,128)(2,1)}), bf16[16,8,4,6,128]{4,1,3,2,0:T(8,128)(2,1)S(1)}, u32[]{:S(2)}, u32[]{:S(2)}) async-start(bf16[16,8,4,6,128]{4,1,3,2,0:T(8,128)(2,1)} %bitcast.331), calls=%async_computation.7 | async-start | bytes 1572864 | tf_op jit(solution)/shard_map/all_to_all | solution.py:174
  458.0 40.2 %all-to-all-start.6 = ((bf16[16,10,4,6,128]{4,2,3,1,0:T(4,128)(2,1)}), bf16[16,10,4,6,128]{4,2,3,1,0:T(4,128)(2,1)S(1)}, u32[]{:S(2)}, u32[]{:S(2)}) async-start(bf16[16,10,4,6,128]{4,2,3,1,0:T(4,128)(2,1)} %bitcast.324), calls=%async_computation.6 | async-start | bytes 1966080 | tf_op jit(solution)/shard_map/all_to_all | solution.py:174
  461.6 338.9 %all-gather.20.cloned.1.call-start = ((), (), s32[]{:S(2)}) async-start(), calls=%async_computation.14 | async-start | bytes 4866048 | tf_op jit(solution)/shard_map/all_gather | solution.py:208
  505.9 36.6 %all-to-all-start.4 = ((bf16[16,10,4,6,128]{4,2,3,1,0:T(4,128)(2,1)}), bf16[16,10,4,6,128]{4,2,3,1,0:T(4,128)(2,1)S(1)}, u32[]{:S(2)}, u32[]{:S(2)}) async-start(bf16[16,10,4,6,128]{4,2,3,1,0:T(4,128)(2,1)} %bitcast.273), calls=%async_computation.4 | async-start | bytes 1966080 | tf_op jit(solution)/shard_map/all_to_all | solution.py:174
  543.5 36.9 %all-to-all-start.5 = ((bf16[16,8,4,6,128]{4,1,3,2,0:T(8,128)(2,1)}), bf16[16,8,4,6,128]{4,1,3,2,0:T(8,128)(2,1)S(1)}, u32[]{:S(2)}, u32[]{:S(2)}) async-start(bf16[16,8,4,6,128]{4,1,3,2,0:T(8,128)(2,1)} %bitcast.280), calls=%async_computation.5 | async-start | bytes 1572864 | tf_op jit(solution)/shard_map/all_to_all | solution.py:174
  548.0 282.8 %all-gather.18.cloned.1.call-start = ((), (), s32[]{:S(2)}) async-start(), calls=%async_computation.13 | async-start | bytes 4866048 | tf_op jit(solution)/shard_map/all_gather | solution.py:208
  587.2 34.6 %all-to-all-start.2 = ((bf16[16,10,4,6,128]{4,2,3,1,0:T(4,128)(2,1)}), bf16[16,10,4,6,128]{4,2,3,1,0:T(4,128)(2,1)S(1)}, u32[]{:S(2)}, u32[]{:S(2)}) async-start(bf16[16,10,4,6,128]{4,2,3,1,0:T(4,128)(2,1)} %bitcast.255), calls=%async_computation.2 | async-start | bytes 1966080 | tf_op jit(solution)/shard_map/all_to_all | solution.py:174
  622.9 43.9 %all-to-all-start.3 = ((bf16[16,8,4,6,128]{4,1,3,2,0:T(8,128)(2,1)}), bf16[16,8,4,6,128]{4,1,3,2,0:T(8,128)(2,1)S(1)}, u32[]{:S(2)}, u32[]{:S(2)}) async-start(bf16[16,8,4,6,128]{4,1,3,2,0:T(8,128)(2,1)} %bitcast.1237), calls=%async_computation.3 | async-start | bytes 1572864 | tf_op jit(solution)/shard_map/all_to_all | solution.py:174
  635.0 213.2 %all-gather.16.cloned.1.call-start = ((), (), s32[]{:S(2)}) async-start(), calls=%async_computation.12 | async-start | bytes 4866048 | tf_op jit(solution)/shard_map/all_gather | solution.py:208
  673.6 46.1 %all-to-all-start = ((bf16[16,10,4,6,128]{4,2,3,1,0:T(4,128)(2,1)}), bf16[16,10,4,6,128]{4,2,3,1,0:T(4,128)(2,1)S(1)}, u32[]{:S(2)}, u32[]{:S(2)}) async-start(bf16[16,10,4,6,128]{4,2,3,1,0:T(4,128)(2,1)} %bitcast.237), calls=%async_computation | async-start | bytes 1966080 | tf_op jit(solution)/shard_map/all_to_all | solution.py:174
  691.7 17.4 %collective-permute-start.106 = (f32[1,2,2,512]{3,2,1,0:T(2,128)S(1)}, f32[1,2,2,512]{3,2,1,0:T(2,128)S(1)}, u32[]{:S(2)}, u32[]{:S(2)}) collective-permute-start(f32[1,2,2,512]{3,2,1,0:T(2,128)S(1)} %add_add_fusion.7), channel_id=1, source_target_pairs={{0,4},{2,6},{4,0},{6,2},{1,5},{3,7},{5,1},{7,3},{8,12},{10,14},{12... | collective-permute-start | bytes 24584 | tf_op jit(solution)/shard_map/ppermute | solution.py:30
  720.8 33.0 %all-to-all-start.1 = ((bf16[16,8,4,6,128]{4,1,3,2,0:T(8,128)(2,1)}), bf16[16,8,4,6,128]{4,1,3,2,0:T(8,128)(2,1)S(1)}, u32[]{:S(2)}, u32[]{:S(2)}) async-start(bf16[16,8,4,6,128]{4,1,3,2,0:T(8,128)(2,1)} %bitcast.244), calls=%async_computation.1 | async-start | bytes 1572864 | tf_op jit(solution)/shard_map/all_to_all | solution.py:174
  727.9 137.9 %all-gather.14.cloned.1.call-start = ((), (), s32[]{:S(2)}) async-start(), calls=%async_computation.11 | async-start | bytes 4866048 | tf_op jit(solution)/shard_map/all_gather | solution.py:208
  (159 other events, 1768.3 us)
Sparse Core Ops, SparseCore 0:
  353.7 68.1 all-gather.11
  427.9 74.2 all-gather.21
  505.2 77.0 all-gather.19
  585.9 79.9 all-gather.17
  672.3 74.1 all-gather.15
  759.3 61.6 all-gather.13

commit v2 on v1

v2 whole, which is shorter than its diff:
```python
import functools

import jax
import jax.numpy as jnp
from jax import lax
from jax.experimental import pallas as pl
from jax.experimental.pallas import tpu as pltpu
from jax.sharding import PartitionSpec as P

TASKS = 2
CONVS = 3
DOMAINS = 2
CORES = 2
REP = 4

EPSILON = 1e-05
HIGHEST = lax.Precision.HIGHEST
BOTH = ("row", "col")


class Place:
    def __init__(self):
        self.rows, self.cols = lax.axis_size("row"), lax.axis_size("col")
        self.groups = self.cols // REP
        self.mirror = 2 if self.groups == 2 else 0
        self.row, self.col = lax.axis_index("row"), lax.axis_index("col")
        self.group, self.rep = self.col // REP, self.col % REP
        self.block = self.rep ^ (self.mirror * (self.group % 2))

    def across(self, k):
        return (k * REP) ^ (self.mirror if k % 2 else 0)

    def swap(self, value, row_bits, col_bits):
        pairs = [
            (i, ((i // self.cols) ^ row_bits) * self.cols + ((i % self.cols) ^ col_bits))
            for i in range(self.rows * self.cols)
        ]
        return lax.ppermute(value, BOTH, pairs)

    def stages(self):
        bits = []
        k = 2
        while k < self.rows:
            bits.append((k, 0))
            k *= 2
        k = 1
        while k < self.groups:
            bits.append((0, self.across(k)))
            k *= 2
        steps = [[(1, 0)]]
        for i in range(0, len(bits), 2):
            pair = bits[i : i + 2]
            if len(pair) == 2:
                (a, b), (c, d) = pair
                pair = [(a, b), (c, d), (a ^ c, b ^ d)]
            steps.append(pair)
        return steps

    def gather(self, tile, axis):
        width = tile.shape[axis]
        shape = list(tile.shape)
        shape[axis] = width * REP
        whole = jnp.zeros(shape, tile.dtype)
        for k in range(REP):
            piece = tile if k == 0 else self.swap(tile, 0, k)
            whole = lax.dynamic_update_slice_in_dim(whole, piece, (self.rep ^ k) * width, axis)
        return whole

    def own(self, tile, axis, extra=0):
        width = (tile.shape[axis] - extra) // REP
        return lax.dynamic_slice_in_dim(tile, self.rep * width, width + extra, axis)

    def halo(self, tiles, pads):
        def edges(dim):
            low, high = [], []
            for tile, pad in zip(tiles, pads):
                axis = tile.ndim - 4 + dim
                length = tile.shape[axis]
                low.append(lax.slice_in_dim(tile, 0, pad, axis=axis))
                high.append(lax.slice_in_dim(tile, length - pad, length, axis=axis))
            shapes = [t.shape for t in low]
            if len(tiles) == 1:
                return low[0], high[0], lambda whole: [whole]

            def join(pieces):
                return jnp.concatenate([p.reshape(-1, *p.shape[-2:]) for p in pieces])

            def split(whole):
                pieces, at = [], 0
                for shape in shapes:
                    count = 1
                    for s in shape[:-2]:
                        count *= s
                    pieces.append(whole[at : at + count].reshape(shape))
                    at += count
                return pieces

            return join(low), join(high), split

        def attach(before, after, split, dim):
            return [
                jnp.concatenate([b, tile, a], axis=tile.ndim - 4 + dim)
                for b, tile, a in zip(split(before), tiles, split(after))
            ]

        low, high, split = edges(0)
        even = self.row % 2 == 0
        near = lax.ppermute(
            jnp.where(even, high, low), "row", [(i, i ^ 1) for i in range(self.rows)]
        )
        pairs = []
        for i in range(1, self.rows - 1, 2):
            pairs += [(i, i + 1), (i + 1, i)]
        far = lax.ppermute(jnp.where(even, low, high), "row", pairs)
        tiles = attach(jnp.where(even, far, near), jnp.where(even, near, far), split, 0)

        low, high, split = edges(1)
        even = self.group % 2 == 0
        near = self.swap(jnp.where(even, high, low), 0, self.across(1))
        far = jnp.zeros_like(near)
        if self.groups > 2:
            pairs = []
            for i in range(self.cols - REP):
                if (i // REP) % 2:
                    pairs += [(i, i + REP), (i + REP, i)]
            far = lax.ppermute(jnp.where(even, low, high), "col", pairs)
        return attach(jnp.where(even, far, near), jnp.where(even, near, far), split, 1)

    def inside(self, height, breadth, pad):
        rows = self.row * height + jnp.arange(height + 2 * pad) - pad
        cols = self.group * breadth + jnp.arange(breadth + 2 * pad) - pad
        return (
            ((rows >= 0) & (rows < height * self.rows))[:, None]
            & ((cols >= 0) & (cols < breadth * self.groups))[None, :]
        )[:, :, None, None]

    def scatter(self, parts):
        m, rows, c = parts.shape
        per = rows // (self.rows * self.groups)
        halves = self.rows // CORES
        parts = parts.reshape(m, halves, CORES, self.groups, per, c)
        core, half = self.row % CORES, self.row // CORES

        def pick(value, index, axis):
            return lax.dynamic_index_in_dim(value, index, axis, keepdims=False)

        other = self.swap(pick(parts, 1 - core, 2).astype(jnp.bfloat16), 1, 0)
        parts = pick(parts, core, 2) + other.astype(jnp.float32)
        got = []
        for a in range(halves):
            for b in range(self.groups):
                piece = pick(pick(parts, half ^ a, 1), self.group ^ b, 1)
                if a or b:
                    piece = self.swap(piece.astype(jnp.bfloat16), a * CORES, self.across(b))
                got.append(piece.astype(jnp.float32))
        return tree_sum(got).astype(jnp.bfloat16)


def tree_sum(values):
    while len(values) > 1:
        values = [a + b for a, b in zip(values[::2], values[1::2])]
    return values[0]


def total_stats(place, average, squares, number):
    for step in place.stages():
        own = jnp.stack([average, squares])
        both = [own] + [place.swap(own, *bits) for bits in step]
        averages = [b[0] for b in both]
        average = tree_sum(averages) * (1.0 / len(both))
        squares = tree_sum([b[1] for b in both]) + number * tree_sum(
            [(a - average) * (a - average) for a in averages]
        )
        number = number * len(both)
    return average, squares / number


def total_sums(place, value):
    for step in place.stages():
        value = tree_sum([value] + [place.swap(value, *bits) for bits in step])
    return value


def inner(tile):
    return tile[1:-1, 1:-1]


def convolve(padded, kernel):
    return lax.conv_general_dilated(
        padded,
        kernel,
        (1, 1),
        "VALID",
        dimension_numbers=("HWNC", "HWIO", "HWNC"),
        preferred_element_type=jnp.float32,
    )


def convolve_back(padded_grad, kernel):
    return lax.conv_general_dilated(
        padded_grad,
        jnp.flip(kernel, (0, 1)),
        (1, 1),
        "VALID",
        dimension_numbers=("HWNC", "HWOI", "HWNC"),
        preferred_element_type=jnp.float32,
    )


def project(values, weight):
    return jnp.einsum("hwnc,cd->hwnd", values, weight, preferred_element_type=jnp.float32)


def project_back(values, weight):
    return jnp.einsum("hwnd,cd->hwnc", values, weight, preferred_element_type=jnp.float32)


def silu_slope(pre_act):
    logistic = jax.nn.sigmoid(pre_act)
    return logistic * (1.0 + pre_act * (1.0 - logistic))


def domain_totals(member, values):
    return jnp.dot(member.T, jnp.sum(values, axis=(0, 1)), precision=HIGHEST)


def per_image(member, stats):
    return jnp.dot(member, stats, precision=HIGHEST)[None, None]


def local_stats(member, tile, number):
    average = domain_totals(member, tile) / number
    centered = tile - per_image(member, average)
    return average, domain_totals(member, centered * centered)


def forward_stats(place, member, tiles, number):
    local = [local_stats(member, tile, number) for tile in tiles]
    average, variance = total_stats(
        place, jnp.stack([a for a, _ in local]), jnp.stack([s for _, s in local]), number[None]
    )
    return average, lax.rsqrt(variance + EPSILON)


def backward_sums(place, member, pairs):
    local = [
        jnp.stack([domain_totals(member, dy), domain_totals(member, dy * form)])
        for dy, form in pairs
    ]
    return total_sums(place, jnp.stack(local))


def backward_input(member, dy, form, inverse, gain, sums, counts):
    plain = per_image(member, sums[0] / counts[:, None])
    cross = per_image(member, sums[1] / counts[:, None])
    return per_image(member, inverse) * gain * (dy - plain - form * cross)


def mean_pool(values):
    h, w, n, c = values.shape
    return jnp.mean(values.reshape(h // 2, 2, w // 2, 2, n, c), axis=(1, 3))


def mean_pool_back(grad_out):
    h, w, n, c = grad_out.shape
    spread = jnp.broadcast_to(
        0.25 * grad_out[:, None, :, None].astype(jnp.float32), (h, 2, w, 2, n, c)
    )
    return spread.reshape(2 * h, 2 * w, n, c)


def kernel_part(act, grads):
    part = lax.conv_general_dilated(
        act,
        grads,
        (1, 1),
        "VALID",
        dimension_numbers=("HWCN", "HWIO", "HWNC"),
        preferred_element_type=jnp.float32,
    )
    return part.reshape(-1, *part.shape[2:])


def matrix_part(act, grads):
    return jnp.einsum("hwnc,hwnd->cd", act, grads, preferred_element_type=jnp.float32)[None]


def spread_kernel(groups, *refs):
    *sources, target = refs
    for g, source in enumerate(sources):
        rows, _, _, _, per, _ = source.shape
        for r in range(rows):
            at = (r * groups + g) * per
            target[:, at : at + per, :] = source[r, 0, 0].astype(jnp.float32)


def spread(place, gathered, start, count, step):
    rows, groups, _, _, per, c = gathered.shape
    block = rows * groups * per

    def source(g):
        return pl.BlockSpec(
            (rows, 1, 1, step, per, c),
            lambda i, b: (0, g, b ^ (place.mirror * (g % 2)), start // step + i, 0, 0),
        )

    return pl.pallas_call(
        functools.partial(spread_kernel, groups),
        out_shape=jax.ShapeDtypeStruct((count, REP * block, c), jnp.float32),
        grid=(count // step, REP),
        in_specs=[source(g) for g in range(groups)],
        out_specs=pl.BlockSpec((step, block, c), lambda i, b: (i, b, 0)),
        compiler_params=pltpu.CompilerParams(vmem_limit_bytes=32 * 1024 * 1024),
        cost_estimate=pl.CostEstimate(
            flops=0, bytes_accessed=6 * count * REP * block * c, transcendentals=0
        ),
        name="spread",
    )(*([gathered] * groups))


def gather_rows(place, chunk):
    whole = lax.all_gather(chunk, BOTH)
    return whole.reshape(place.rows, place.groups, REP, *chunk.shape)


def body(
    features,
    priors,
    domain,
    shared_w,
    shared_gain,
    shared_bias,
    first_w,
    second_w,
    task_conv,
    task_gain,
    task_bias,
    shared_cot,
    task_cot,
):
    place = Place()
    images, height, breadth, channels = features.shape
    wide = breadth * REP
    member = (domain[:, None] == jnp.arange(DOMAINS, dtype=jnp.int32)[None, :]).astype(jnp.float32)
    named = jnp.sum(member, axis=0)[:, None]
    number = named * (height * wide)
    counts = named[:, 0] * (height * wide * place.rows * place.groups)
    inside = place.inside(height, wide, 1)

    def only_inside(tile):
        return jnp.where(inside, tile, 0.0).astype(jnp.bfloat16)

    def mine(act):
        size = channels // REP
        return lax.dynamic_slice_in_dim(act, place.block * size, size, act.ndim - 1)

    features = place.gather(features.transpose(1, 2, 0, 3), 1)
    (features,) = place.halo([features], [2])
    priors = priors.transpose(0, 2, 3, 1, 4)
    cots = jnp.concatenate([task_cot, shared_cot[None]]).transpose(0, 2, 3, 1, 4)
    half_h, half_w = height // 2, breadth // 2
    small = TASKS * height
    rest = jnp.concatenate(
        [
            priors.reshape(small, breadth, images, channels),
            cots.reshape(-1, breadth, images, channels),
        ]
    )
    rest = place.gather(rest[:, None], 1)
    priors = rest[:small].reshape(TASKS, height, REP * breadth, images, channels)
    priors = rest[:small].reshape(TASKS, height, wide, images, channels)
    cots = (
        rest[small:]
        .reshape(TASKS + 1, half_h // 2, REP, 2, half_w, images, channels)
        .transpose(0, 1, 3, 2, 4, 5, 6)
        .reshape(TASKS + 1, half_h, REP * half_w, images, channels)
    )
    task_cot, shared_cot = cots[:TASKS], cots[TASKS]
    priors, shared_cot = place.halo([priors, shared_cot], [1, 1])

    def apply_norm(tile, average, inverse, gain, bias):
        form = (tile - per_image(member, average)) * per_image(member, inverse)
        return form, form * gain + bias

    product = convolve(features, shared_w[0])
    average, inverse = forward_stats(place, member, [inner(product)], number)
    inverse1 = inverse[0]
    form1, normed1 = apply_norm(product, average[0], inverse1, shared_gain[0], shared_bias[0])
    act1 = only_inside(jax.nn.silu(normed1))

    product = convolve(act1, shared_w[1])
    hidden = [
        project(act1, first_w[t, :channels]) + project(priors[t], first_w[t, channels:])
        for t in range(TASKS)
    ]
    average, inverse = forward_stats(
        place, member, [product] + [inner(h) for h in hidden], number
    )
    inverse2, inverse_h = inverse[0], inverse[1:]
    form2, normed2 = apply_norm(product, average[0], inverse2, shared_gain[1], shared_bias[1])
    (act2,) = place.halo([jax.nn.silu(normed2).astype(jnp.bfloat16)], [2])
    form_h, normed_h, hidden_act = [], [], []
    for t in range(TASKS):
        form, normed = apply_norm(
            hidden[t], average[1 + t], inverse_h[t], task_gain[t, 0], task_bias[t, 0]
        )
        form_h.append(form)
        normed_h.append(normed)
        hidden_act.append(jax.nn.silu(normed).astype(jnp.bfloat16))

    product = convolve(act2, shared_w[2])
    gate = [project(hidden_act[t], second_w[t]) for t in range(TASKS)]
    average, inverse = forward_stats(
        place, member, [inner(product)] + [inner(g) for g in gate], number
    )
    inverse3, inverse_g = inverse[0], inverse[1:]
    form3, normed3 = apply_norm(product, average[0], inverse3, shared_gain[2], shared_bias[2])
    last = jax.nn.silu(normed3)
    shared_out = mean_pool(place.own(inner(last), 1)).astype(jnp.bfloat16)
    form_g, attention, masked = [], [], []
    for t in range(TASKS):
        form, normed = apply_norm(
            gate[t], average[1 + t], inverse_g[t], task_gain[t, 1], task_bias[t, 1]
        )
        form_g.append(form)
        attention.append(jax.nn.sigmoid(normed))
        masked.append(only_inside(attention[t] * last))

    refined = [convolve(masked[t], task_conv[t]) for t in range(TASKS)]
    average, inverse_r = forward_stats(place, member, refined, number)
    form_r, dy_r, task_outs = [], [], []
    for t in range(TASKS):
        form, normed = apply_norm(
            refined[t], average[t], inverse_r[t], task_gain[t, 2], task_bias[t, 2]
        )
        form_r.append(form)
        task_outs.append(mean_pool(place.own(jax.nn.silu(normed), 1)).astype(jnp.bfloat16))
        dy_r.append(mean_pool_back(task_cot[t]) * silu_slope(normed))

    sums_r = backward_sums(place, member, [(dy_r[t], form_r[t]) for t in range(TASKS)])
    dv_r = jnp.stack(
        [
            backward_input(
                member, dy_r[t], form_r[t], inverse_r[t], task_gain[t, 2], sums_r[t], counts
            ).astype(jnp.bfloat16)
            for t in range(TASKS)
        ]
    )
    task_parts = [kernel_part(mine(masked[t]), dv_r[t]) for t in range(TASKS)]
    task_rows = gather_rows(place, place.scatter(jnp.concatenate(task_parts)))
    (dv_r,) = place.halo([dv_r], [2])
    grad_masked = [convolve_back(dv_r[t], task_conv[t]) for t in range(TASKS)]

    grad_last = inner(mean_pool_back(shared_cot))
    dy_g = []
    for t in range(TASKS):
        grad_last = grad_last + grad_masked[t] * attention[t]
        dy_g.append(grad_masked[t] * last * attention[t] * (1.0 - attention[t]))
    dy3 = grad_last * silu_slope(normed3)
    sums = backward_sums(
        place,
        member,
        [(inner(dy3), inner(form3))] + [(inner(dy_g[t]), inner(form_g[t])) for t in range(TASKS)],
    )
    sums3, sums_g = sums[0], sums[1:]
    dv3 = only_inside(
        backward_input(member, dy3, form3, inverse3, shared_gain[2], sums3, counts)
    )
    dv_g = [
        backward_input(
            member, dy_g[t], form_g[t], inverse_g[t], task_gain[t, 1], sums_g[t], counts
        ).astype(jnp.bfloat16)
        for t in range(TASKS)
    ]
    grad_act2 = convolve_back(dv3, shared_w[2])
    parts3 = [kernel_part(mine(inner(act2)), inner(dv3))]
    parts_s = [matrix_part(mine(inner(hidden_act[t])), inner(dv_g[t])) for t in range(TASKS)]

    dy2 = grad_act2 * silu_slope(normed2)
    dy_h = [project_back(dv_g[t], second_w[t]) * silu_slope(normed_h[t]) for t in range(TASKS)]
    sums = backward_sums(
        place,
        member,
        [(dy2, form2)] + [(inner(dy_h[t]), inner(form_h[t])) for t in range(TASKS)],
    )
    sums2, sums_h = sums[0], sums[1:]
    dv2 = backward_input(
        member, dy2, form2, inverse2, shared_gain[1], sums2, counts
    ).astype(jnp.bfloat16)
    parts2 = [kernel_part(mine(act1), dv2)]
    (dv2,) = place.halo([dv2], [2])
    dv_h = [
        backward_input(
            member, dy_h[t], form_h[t], inverse_h[t], task_gain[t, 0], sums_h[t], counts
        ).astype(jnp.bfloat16)
        for t in range(TASKS)
    ]
    grad_act1 = convolve_back(dv2, shared_w[1])
    for t in range(TASKS):
        grad_act1 = grad_act1 + project_back(dv_h[t], first_w[t, :channels])
    parts_f = []
    for t in range(TASKS):
        parts_f.append(matrix_part(mine(inner(act1)), inner(dv_h[t])))
        parts_f.append(matrix_part(mine(inner(priors[t])), inner(dv_h[t])))

    dy1 = grad_act1 * silu_slope(normed1)
    sums1 = backward_sums(place, member, [(inner(dy1), inner(form1))])[0]
    dv1 = only_inside(
        backward_input(member, dy1, form1, inverse1, shared_gain[0], sums1, counts)
    )
    parts1 = [kernel_part(mine(inner(features)), inner(dv1))]
    grad_features = convolve_back(place.own(dv1, 1, 2), shared_w[0])
    grad_priors = [
        project_back(place.own(inner(dv_h[t]), 1), first_w[t, channels:]) for t in range(TASKS)
    ]

    chunk = jnp.concatenate(
        [
            place.scatter(jnp.concatenate(parts_f + parts_s)),
            place.scatter(jnp.concatenate(parts1)),
            place.scatter(jnp.concatenate(parts2)),
            place.scatter(jnp.concatenate(parts3)),
        ]
    )
    rest_rows = gather_rows(place, chunk)
    taps = 9
    grad_first = spread(place, rest_rows, 0, 2 * TASKS, 2)
    grad_second = spread(place, rest_rows, 2 * TASKS, TASKS, 2)
    grad_shared = spread(place, rest_rows, 3 * TASKS, CONVS * taps, 3)
    grad_task = spread(place, task_rows, 0, TASKS * taps, 3)

    shared_sums = jnp.sum(jnp.stack([sums1, sums2, sums3]), axis=2)
    task_sums = jnp.sum(jnp.stack([sums_h, sums_g, sums_r], axis=1), axis=3)

    def images_first(tile):
        return tile.transpose(2, 0, 1, 3)

    return (
        images_first(shared_out),
        jnp.stack([images_first(o) for o in task_outs]),
        images_first(grad_features),
        jnp.stack([images_first(g) for g in grad_priors]),
        grad_shared.reshape(shared_w.shape),
        shared_sums[:, 1],
        shared_sums[:, 0],
        grad_first.reshape(first_w.shape),
        grad_second.reshape(second_w.shape),
        grad_task.reshape(task_conv.shape),
        task_sums[:, :, 1],
        task_sums[:, :, 0],
    )


def solution(mesh):
    return jax.shard_map(
        body,
        mesh=mesh,
        in_specs=(
            P(None, "row", "col", None),
            P(None, None, "row", "col", None),
            P(),
            P(),
            P(),
            P(),
            P(),
            P(),
            P(),
            P(),
            P(),
            P(None, "row", "col", None),
            P(None, None, "row", "col", None),
        ),
        out_specs=(
            P(None, "row", "col", None),
            P(None, None, "row", "col", None),
            P(None, "row", "col", None),
            P(None, None, "row", "col", None),
            P(),
            P(),
            P(),
            P(),
            P(),
            P(),
            P(),
            P(),
        ),
        check_vma=False,
    )
```

time: 918 us -> 637 us (0.69)
  starting transfers between devices: 265 us -> 114 us
  waiting for transfers between devices: 351 us -> 201 us
  local copies, waits for them, and re-layouts: 136 us -> 54.4 us
  matrix products: 83 us -> 151 us
  Pallas kernels: 0 us -> 35.2 us
    all_to_all x10 -> x0, waiting for transfers between devices: 242 us -> none  [to_blocks(): got = lax.all_to_all(cut, CHIPS, 0, 0)]
    all_gather x6 -> x2, waiting for transfers between devices: 0.01 us -> 110 us  [gather_rows(): whole = lax.all_gather(chunk, BOTH)]
    ppermute x120 -> x73, starting transfers between devices: 212 us -> 113 us  [the longest x63 95.4 us: swap(): return lax.ppermute(value, BOTH, pairs)]
    convert_element_type x18 -> x9, local copies, waits for them, and re-layouts: 90 us -> 1.55 us  [the longest x4 1.14 us: scatter(): other = self.swap(pick(parts, 1 - core, 2).astype(jnp.bfloat16), 1, 0)]
    all_to_all x10 -> x0, starting transfers between devices: 52.3 us -> none  [to_blocks(): got = lax.all_to_all(cut, CHIPS, 0, 0)]
    conv_general_dilated x4, matrix products: 17.9 us -> 53.4 us  [convolve_back(): lax.conv_general_dilated(padded_grad, jnp.flip(kernel, (0, 1)), (1, 1), '...]
    pallas_call x0 -> x4, Pallas kernels: none -> 35.2 us  [spread(): pl.pallas_call(functools.partial(spread_kernel, groups), out_shape=jax.Sh...]
    another operation x33 -> x27, other arithmetic: 27.6 us -> 0.31 us  [the longest x15 0.21 us: total_stats(): own = jnp.stack([average, squares])]
  transfers between devices with their start and end apart: 136 -> 75, of which waited for: 67 -> 40; matrix products, arithmetic and copies ran while one was open for 23% -> 20% of each run, Pallas kernels for 0% -> 2%
where the time goes in v2:
time: 637 us; the launch traced here: 633 us
  waiting for transfers between devices  201 us (32%)
  matrix products  151 us (24%)
  starting transfers between devices  114 us (18%)
  other arithmetic  59.9 us (9%)
  local copies, waits for them, and re-layouts  54.4 us (9%)
  Pallas kernels  35.2 us (6%)
  between operations  17.2 us (3%)
    all_gather x2, waiting for transfers between devices, gather_rows(): whole = lax.all_gather(chunk, BOTH)  110 us
    ppermute x63, starting transfers between devices, swap(): return lax.ppermute(value, BOTH, pairs)  95.4 us
    ppermute x63, waiting for transfers between devices, swap(): return lax.ppermute(value, BOTH, pairs)  89.6 us
    conv_general_dilated x4, matrix products, convolve_back(): lax.conv_general_dilated(padded_grad, jnp.flip(kernel, (0, 1)), (1, 1), '...  53.4 us
    conv_general_dilated x5, matrix products, convolve(): lax.conv_general_dilated(padded, kernel, (1, 1), 'VALID', dimension_numbe...  44 us
    pallas_call x4, Pallas kernels, spread(): pl.pallas_call(functools.partial(spread_kernel, groups), out_shape=jax.Sh...  35.2 us
    unnamed x285, local copies, waits for them, and re-layouts  27.4 us
    reduce_sum x23, other arithmetic, domain_totals(): return jnp.dot(member.T, jnp.sum(values, axis=(0, 1)), precision=HIGHEST)  14.5 us
  transfers between devices with their start and end apart: 75, of which 40 were waited for; matrix products, arithmetic and copies ran while one was open for 20% of the time, Pallas kernels for 2%

profile of v2, /device:TPU:0, one launch (start us, length us, event | category | flops | bytes accessed | tf_op | source)
XLA Modules:
  0.0 632.6 jit_solution(15835021754461636409)
XLA Ops:
  32.8 3.5 collective-permute-start.4
  38.7 3.7 collective-permute-start.5
  44.8 4.6 collective-permute-done.12
  49.8 5.2 collective-permute-done.5
  55.1 10.5 %fusion.18 = f32[10,18,6,512]{3,2,1,0:T(8,128)S(1)} fusion(bf16[3,3,3,512,512]{4,3,2,1,0:T(8,128)(2,1)S(1)} %copy-done.135, bf16[12,2,6,512]{3,2,1,0:T(8,128)(2,1)S(1)} %get-tuple-element.160, bf16[2,16,6,512]{3,2,1,0:T(8,128)(2,1)S(1)} %get-tuple-element.146, bf16[8,16,6,512]{3,2,1,0:T(8,128)(2,1)} %constant_dynamic-update-slice_fusion, ...), kind=kOutput, calls=%fused_computation.22 | convolution fusion | flops 5099028480 | bytes 8634368 | tf_op jit(solution)/shard_map/conv_general_dilated | solution.py:189
  82.9 6.7 %fusion.448 = (f32[6,512]{1,0:T(8,128)S(1)}, f32[8,16,6,512]{3,2,1,0:T(8,128)S(1)}) fusion(bf16[10,18,6,512]{3,2,1,0:T(8,128)(2,1)S(1)} %get-tuple-element.101, bf16[3,3,3,512,512]{4,3,2,1,0:T(8,128)(2,1)S(1)} %copy-done.135), kind=kOutput, calls=%fused_computation.831 | convolution fusion | flops 3624268800 | bytes 7778304 | tf_op jit(solution)/shard_map/conv_general_dilated | solution.py:189
  92.7 6.9 %collective-permute-done.15 = bf16[26,6,512]{2,1,0:T(8,128)(2,1)S(1)} collective-permute-done((bf16[26,6,512]{2,1,0:T(8,128)(2,1)S(1)}, bf16[26,6,512]{2,1,0:T(8,128)(2,1)S(1)}, u32[]{:S(2)}, u32[]{:S(2)}) %collective-permute-start.15) | collective-permute-done | bytes 159776 | tf_op jit(solution)/shard_map/ppermute | solution.py:38
  135.7 5.8 collective-permute-done.22
  141.6 9.1 %fusion.10 = f32[10,18,6,512]{3,2,1,0:T(8,128)S(1)} fusion(bf16[3,3,3,512,512]{4,3,2,1,0:T(8,128)(2,1)S(1)} %copy-done.135, bf16[12,2,6,512]{3,2,1,0:T(8,128)(2,1)S(1)} %get-tuple-element.158, bf16[2,16,6,512]{3,2,1,0:T(8,128)(2,1)S(1)} %get-tuple-element.144, bf16[8,16,6,512]{3,2,1,0:T(8,128)(2,1)S(1)} %multiply_convert_fusion.9, ...), kind=kOutput, calls=%fused_computation.14 | convolution fusion | flops 5099028480 | bytes 8896512 | tf_op jit(solution)/shard_map/conv_general_dilated | solution.py:189
  156.2 4.1 collective-permute-start.26
  169.2 4.0 select_convert_fusion.3
  174.4 9.0 %fusion.449 = (f32[6,512]{1,0:T(8,128)S(1)}, f32[8,16,6,512]{3,2,1,0:T(8,128)S(1)}) fusion(bf16[10,18,6,512]{3,2,1,0:T(8,128)(2,1)S(1)} %get-tuple-element.91, bf16[2,3,3,512,512]{4,3,2,1,0:T(8,128)(2,1)} %param.21), kind=kOutput, calls=%fused_computation.832 | convolution fusion | flops 3624268800 | bytes 7409664 | tf_op jit(solution)/shard_map/conv_general_dilated | solution.py:189
  183.6 8.8 %fusion.450 = (f32[6,512]{1,0:T(8,128)S(1)}, f32[8,16,6,512]{3,2,1,0:T(8,128)S(1)}) fusion(bf16[10,18,6,512]{3,2,1,0:T(8,128)(2,1)S(1)} %get-tuple-element.87, bf16[2,3,3,512,512]{4,3,2,1,0:T(8,128)(2,1)} %param.21), kind=kOutput, calls=%fused_computation.833 | convolution fusion | flops 3624268800 | bytes 7409664 | tf_op jit(solution)/shard_map/conv_general_dilated | solution.py:189
  233.5 7.3 %collective-permute-done.37 = bf16[2,12,2,6,512]{4,3,2,1,0:T(8,128)(2,1)S(1)} collective-permute-done((bf16[2,12,2,6,512]{4,3,2,1,0:T(8,128)(2,1)S(1)}, bf16[2,12,2,6,512]{4,3,2,1,0:T(8,128)(2,1)S(1)}, u32[]{:S(2)}, u32[]{:S(2)}) %collective-permute-start.37) | collective-permute-done | bytes 294944 | tf_op jit(solution)/shard_map/ppermute | solution.py:38
  242.3 13.0 %fusion.4 = f32[10,18,6,512]{3,2,1,0:T(8,128)} fusion(bf16[2,3,3,512,512]{4,3,2,1,0:T(8,128)(2,1)} %param.21, bf16[2,12,20,6,512]{4,3,2,1,0:T(8,128)(2,1)S(1)} %pad_maximum_fusion), kind=kOutput, calls=%fused_computation.8 | convolution fusion | flops 5096079360 | bytes 8896512 | tf_op jit(solution)/shard_map/conv_general_dilated | solution.py:200
  257.8 17.3 %fusion.31 = (f32[10,18,6,512]{3,2,1,0:T(8,128)}, f32[10,18,6,512]{3,2,1,0:T(8,128)}, f32[10,18,6,512]{3,2,1,0:T(8,128)}) fusion(f32[12,20,6,512]{3,2,1,0:T(8,128)} %bitcast.986, f32[10,18,6,512]{3,2,1,0:T(8,128)} %fusion.4, f32[10,18,6,512]{3,2,1,0:T(8,128)S(1)} %get-tuple-element.90, f32[512]{0:T(512)S(1)} %bitcast.1114, f32[512]{0:T(512)S(1)} %bitcast.1094, ...), kind=kOutput, calls=%fused_computation.37 | convolution fusion | flops 5113774080 | bytes 28078080 | tf_op jit(solution)/shard_map/conv_general_dilated | solution.py:200
  297.1 9.9 %fusion.434 = (f32[6,512]{1,0:T(8,128)S(1)}, f32[6,512]{1,0:T(8,128)S(1)}, f32[8,16,6,512]{3,2,1,0:T(8,128)S(1)}) fusion(f32[6,512]{1,0:T(8,128)S(1)} %copy-done.74, f32[8,16,6,512]{3,2,1,0:T(8,128)S(1)} %copy-done.13, f32[6,512]{1,0:T(8,128)S(1)} %copy-done.72, f32[512]{0:T(512)S(1)} %bitcast.1101, f32[512]{0:T(512)S(1)} %bitcast.1081, ...), kind=kOutput, calls=%fused_computation.821 | convolution fusion | flops 3629770752 | bytes 9023488 | tf_op jit(solution)/shard_map/conv_general_dilated | solution.py:200
  343.0 6.3 collective-permute-done.72
  350.4 5.1 collective-permute-done.71
  372.7 8.3 %collective-permute-done.48 = bf16[12,2,6,512]{3,2,1,0:T(8,128)(2,1)S(1)} collective-permute-done((bf16[12,2,6,512]{3,2,1,0:T(8,128)(2,1)S(1)}, bf16[12,2,6,512]{3,2,1,0:T(8,128)(2,1)S(1)}, u32[]{:S(2)}, u32[]{:S(2)}) %collective-permute-start.48) | collective-permute-done | bytes 147488 | tf_op jit(solution)/shard_map/ppermute | solution.py:38
  381.0 13.1 %multiply_multiply_fusion = f32[10,18,6,512]{3,2,1,0:T(8,128)S(1)} fusion(f32[10,18,6,512]{3,2,1,0:T(8,128)S(1)} %fusion.102, f32[10,18,6,512]{3,2,1,0:T(8,128)S(1)} %fusion.106, f32[10,18,6,512]{3,2,1,0:T(8,128)S(1)} %copy-done.10, bf16[3,3,3,512,512]{4,3,2,1,0:T(8,128)(2,1)} %param.16, bf16[12,2,6,512]{3,2,1,0:T(8,128)(2,1)S(1)} %get-tuple-element.156, ...), kind=kOutput, calls=%fused_computation.40 | convolution fusion | flops 5105664000 | bytes 15044608 | tf_op jit(solution)/shard_map/conv_general_dilated | solution.py:200
  415.4 4.9 collective-permute-done.56
  432.6 4.3 collective-permute-done.68
  441.7 4.9 collective-permute-start.60
  464.9 4.5 fusion.16
  471.1 5.3 all-gather.7.cloned.1.call-done
  476.4 3.7 copy-done.1
  480.1 11.9 %spread.7 = f32[18,512,512]{2,1,0:T(8,128)} custom-call(bf16[4,2,4,18,16,512]{5,4,3,2,1,0:T(8,128)(2,1)S(1)} %bitcast.966, bf16[4,2,4,18,16,512]{5,4,3,2,1,0:T(8,128)(2,1)S(1)} %bitcast.967), custom_call_target="tpu_custom_call" | custom-call | bytes 28311552 | tf_op jit(solution)/shard_map/spread/pallas_call | solution.py:307
  492.0 104.3 %all-gather.5.cloned.1.call-done = bf16[1056,16,512]{2,1,0:T(8,128)(2,1)} async-done(((bf16[33,16,512]{2,1,0:T(8,128)(2,1)}), bf16[1056,16,512]{2,1,0:T(8,128)(2,1)}) %all-gather.5.cloned.1.call-update) | async-done | bytes 17301520 | tf_op jit(solution)/shard_map/all_gather | solution.py:322
  596.3 5.9 copy-done
  602.2 17.7 %spread.4 = f32[27,512,512]{2,1,0:T(8,128)} custom-call(bf16[4,2,4,33,16,512]{5,4,3,2,1,0:T(8,128)(2,1)S(1)} %bitcast.960, bf16[4,2,4,33,16,512]{5,4,3,2,1,0:T(8,128)(2,1)S(1)} %bitcast.961), custom_call_target="tpu_custom_call" | custom-call | bytes 42467328 | tf_op jit(solution)/shard_map/spread/pallas_call | solution.py:307
  619.9 3.7 spread.5
  (731 shorter events, 282.3 us)
Async XLA Ops:
  7.2 469.2 %all-gather.7.cloned.1.call-start = ((), (), s32[]{:S(2)}) async-start(), calls=%async_computation.1 | async-start | bytes 9732096 | tf_op jit(solution)/shard_map/all_gather | solution.py:322
  9.0 15.7 %collective-permute-start = (bf16[8,4,6,512]{3,2,1,0:T(8,128)(2,1)}, bf16[8,4,6,512]{3,2,1,0:T(8,128)(2,1)}, u32[]{:S(2)}, u32[]{:S(2)}) collective-permute-start(bf16[8,4,6,512]{3,2,1,0:T(8,128)(2,1)} %bitcast.959), channel_id=1, source_target_pairs={{0,1},{1,0},{2,3},{3,2},{4,5},{5,4},{6,7},{7,6},{8,9},{9,8},{10,11... | collective-permute-start | bytes 589832 | tf_op jit(solution)/shard_map/ppermute | solution.py:38
  11.9 14.6 %collective-permute-start.1 = (bf16[8,4,6,512]{3,2,1,0:T(8,128)(2,1)}, bf16[8,4,6,512]{3,2,1,0:T(8,128)(2,1)}, u32[]{:S(2)}, u32[]{:S(2)}) collective-permute-start(bf16[8,4,6,512]{3,2,1,0:T(8,128)(2,1)} %bitcast.959), channel_id=1, source_target_pairs={{0,2},{1,3},{2,0},{3,1},{4,6},{5,7},{6,4},{7,5},{8,10},{9,11},{10,... | collective-permute-start | bytes 589832 | tf_op jit(solution)/shard_map/ppermute | solution.py:38
  13.5 14.7 %collective-permute-start.2 = (bf16[8,4,6,512]{3,2,1,0:T(8,128)(2,1)}, bf16[8,4,6,512]{3,2,1,0:T(8,128)(2,1)}, u32[]{:S(2)}, u32[]{:S(2)}) collective-permute-start(bf16[8,4,6,512]{3,2,1,0:T(8,128)(2,1)} %bitcast.959), channel_id=1, source_target_pairs={{0,3},{1,2},{2,1},{3,0},{4,7},{5,6},{6,5},{7,4},{8,11},{9,10},{10,... | collective-permute-start | bytes 589832 | tf_op jit(solution)/shard_map/ppermute | solution.py:38
  17.3 25.1 %collective-permute-start.10 = (bf16[22,1,4,6,512]{4,2,3,1,0:T(4,128)(2,1)}, bf16[22,1,4,6,512]{4,2,3,1,0:T(4,128)(2,1)}, u32[]{:S(2)}, u32[]{:S(2)}) collective-permute-start(bf16[22,1,4,6,512]{4,2,3,1,0:T(4,128)(2,1)} %copy.154), channel_id=1, source_target_pairs={{0,1},{1,0},{2,3},{3,2},{4,5},{5,4},{6,7},{7,6},{8,9},{9,8},{10,11... | collective-permute-start | bytes 1622024 | tf_op jit(solution)/shard_map/ppermute | solution.py:38
  19.2 24.4 %collective-permute-start.11 = (bf16[22,1,4,6,512]{4,2,3,1,0:T(4,128)(2,1)}, bf16[22,1,4,6,512]{4,2,3,1,0:T(4,128)(2,1)}, u32[]{:S(2)}, u32[]{:S(2)}) collective-permute-start(bf16[22,1,4,6,512]{4,2,3,1,0:T(4,128)(2,1)} %copy.154), channel_id=1, source_target_pairs={{0,2},{1,3},{2,0},{3,1},{4,6},{5,7},{6,4},{7,5},{8,10},{9,11},{10,... | collective-permute-start | bytes 1622024 | tf_op jit(solution)/shard_map/ppermute | solution.py:38
  24.7 24.7 %collective-permute-start.12 = (bf16[22,1,4,6,512]{4,2,3,1,0:T(4,128)(2,1)}, bf16[22,1,4,6,512]{4,2,3,1,0:T(4,128)(2,1)S(1)}, u32[]{:S(2)}, u32[]{:S(2)}) collective-permute-start(bf16[22,1,4,6,512]{4,2,3,1,0:T(4,128)(2,1)} %copy.154), channel_id=1, source_target_pairs={{0,3},{1,2},{2,1},{3,0},{4,7},{5,6},{6,5},{7,4},{8,11},{9,10},{10,... | collective-permute-start | bytes 1622024 | tf_op jit(solution)/shard_map/ppermute | solution.py:38
  38.7 16.3 %collective-permute-start.5 = (bf16[12,2,6,512]{3,2,1,0:T(8,128)(2,1)S(1)}, bf16[12,2,6,512]{3,2,1,0:T(8,128)(2,1)S(1)}, u32[]{:S(2)}, u32[]{:S(2)}) collective-permute-start(bf16[12,2,6,512]{3,2,1,0:T(8,128)(2,1)S(1)} %fusion.158), channel_id=1, source_target_pairs={{0,6},{1,7},{2,4},{3,5},{4,2},{5,3},{6,0},{7,1},{8,14},{9,15},{10,... | collective-permute-start | bytes 442376 | tf_op jit(solution)/shard_map/ppermute | solution.py:38
  67.9 9.3 %collective-permute-start.9 = (f32[2,1,2,512]{3,2,1,0:T(2,128)S(1)}, f32[2,1,2,512]{3,2,1,0:T(2,128)S(1)}, u32[]{:S(2)}, u32[]{:S(2)}) collective-permute-start(f32[2,1,2,512]{3,2,1,0:T(2,128)S(1)} %pad_maximum_fusion.39), channel_id=1, source_target_pairs={{0,22},{1,23},{2,20},{3,21},{4,18},{5,19},{6,16},{7,17},{8,30},{9,... | collective-permute-start | bytes 24584 | tf_op jit(solution)/shard_map/ppermute | solution.py:38
  73.4 16.8 %collective-permute-start.13 = (bf16[40,6,512]{2,1,0:T(8,128)(2,1)S(1)}, bf16[40,6,512]{2,1,0:T(8,128)(2,1)S(1)}, u32[]{:S(2)}, u32[]{:S(2)}) collective-permute-start(bf16[40,6,512]{2,1,0:T(8,128)(2,1)S(1)} %get-tuple-element.139), channel_id=1, source_target_pairs={{8,16},{16,8},{9,17},{17,9},{10,18},{18,10},{11,19},{19,11},{12,20... | collective-permute-start | bytes 737288 | tf_op jit(solution)/shard_map/ppermute | solution.py:114
  74.3 15.9 %collective-permute-start.14 = (bf16[40,6,512]{2,1,0:T(8,128)(2,1)S(1)}, bf16[40,6,512]{2,1,0:T(8,128)(2,1)S(1)}, u32[]{:S(2)}, u32[]{:S(2)}) collective-permute-start(bf16[40,6,512]{2,1,0:T(8,128)(2,1)S(1)} %get-tuple-element.140), channel_id=1, source_target_pairs={{0,8},{8,0},{16,24},{24,16},{1,9},{9,1},{17,25},{25,17},{2,10},{10... | collective-permute-start | bytes 737288 | tf_op jit(solution)/shard_map/ppermute | solution.py:108
  229.4 11.3 %collective-permute-start.37 = (bf16[2,12,2,6,512]{4,3,2,1,0:T(8,128)(2,1)S(1)}, bf16[2,12,2,6,512]{4,3,2,1,0:T(8,128)(2,1)S(1)}, u32[]{:S(2)}, u32[]{:S(2)}) collective-permute-start(bf16[2,12,2,6,512]{4,3,2,1,0:T(8,128)(2,1)S(1)} %fusion.130), channel_id=1, source_target_pairs={{0,6},{1,7},{2,4},{3,5},{4,2},{5,3},{6,0},{7,1},{8,14},{9,15},{10,... | collective-permute-start | bytes 884744 | tf_op jit(solution)/shard_map/ppermute | solution.py:38
  291.2 45.4 %collective-permute-start.69 = (bf16[18,2,2,16,512]{4,3,0,2,1:T(8,128)(2,1)S(1)}, bf16[18,2,2,16,512]{4,3,0,2,1:T(8,128)(2,1)S(1)}, u32[]{:S(2)}, u32[]{:S(2)}) collective-permute-start(bf16[18,2,2,16,512]{4,3,0,2,1:T(8,128)(2,1)S(1)} %fusion.75), channel_id=1, source_target_pairs={{0,8},{1,9},{2,10},{3,11},{4,12},{5,13},{6,14},{7,15},{8,0},{9,1},... | collective-permute-start | bytes 3538952 | tf_op jit(solution)/shard_map/ppermute | solution.py:38
  321.2 101.6 %collective-permute-start.65 = (bf16[9,2,2,16,512]{4,3,0,2,1:T(8,128)(2,1)}, bf16[9,2,2,16,512]{4,3,0,2,1:T(8,128)(2,1)}, u32[]{:S(2)}, u32[]{:S(2)}) collective-permute-start(bf16[9,2,2,16,512]{4,3,0,2,1:T(8,128)(2,1)} %fusion.87), channel_id=1, source_target_pairs={{0,8},{1,9},{2,10},{3,11},{4,12},{5,13},{6,14},{7,15},{8,0},{9,1},... | collective-permute-start | bytes 1769480 | tf_op jit(solution)/shard_map/ppermute | solution.py:38
  332.8 36.5 %collective-permute-start.46 = (bf16[2,16,6,512]{3,2,1,0:T(8,128)(2,1)}, bf16[2,16,6,512]{3,2,1,0:T(8,128)(2,1)}, u32[]{:S(2)}, u32[]{:S(2)}) collective-permute-start(bf16[2,16,6,512]{3,2,1,0:T(8,128)(2,1)} %get-tuple-element.124), channel_id=1, source_target_pairs={{8,16},{16,8},{9,17},{17,9},{10,18},{18,10},{11,19},{19,11},{12,20... | collective-permute-start | bytes 589832 | tf_op jit(solution)/shard_map/ppermute | solution.py:114
  337.3 12.1 %collective-permute-start.72 = (bf16[18,16,512]{2,1,0:T(8,128)(2,1)S(1)}, bf16[18,16,512]{2,1,0:T(8,128)(2,1)S(1)}, u32[]{:S(2)}, u32[]{:S(2)}) collective-permute-start(bf16[18,16,512]{2,1,0:T(8,128)(2,1)S(1)} %get-tuple-element.111), channel_id=1, source_target_pairs={{0,22},{1,23},{2,20},{3,21},{4,18},{5,19},{6,16},{7,17},{8,30},{9,... | collective-permute-start | bytes 884744 | tf_op jit(solution)/shard_map/ppermute | solution.py:38
  340.2 15.3 %collective-permute-start.71 = (bf16[18,16,512]{2,1,0:T(8,128)(2,1)S(1)}, bf16[18,16,512]{2,1,0:T(8,128)(2,1)S(1)}, u32[]{:S(2)}, u32[]{:S(2)}) collective-permute-start(bf16[18,16,512]{2,1,0:T(8,128)(2,1)S(1)} %get-tuple-element.112), channel_id=1, source_target_pairs={{0,16},{1,17},{2,18},{3,19},{4,20},{5,21},{6,22},{7,23},{8,24},{9,... | collective-permute-start | bytes 884744 | tf_op jit(solution)/shard_map/ppermute | solution.py:38
  340.7 14.9 %collective-permute-start.70 = (bf16[18,16,512]{2,1,0:T(8,128)(2,1)S(1)}, bf16[18,16,512]{2,1,0:T(8,128)(2,1)S(1)}, u32[]{:S(2)}, u32[]{:S(2)}) collective-permute-start(bf16[18,16,512]{2,1,0:T(8,128)(2,1)S(1)} %get-tuple-element.110), channel_id=1, source_target_pairs={{0,6},{1,7},{2,4},{3,5},{4,2},{5,3},{6,0},{7,1},{8,14},{9,15},{10,... | collective-permute-start | bytes 884744 | tf_op jit(solution)/shard_map/ppermute | solution.py:38
  349.3 20.0 %collective-permute-start.47 = (bf16[2,16,6,512]{3,2,1,0:T(8,128)(2,1)}, bf16[2,16,6,512]{3,2,1,0:T(8,128)(2,1)}, u32[]{:S(2)}, u32[]{:S(2)}) collective-permute-start(bf16[2,16,6,512]{3,2,1,0:T(8,128)(2,1)} %get-tuple-element.125), channel_id=1, source_target_pairs={{0,8},{8,0},{16,24},{24,16},{1,9},{9,1},{17,25},{25,17},{2,10},{10... | collective-permute-start | bytes 589832 | tf_op jit(solution)/shard_map/ppermute | solution.py:108
  356.5 239.8 %all-gather.5.cloned.1.call-start = ((), (), s32[]{:S(2)}) async-start(), calls=%async_computation | async-start | bytes 17842176 | tf_op jit(solution)/shard_map/all_gather | solution.py:322
  364.7 65.0 %collective-permute-start.61 = (bf16[9,2,2,16,512]{4,3,0,2,1:T(8,128)(2,1)S(1)}, bf16[9,2,2,16,512]{4,3,0,2,1:T(8,128)(2,1)S(1)}, u32[]{:S(2)}, u32[]{:S(2)}) collective-permute-start(bf16[9,2,2,16,512]{4,3,0,2,1:T(8,128)(2,1)S(1)} %fusion.86), channel_id=1, source_target_pairs={{0,8},{1,9},{2,10},{3,11},{4,12},{5,13},{6,14},{7,15},{8,0},{9,1},... | collective-permute-start | bytes 1769480 | tf_op jit(solution)/shard_map/ppermute | solution.py:38
  370.7 10.3 %collective-permute-start.48 = (bf16[12,2,6,512]{3,2,1,0:T(8,128)(2,1)S(1)}, bf16[12,2,6,512]{3,2,1,0:T(8,128)(2,1)S(1)}, u32[]{:S(2)}, u32[]{:S(2)}) collective-permute-start(bf16[12,2,6,512]{3,2,1,0:T(8,128)(2,1)S(1)} %fusion.156), channel_id=1, source_target_pairs={{0,6},{1,7},{2,4},{3,5},{4,2},{5,3},{6,0},{7,1},{8,14},{9,15},{10,... | collective-permute-start | bytes 442376 | tf_op jit(solution)/shard_map/ppermute | solution.py:38
  410.0 10.3 %collective-permute-start.56 = (bf16[6,16,512]{2,1,0:T(8,128)(2,1)S(1)}, bf16[6,16,512]{2,1,0:T(8,128)(2,1)S(1)}, u32[]{:S(2)}, u32[]{:S(2)}) collective-permute-start(bf16[6,16,512]{2,1,0:T(8,128)(2,1)S(1)} %get-tuple-element.133), channel_id=1, source_target_pairs={{0,22},{1,23},{2,20},{3,21},{4,18},{5,19},{6,16},{7,17},{8,30},{9,... | collective-permute-start | bytes 294920 | tf_op jit(solution)/shard_map/ppermute | solution.py:38
  413.3 9.5 %collective-permute-start.54 = (bf16[6,16,512]{2,1,0:T(8,128)(2,1)S(1)}, bf16[6,16,512]{2,1,0:T(8,128)(2,1)S(1)}, u32[]{:S(2)}, u32[]{:S(2)}) collective-permute-start(bf16[6,16,512]{2,1,0:T(8,128)(2,1)S(1)} %get-tuple-element.132), channel_id=1, source_target_pairs={{0,6},{1,7},{2,4},{3,5},{4,2},{5,3},{6,0},{7,1},{8,14},{9,15},{10,... | collective-permute-start | bytes 294920 | tf_op jit(solution)/shard_map/ppermute | solution.py:38
  420.3 21.1 %collective-permute-start.57 = (bf16[9,2,2,16,512]{4,3,0,2,1:T(8,128)(2,1)S(1)}, bf16[9,2,2,16,512]{4,3,0,2,1:T(8,128)(2,1)S(1)}, u32[]{:S(2)}, u32[]{:S(2)}) collective-permute-start(bf16[9,2,2,16,512]{4,3,0,2,1:T(8,128)(2,1)S(1)} %fusion.85), channel_id=1, source_target_pairs={{0,8},{1,9},{2,10},{3,11},{4,12},{5,13},{6,14},{7,15},{8,0},{9,1},... | collective-permute-start | bytes 1769480 | tf_op jit(solution)/shard_map/ppermute | solution.py:38
  424.3 12.6 %collective-permute-start.68 = (bf16[9,16,512]{2,1,0:T(8,128)(2,1)S(1)}, bf16[9,16,512]{2,1,0:T(8,128)(2,1)S(1)}, u32[]{:S(2)}, u32[]{:S(2)}) collective-permute-start(bf16[9,16,512]{2,1,0:T(8,128)(2,1)S(1)} %get-tuple-element.122), channel_id=1, source_target_pairs={{0,22},{1,23},{2,20},{3,21},{4,18},{5,19},{6,16},{7,17},{8,30},{9,... | collective-permute-start | bytes 442376 | tf_op jit(solution)/shard_map/ppermute | solution.py:38
  427.0 12.0 %collective-permute-start.67 = (bf16[9,16,512]{2,1,0:T(8,128)(2,1)S(1)}, bf16[9,16,512]{2,1,0:T(8,128)(2,1)S(1)}, u32[]{:S(2)}, u32[]{:S(2)}) collective-permute-start(bf16[9,16,512]{2,1,0:T(8,128)(2,1)S(1)} %get-tuple-element.123), channel_id=1, source_target_pairs={{0,16},{1,17},{2,18},{3,19},{4,20},{5,21},{6,22},{7,23},{8,24},{9,... | collective-permute-start | bytes 442376 | tf_op jit(solution)/shard_map/ppermute | solution.py:38
  428.4 12.9 %collective-permute-start.66 = (bf16[9,16,512]{2,1,0:T(8,128)(2,1)S(1)}, bf16[9,16,512]{2,1,0:T(8,128)(2,1)S(1)}, u32[]{:S(2)}, u32[]{:S(2)}) collective-permute-start(bf16[9,16,512]{2,1,0:T(8,128)(2,1)S(1)} %get-tuple-element.121), channel_id=1, source_target_pairs={{0,6},{1,7},{2,4},{3,5},{4,2},{5,3},{6,0},{7,1},{8,14},{9,15},{10,... | collective-permute-start | bytes 442376 | tf_op jit(solution)/shard_map/ppermute | solution.py:38
  429.9 16.7 %collective-permute-start.64 = (bf16[9,16,512]{2,1,0:T(8,128)(2,1)S(1)}, bf16[9,16,512]{2,1,0:T(8,128)(2,1)S(1)}, u32[]{:S(2)}, u32[]{:S(2)}) collective-permute-start(bf16[9,16,512]{2,1,0:T(8,128)(2,1)S(1)} %get-tuple-element.119), channel_id=1, source_target_pairs={{0,22},{1,23},{2,20},{3,21},{4,18},{5,19},{6,16},{7,17},{8,30},{9,... | collective-permute-start | bytes 442376 | tf_op jit(solution)/shard_map/ppermute | solution.py:38
  436.9 12.6 %collective-permute-start.63 = (bf16[9,16,512]{2,1,0:T(8,128)(2,1)S(1)}, bf16[9,16,512]{2,1,0:T(8,128)(2,1)S(1)}, u32[]{:S(2)}, u32[]{:S(2)}) collective-permute-start(bf16[9,16,512]{2,1,0:T(8,128)(2,1)S(1)} %get-tuple-element.120), channel_id=1, source_target_pairs={{0,16},{1,17},{2,18},{3,19},{4,20},{5,21},{6,22},{7,23},{8,24},{9,... | collective-permute-start | bytes 442376 | tf_op jit(solution)/shard_map/ppermute | solution.py:38
  439.0 10.5 %collective-permute-start.62 = (bf16[9,16,512]{2,1,0:T(8,128)(2,1)S(1)}, bf16[9,16,512]{2,1,0:T(8,128)(2,1)S(1)}, u32[]{:S(2)}, u32[]{:S(2)}) collective-permute-start(bf16[9,16,512]{2,1,0:T(8,128)(2,1)S(1)} %get-tuple-element.118), channel_id=1, source_target_pairs={{0,6},{1,7},{2,4},{3,5},{4,2},{5,3},{6,0},{7,1},{8,14},{9,15},{10,... | collective-permute-start | bytes 442376 | tf_op jit(solution)/shard_map/ppermute | solution.py:38
  441.7 10.8 %collective-permute-start.60 = (bf16[9,16,512]{2,1,0:T(8,128)(2,1)S(1)}, bf16[9,16,512]{2,1,0:T(8,128)(2,1)S(1)}, u32[]{:S(2)}, u32[]{:S(2)}) collective-permute-start(bf16[9,16,512]{2,1,0:T(8,128)(2,1)S(1)} %get-tuple-element.116), channel_id=1, source_target_pairs={{0,22},{1,23},{2,20},{3,21},{4,18},{5,19},{6,16},{7,17},{8,30},{9,... | collective-permute-start | bytes 442376 | tf_op jit(solution)/shard_map/ppermute | solution.py:38
  (181 other events, 1954.4 us)
Sparse Core Ops, SparseCore 0:
  356.6 119.7 all-gather.6
  480.0 116.2 all-gather.4

commit v3 on v2

v3 whole, which is shorter than its diff:
```python
import functools

import jax
import jax.numpy as jnp
from jax import lax
from jax.experimental import pallas as pl
from jax.experimental.pallas import tpu as pltpu
from jax.sharding import PartitionSpec as P

TASKS = 2
CONVS = 3
DOMAINS = 2
CORES = 2
REP = 4
TAPS = 9
LANES = 128
ROWS, WIDTH = 16, 256
PAD = 16

EPSILON = 1e-05
BOTH = ("row", "col")
MIB = 1024 * 1024


class Place:
    def __init__(self):
        self.rows, self.cols = lax.axis_size("row"), lax.axis_size("col")
        self.groups = self.cols // REP
        self.row, self.col = lax.axis_index("row"), lax.axis_index("col")
        self.group, self.rep = self.col // REP, self.col % REP

    def swap(self, value, row_bits, col_bits):
        pairs = [
            (i, ((i // self.cols) ^ row_bits) * self.cols + ((i % self.cols) ^ col_bits))
            for i in range(self.rows * self.cols)
        ]
        return lax.ppermute(value, BOTH, pairs)

    def stages(self):
        bits = []
        k = 2
        while k < self.rows:
            bits.append((k, 0))
            k *= 2
        k = 1
        while k < self.groups:
            bits.append((0, k * REP))
            k *= 2
        steps = [[(1, 0)]]
        for i in range(0, len(bits), 2):
            pair = bits[i : i + 2]
            if len(pair) == 2:
                (a, b), (c, d) = pair
                pair = [(a, b), (c, d), (a ^ c, b ^ d)]
            steps.append(pair)
        return steps

    def pieces(self, tile):
        return [tile] + [self.swap(tile, 0, k) for k in range(1, REP)]

    def gather(self, tile, axis):
        return self.join(self.pieces(tile), axis)

    def join(self, pieces, axis):
        bit = 1
        while bit < REP:
            odd = (self.rep & bit) != 0
            pieces = [jnp.where(odd, pieces[j ^ bit], pieces[j]) for j in range(REP)]
            bit *= 2
        return jnp.concatenate(pieces, axis=axis)

    def halo_rows(self, low, high):
        even = self.row % 2 == 0
        near = lax.ppermute(
            jnp.where(even, high, low), "row", [(i, i ^ 1) for i in range(self.rows)]
        )
        pairs = []
        for i in range(1, self.rows - 1, 2):
            pairs += [(i, i + 1), (i + 1, i)]
        far = lax.ppermute(jnp.where(even, low, high), "row", pairs)
        return jnp.where(even, far, near), jnp.where(even, near, far)

    def halo_cols(self, low, high):
        even = self.group % 2 == 0
        near = self.swap(jnp.where(even, high, low), 0, REP)
        far = jnp.zeros_like(near)
        if self.groups > 2:
            pairs = []
            for i in range(self.cols - REP):
                if (i // REP) % 2:
                    pairs += [(i, i + REP), (i + REP, i)]
            far = lax.ppermute(jnp.where(even, low, high), "col", pairs)
        return jnp.where(even, far, near), jnp.where(even, near, far)

    def halo(self, tiles, pad, images):
        size = pad * images
        count = len(tiles)

        def columns(tiles):
            def edge(at):
                edges = [t[..., at, :].reshape(-1, size, t.shape[-1]) for t in tiles]
                extra = -(size * count) % 8
                if extra:
                    edges.append(jnp.zeros((edges[0].shape[0], extra, edges[0].shape[-1]), edges[0].dtype))
                edges = jnp.concatenate(edges, axis=1)
                return edges.reshape(-1, edges.shape[-1])

            got = self.halo_cols(edge(slice(0, size)), edge(slice(-size, None)))
            shape = tiles[0].shape
            width = -(-(size * count) // 8) * 8
            got = [x.reshape(-1, width, x.shape[-1]) for x in got]
            return [
                [x[:, t * size : (t + 1) * size].reshape(*shape[:-2], size, shape[-1]) for x in got]
                for t in range(count)
            ]

        sides = columns(tiles)
        ends = self.halo_rows(
            jnp.stack([t[..., :pad, :, :] for t in tiles]),
            jnp.stack([t[..., -pad:, :, :] for t in tiles]),
        )
        ends = [(ends[0][t], ends[1][t]) for t in range(count)]
        corners = columns([jnp.concatenate(e, axis=-3) for e in ends])
        whole = []
        for tile, (above, below), side, corner in zip(tiles, ends, sides, corners):
            tile = jnp.concatenate([above, tile, below], axis=-3)
            before, after = (
                jnp.concatenate([x[..., :pad, :, :], y, x[..., pad:, :, :]], axis=-3)
                for x, y in zip(corner, side)
            )
            fill = jnp.zeros((*tile.shape[:-2], pad * PAD - 2 * size, tile.shape[-1]), tile.dtype)
            whole.append(jnp.concatenate([before, tile, after, fill], axis=-2))
        return whole

    def scatter_core(self, parts):
        m, rows, c = parts.shape
        per = rows // (self.rows * self.groups)
        parts = parts.reshape(m, self.rows // CORES, CORES, self.groups, per, c)
        core = self.row % CORES
        other = lax.dynamic_index_in_dim(parts, 1 - core, 2, keepdims=False)
        other = self.swap(other.astype(jnp.bfloat16), 1, 0)
        mine = lax.dynamic_index_in_dim(parts, core, 2, keepdims=False)
        return mine + other.astype(jnp.float32)

    def scatter_chips(self, parts):
        halves = self.rows // CORES
        cut = parts.shape[0] * 2 // 3

        def along_row(parts, axis=1):
            half = self.row // CORES
            got = []
            for a in range(halves):
                piece = lax.dynamic_index_in_dim(parts, half ^ a, axis, keepdims=False)
                if a:
                    piece = self.swap(piece.astype(jnp.bfloat16), a * CORES, 0)
                got.append(piece.astype(jnp.float32))
            return tree_sum(got)

        def along_col(parts, axis):
            got = []
            for b in range(self.groups):
                piece = lax.dynamic_index_in_dim(parts, self.group ^ b, axis, keepdims=False)
                if b:
                    piece = self.swap(piece.astype(jnp.bfloat16), 0, b * REP)
                got.append(piece.astype(jnp.float32))
            return tree_sum(got)

        first, last = along_row(parts[:cut]), along_col(parts[cut:], 2)
        first, last = lax.optimization_barrier((first, last))
        first, last = along_col(first, 1), along_row(last)
        return jnp.concatenate([first, last]).astype(jnp.bfloat16)


def tree_sum(values):
    while len(values) > 1:
        values = [a + b for a, b in zip(values[::2], values[1::2])]
    return values[0]


def total_stats(place, local, number):
    for step in place.stages():
        both = [local] + [place.swap(local, *bits) for bits in step]
        averages = [b[0] for b in both]
        average = tree_sum(averages) * (1.0 / len(both))
        squares = tree_sum([b[1] for b in both]) + number * tree_sum(
            [(a - average) * (a - average) for a in averages]
        )
        local = jnp.stack([average, squares])
        number = number * len(both)
    return jnp.stack([local[0], local[1] / number])


def total_sums(place, value):
    for step in place.stages():
        value = tree_sum([value] + [place.swap(value, *bits) for bits in step])
    return value


def sweep(rows, c, step):
    for lane in range(0, c, WIDTH):

        @pl.loop(0, rows // ROWS)
        def block(i):
            step(pl.ds(pl.multiple_of(i * ROWS, ROWS), ROWS), slice(lane, lane + WIDTH))


def own_lines(tile_ref):
    h = tile_ref.shape[0]
    border = (h - 8) // 2
    return border, h - border


def wide(column):
    return jnp.broadcast_to(column, (column.shape[0], WIDTH))


class Norm:
    def __init__(self, sel_ref, stat_ref, gb_ref, i, at):
        rows, self.lanes = at
        self.first = wide(sel_ref[rows, 0:1]) > 0.5
        self.average = self.by_row(stat_ref[0, i, :, self.lanes])
        self.inverse = self.by_row(lax.rsqrt(stat_ref[1, i, :, self.lanes] + EPSILON))
        self.gain = gb_ref[i, 0:1, self.lanes]
        self.half_gain, self.half_bias = 0.5 * self.gain, 0.5 * gb_ref[i, 1:2, self.lanes]

    def by_row(self, pair):
        return jnp.where(self.first, pair[0:1], pair[1:2])

    def form(self, value):
        return (value - self.average) * self.inverse

    def half(self, form):
        return form * self.half_gain + self.half_bias

    def fold(self):
        self.times = self.inverse * self.half_gain
        self.plus = self.half_bias - self.average * self.times
        return self

    def __call__(self, value):
        return value * self.times + self.plus

    def set_sums(self, sums_ref, scal_ref, i):
        plain, cross = (
            self.by_row(
                jnp.concatenate(
                    [sums_ref[i, j, k : k + 1, self.lanes] * scal_ref[2 + k] for k in range(DOMAINS)]
                )
            )
            for j in range(2)
        )
        self.scale = self.inverse * self.gain
        self.plain, self.cross = plain, cross

    def back(self, dy, value):
        return self.scale * (dy - self.plain - self.form(value) * self.cross)


def sigmoid(t):
    return 0.5 * jnp.tanh(t) + 0.5


def silu(t):
    return t + t * jnp.tanh(t)


def silu_slope(t, h):
    return (0.5 + 0.5 * h) * (1.0 + t * (1.0 - h))


def slope(t):
    return silu_slope(t, jnp.tanh(t))


def seen(sel_ref, scal_ref, rows, lines):
    column = wide(sel_ref[rows, 3:4])
    return [column * scal_ref[4]] + [column] * (lines - 2) + [column * scal_ref[5]]


def add_by_domain(sel_ref, rows, values, out, lanes):
    for k in range(DOMAINS):
        out[k : k + 1, lanes] += jnp.sum(
            values * wide(sel_ref[rows, 1 + k : 2 + k]), axis=0, keepdims=True
        )


def local_stats(tile_ref, sel_ref, scal_ref, out_ref, i):
    _, r, c = tile_ref.shape
    lines = range(*own_lines(tile_ref))
    out_ref[:, i] = jnp.zeros((2, DOMAINS, c), jnp.float32)

    def total(rows, lanes):
        value = tree_sum([tile_ref[h, rows, lanes] for h in lines])
        add_by_domain(sel_ref, rows, value, out_ref.at[0, i], lanes)

    sweep(r, c, total)
    for k in range(DOMAINS):
        out_ref[0, i, k : k + 1] = out_ref[0, i, k : k + 1] * scal_ref[k]

    def square(rows, lanes):
        average = jnp.where(
            wide(sel_ref[rows, 0:1]) > 0.5, out_ref[0, i, 0:1, lanes], out_ref[0, i, 1:2, lanes]
        )
        apart = [tile_ref[h, rows, lanes] - average for h in lines]
        add_by_domain(sel_ref, rows, tree_sum([a * a for a in apart]), out_ref.at[1, i], lanes)

    sweep(r, c, square)


def fetch(w_ref, wv_ref, sem, start, back=False):
    c = w_ref.shape[-1]
    copies = []
    for t in range(TAPS):
        part = pl.ds((t % 3) * c, c)
        if back:
            source, target = w_ref.at[start + TAPS - 1 - t], wv_ref.at[t // 3, :, part]
        else:
            source, target = w_ref.at[start + t], wv_ref.at[t // 3, part, :]
        copies.append(pltpu.make_async_copy(source, target, sem.at[t]))
        copies[-1].start()
    return copies


def convolve(x_ref, xs_ref, wv_ref, copies, o_ref, images, back=False):
    hp, rp, c = x_ref.shape
    r = rp - PAD
    m = (hp - 2) * r
    for b in range(3):
        xs_ref[:, b * c : (b + 1) * c] = x_ref[:, b * images : b * images + r, :].reshape(hp * r, c)
    for a in range(3):
        for b in range(3):
            copies[3 * a + b].wait()
        part = lax.dot_general(
            xs_ref[a * r : a * r + m, :],
            wv_ref[a],
            (((1,), (1 if back else 0,)), ((), ())),
            preferred_element_type=jnp.float32,
        ).reshape(o_ref.shape)
        o_ref[...] = part if a == 0 else o_ref[...] + part


def flat(ref):
    h, r, c = ref.shape
    return ref[...].reshape(h * r, c)


def matmul(a, b):
    return jnp.dot(a, b, preferred_element_type=jnp.float32)


def matmul_back(a, b):
    return lax.dot_general(a, b, (((1,), (1,)), ((), ())), preferred_element_type=jnp.float32)


def first_kernel(images, tap, x_ref, w_ref, sel_ref, scal_ref, p_ref, st_ref, xs_ref, wv_ref, sem):
    copies = fetch(w_ref, wv_ref, sem, tap)
    convolve(x_ref, xs_ref, wv_ref, copies, p_ref, images)
    local_stats(p_ref, sel_ref, scal_ref, st_ref, 0)


def second_kernel(
    images, p1_ref, w_ref, st1_ref, gb_ref, sel_ref, sel0_ref, scal_ref,
    act_ref, p2_ref, st_ref, xs_ref, wv_ref, sem,
):
    copies = fetch(w_ref, wv_ref, sem, TAPS)
    lines, r, c = p1_ref.shape

    def activate(rows, lanes):
        norm = Norm(sel_ref, st1_ref, gb_ref, 0, (rows, lanes)).fold()
        for h, inside in enumerate(seen(sel_ref, scal_ref, rows, lines)):
            act_ref[h, rows, lanes] = (silu(norm(p1_ref[h, rows, lanes])) * inside).astype(
                jnp.bfloat16
            )

    sweep(r, c, activate)
    convolve(act_ref, xs_ref, wv_ref, copies, p2_ref, images)
    local_stats(p2_ref, sel0_ref, scal_ref, st_ref, 0)


def hidden_kernel(act_ref, pr_ref, fw_ref, sel_ref, scal_ref, h0_ref, h1_ref, st_ref):
    lines, r, c = act_ref.shape
    for t, h_ref in enumerate((h0_ref, h1_ref)):
        value = matmul(flat(act_ref), fw_ref[t, :c])
        h_ref[...] = (value + matmul(pr_ref[t].reshape(lines * r, c), fw_ref[t, c:])).reshape(
            h_ref.shape
        )
        local_stats(h_ref, sel_ref, scal_ref, st_ref, t)


def act_kernel(which, p_ref, st_ref, gb_ref, sel_ref, act_ref):
    lines, r, c = p_ref.shape

    def activate(rows, lanes):
        norm = Norm(sel_ref, st_ref, gb_ref, which, (rows, lanes)).fold()
        for h in range(lines):
            act_ref[h, rows, lanes] = silu(norm(p_ref[h, rows, lanes])).astype(jnp.bfloat16)

    sweep(r, c, activate)


def gate_kernel(
    h0_ref, h1_ref, sw_ref, st2_ref, gb_ref, sel_ref, scal_ref, a0_ref, a1_ref, g0_ref, g1_ref, st_ref,
):
    for t, (h_ref, a_ref, g_ref) in enumerate(((h0_ref, a0_ref, g0_ref), (h1_ref, a1_ref, g1_ref))):
        act_kernel(1 + t, h_ref, st2_ref, gb_ref, sel_ref, a_ref)
        g_ref[...] = matmul(flat(a_ref), sw_ref[t]).reshape(g_ref.shape)
        local_stats(g_ref, sel_ref, scal_ref, st_ref, t)


def fourth_kernel(
    images, p3_ref, g0_ref, g1_ref, w_ref, st3_ref, gb_ref, sel_ref, sel0_ref, scal_ref,
    m0_ref, m1_ref, r0_ref, r1_ref, st_ref, xs_ref, wv_ref, sem, wv2_ref, sem2,
):
    copies = [fetch(w_ref, wv_ref, sem, 0), fetch(w_ref, wv2_ref, sem2, TAPS)]
    lines, r, c = p3_ref.shape

    def mask(rows, lanes):
        norm = Norm(sel_ref, st3_ref, gb_ref, 0, (rows, lanes)).fold()
        gates = [
            Norm(sel_ref, st3_ref, gb_ref, 1 + t, (rows, lanes)).fold() for t in range(TASKS)
        ]
        for h, inside in enumerate(seen(sel_ref, scal_ref, rows, lines)):
            last = silu(norm(p3_ref[h, rows, lanes])) * inside
            for gate, g_ref, m_ref in zip(gates, (g0_ref, g1_ref), (m0_ref, m1_ref)):
                attention = sigmoid(gate(g_ref[h, rows, lanes]))
                m_ref[h, rows, lanes] = (attention * last).astype(jnp.bfloat16)

    sweep(r, c, mask)
    convolve(m0_ref, xs_ref, wv_ref, copies[0], r0_ref, images)
    convolve(m1_ref, xs_ref, wv2_ref, copies[1], r1_ref, images)
    local_stats(r0_ref, sel0_ref, scal_ref, st_ref, 0)
    local_stats(r1_ref, sel0_ref, scal_ref, st_ref, 1)


def store_sums(sel_ref, rows, lanes, out_ref, i, dys, forms):
    add_by_domain(sel_ref, rows, tree_sum(list(dys)), out_ref.at[i, 0], lanes)
    cross = tree_sum([dy * form for dy, form in zip(dys, forms)])
    add_by_domain(sel_ref, rows, cross, out_ref.at[i, 1], lanes)


def upsample(up_ref, low_ref, out_ref):
    for h in range(low_ref.shape[0]):
        out_ref[h] = matmul(up_ref[...], low_ref[h])


def refined_sums_kernel(
    r0_ref, r1_ref, c0_ref, c1_ref, up_ref, st_ref, gb_ref, sel_ref, out_ref, dy_ref, low_ref
):
    lines, r, c = r0_ref.shape
    out_ref[...] = jnp.zeros_like(out_ref)
    for t, (r_ref, c_ref) in enumerate(((r0_ref, c0_ref), (r1_ref, c1_ref))):
        upsample(up_ref, c_ref, low_ref)

        def sums(rows, lanes):
            norm = Norm(sel_ref, st_ref, gb_ref, t, (rows, lanes))
            dys, forms = [], []
            for h in range(lines):
                forms.append(norm.form(r_ref[h, rows, lanes]))
                dys.append(low_ref[h // 2, rows, lanes] * slope(norm.half(forms[-1])))
                dy_ref[t, h, rows, lanes] = dys[-1]
            store_sums(sel_ref, rows, lanes, out_ref, t, dys, forms)

        sweep(r, c, sums)


def refined_back_kernel(
    r0_ref, r1_ref, dy_ref, st_ref, gb_ref, sums_ref, sel_ref, scal_ref, dv0_ref, dv1_ref
):
    for t, (r_ref, dv_ref) in enumerate(((r0_ref, dv0_ref), (r1_ref, dv1_ref))):
        back_kernel(
            t, False, dy_ref.at[t], r_ref, st_ref, gb_ref, sums_ref, sel_ref, scal_ref, dv_ref
        )


def conv_back_kernel(images, start, x_ref, w_ref, o_ref, xs_ref, wv_ref, sem):
    copies = fetch(w_ref, wv_ref, sem, start, True)
    convolve(x_ref, xs_ref, wv_ref, copies, o_ref, images, True)


def masked_back_kernel(
    images, dv_ref, w_ref, grad_ref, p3_ref, g0_ref, g1_ref, cot_ref, up_ref, st3_ref, gb_ref,
    sel_ref, dy3_ref, dy0_ref, dy1_ref, sums_ref, xs_ref, wv_ref, sem, low_ref,
):
    copies = fetch(w_ref, wv_ref, sem, TAPS, True)
    convolve(dv_ref, xs_ref, wv_ref, copies, dy1_ref, images, True)
    lines, r, c = p3_ref.shape
    own = slice(*own_lines(p3_ref))
    upsample(up_ref, cot_ref, low_ref)
    sums_ref[...] = jnp.zeros_like(sums_ref)

    def step(rows, lanes):
        norm = Norm(sel_ref, st3_ref, gb_ref, 0, (rows, lanes))
        gates = [Norm(sel_ref, st3_ref, gb_ref, 1 + t, (rows, lanes)) for t in range(TASKS)]
        dys, forms = [[], [], []], [[], [], []]
        for h in range(lines):
            form = norm.form(p3_ref[h, rows, lanes])
            half = norm.half(form)
            tanh = jnp.tanh(half)
            last = half + half * tanh
            grad_last = low_ref[(h + 1) // 2, rows, lanes]
            for i, (gate, g_ref, from_ref, d_ref) in enumerate(
                zip(gates, (g0_ref, g1_ref), (grad_ref, dy1_ref), (dy0_ref, dy1_ref))
            ):
                gate_form = gate.form(g_ref[h, rows, lanes])
                attention = sigmoid(gate.half(gate_form))
                grad = from_ref[h, rows, lanes] * attention
                grad_last = grad_last + grad
                dy = grad * last * (1.0 - attention)
                d_ref[h, rows, lanes] = dy
                dys[1 + i].append(dy)
                forms[1 + i].append(gate_form)
            dy = grad_last * silu_slope(half, tanh)
            dy3_ref[h, rows, lanes] = dy
            dys[0].append(dy)
            forms[0].append(form)
        for i in range(3):
            store_sums(sel_ref, rows, lanes, sums_ref, i, dys[i][own], forms[i][own])

    sweep(r, c, step)


def slope_sums(which, out_at, grad_ref, add_ref, p_ref, st_ref, gb_ref, sel_ref, sums_ref):
    lines, r, c = p_ref.shape
    own = slice(*own_lines(p_ref))

    def step(rows, lanes):
        norm = Norm(sel_ref, st_ref, gb_ref, which, (rows, lanes))
        dys, forms = [], []
        for h in range(lines):
            form = norm.form(p_ref[h, rows, lanes])
            grad = grad_ref[h, rows, lanes]
            if add_ref is not None:
                grad = grad + add_ref[h, rows, lanes]
            dy = grad * slope(norm.half(form))
            grad_ref[h, rows, lanes] = dy
            dys.append(dy)
            forms.append(form)
        store_sums(sel_ref, rows, lanes, sums_ref, out_at, dys[own], forms[own])

    sweep(r, c, step)


def back_kernel(which, masked, dy_ref, p_ref, st_ref, gb_ref, sums_ref, sel_ref, scal_ref, dv_ref):
    lines, r, c = p_ref.shape

    def step(rows, lanes):
        norm = Norm(sel_ref, st_ref, gb_ref, which, (rows, lanes))
        norm.set_sums(sums_ref, scal_ref, which)
        inside = seen(sel_ref, scal_ref, rows, lines)
        for h in range(lines):
            dv = norm.back(dy_ref[h, rows, lanes], p_ref[h, rows, lanes])
            if masked:
                dv = dv * inside[h]
            dv_ref[h, rows, lanes] = dv.astype(jnp.bfloat16)

    sweep(r, c, step)


def third_back_kernel(
    images, dy3_ref, p3_ref, p2_ref, w_ref, st3_ref, gb3_ref, sums_ref, st2_ref, gb2_ref,
    sel_ref, sel0_ref, scal_ref, dv3_ref, dy2_ref, out_ref, xs_ref, wv_ref, sem,
):
    copies = fetch(w_ref, wv_ref, sem, 2 * TAPS, True)
    back_kernel(0, True, dy3_ref, p3_ref, st3_ref, gb3_ref, sums_ref, sel_ref, scal_ref, dv3_ref)
    convolve(dv3_ref, xs_ref, wv_ref, copies, dy2_ref, images, True)
    out_ref[...] = jnp.zeros_like(out_ref)
    slope_sums(0, 0, dy2_ref, None, p2_ref, st2_ref, gb2_ref, sel0_ref, out_ref)


def gate_back_kernel(
    dy0_ref, dy1_ref, g0_ref, g1_ref, h0_ref, h1_ref, sw_ref, st3_ref, gb3_ref, sums_ref,
    st2_ref, gb2_ref, sel_ref, scal_ref, dv0_ref, dv1_ref, dh0_ref, dh1_ref, out_ref,
):
    out_ref[...] = jnp.zeros_like(out_ref)
    for t, (dy_ref, g_ref, dv_ref, h_ref, dh_ref) in enumerate(
        (
            (dy0_ref, g0_ref, dv0_ref, h0_ref, dh0_ref),
            (dy1_ref, g1_ref, dv1_ref, h1_ref, dh1_ref),
        )
    ):
        back_kernel(
            1 + t, False, dy_ref, g_ref, st3_ref, gb3_ref, sums_ref, sel_ref, scal_ref, dv_ref
        )
        dh_ref[...] = matmul_back(flat(dv_ref), sw_ref[t]).reshape(dh_ref.shape)
        slope_sums(1 + t, t, dh_ref, None, h_ref, st2_ref, gb2_ref, sel_ref, out_ref)


def hidden_back_kernel(
    dyh0_ref, dyh1_ref, h0_ref, h1_ref, fw_ref, st_ref, gb_ref, sums_ref, sel_ref, scal_ref,
    dv0_ref, dv1_ref, grad_ref,
):
    _, _, c = h0_ref.shape
    for t, (dy_ref, h_ref, dv_ref) in enumerate(
        ((dyh0_ref, h0_ref, dv0_ref), (dyh1_ref, h1_ref, dv1_ref))
    ):
        back_kernel(1 + t, False, dy_ref, h_ref, st_ref, gb_ref, sums_ref, sel_ref, scal_ref, dv_ref)
        value = matmul_back(flat(dv_ref), fw_ref[t, :c]).reshape(grad_ref.shape)
        grad_ref[...] = value if t == 0 else grad_ref[...] + value


def second_back_kernel(
    images, dv2_ref, w_ref, add_ref, p1_ref, st_ref, gb_ref, sel_ref,
    dy_ref, sums_ref, xs_ref, wv_ref, sem,
):
    copies = fetch(w_ref, wv_ref, sem, TAPS, True)
    convolve(dv2_ref, xs_ref, wv_ref, copies, dy_ref, images, True)
    sums_ref[...] = jnp.zeros_like(sums_ref)
    slope_sums(0, 0, dy_ref, add_ref, p1_ref, st_ref, gb_ref, sel_ref, sums_ref)


def parts_kernel(plan, images, block_ref, *refs):
    *sources, out_ref, xs_ref = refs
    at = 0
    for x, g, conv in plan:
        x_ref, g_ref = sources[x], sources[g]
        border = (g_ref.shape[0] - 8) // 2
        cols = g_ref.shape[1] - border * PAD
        k = 8 * cols
        grad = g_ref[border : border + 8, border * images : border * images + cols, :]
        grad = grad.reshape(k, grad.shape[-1])
        border = (x_ref.shape[0] - 8) // 2
        taps = [(a, b) for a in (-1, 0, 1) for b in (-1, 0, 1)] if conv else [(0, 0)]
        for t, (a, b) in enumerate(taps):
            start = (border + b) * images
            xs_ref[:, t * LANES : (t + 1) * LANES] = x_ref[
                border + a : border + a + 8, start : start + cols, :
            ].reshape(k, LANES)
        size = len(taps) * LANES
        part = lax.dot_general(
            xs_ref[:, :size], grad, (((0,), (0,)), ((), ())), preferred_element_type=jnp.float32
        )
        out_ref[at : at + len(taps)] = part.reshape(len(taps), LANES, part.shape[-1])
        at += len(taps)


def parts(place, plan, images, acts, grads):
    c = grads[0].shape[-1]
    count = sum(TAPS if conv else 1 for _, _, conv in plan)

    def act_spec(x):
        return pl.BlockSpec((*x.shape[:2], LANES), lambda i, b: (0, 0, b[0]))

    def grad_spec(x):
        return pl.BlockSpec(x.shape, lambda i, b: (0, 0, 0))

    return pl.pallas_call(
        functools.partial(parts_kernel, plan, images),
        out_shape=jax.ShapeDtypeStruct((count, LANES, c), jnp.float32),
        grid_spec=pltpu.PrefetchScalarGridSpec(
            num_scalar_prefetch=1,
            grid=(1,),
            in_specs=[act_spec(x) for x in acts] + [grad_spec(x) for x in grads],
            out_specs=pl.BlockSpec((count, LANES, c), lambda i, b: (0, 0, 0)),
            scratch_shapes=[pltpu.VMEM((8 * 16 * images, TAPS * LANES), jnp.bfloat16)],
        ),
        compiler_params=pltpu.CompilerParams(vmem_limit_bytes=32 * MIB),
        name="parts",
    )(place.rep.astype(jnp.int32)[None], *acts, *grads)


def spread_kernel(groups, sources_per, *refs):
    sources, targets = refs[: groups * sources_per], refs[groups * sources_per :]
    at = 0
    places = [(target, i) for target in targets for i in range(target.shape[0])]
    for s in range(sources_per):
        for i in range(sources[0].shape[3]):
            target, m = places[s * sources[0].shape[3] + i]
            for g in range(groups):
                source = sources[s * groups + g]
                rows, _, _, _, per, _ = source.shape
                for r in range(rows):
                    at = (r * groups + g) * per
                    target[m, at : at + per, :] = source[r, 0, 0, i].astype(jnp.float32)


def spread(place, gathered, start, counts, step):
    rows, groups, _, _, per, c = gathered.shape
    block = rows * groups * per
    sources = 1 if len(counts) == 1 else sum(counts) // step

    def source(s, g):
        return pl.BlockSpec(
            (rows, 1, 1, step, per, c),
            lambda i, b: (0, g, b, start // step + s + i, 0, 0),
        )

    takes = [step] if len(counts) == 1 else counts
    return pl.pallas_call(
        functools.partial(spread_kernel, groups, sources),
        out_shape=[jax.ShapeDtypeStruct((n, REP * block, c), jnp.float32) for n in counts],
        grid=(sum(counts) // (step * sources), REP),
        in_specs=[source(s, g) for s in range(sources) for g in range(groups)],
        out_specs=[pl.BlockSpec((n, block, c), lambda i, b: (i, b, 0)) for n in takes],
        compiler_params=pltpu.CompilerParams(vmem_limit_bytes=58 * MIB),
        cost_estimate=pl.CostEstimate(
            flops=0, bytes_accessed=6 * sum(counts) * REP * block * c, transcendentals=0
        ),
        name="spread",
    )(*([gathered] * (groups * sources)))


def gather_rows(place, chunk):
    whole = lax.all_gather(chunk, BOTH)
    return whole.reshape(place.rows, place.groups, REP, *chunk.shape)


VMEM_SPEC = pl.BlockSpec(memory_space=pltpu.VMEM)
SMEM_SPEC = pl.BlockSpec(memory_space=pltpu.SMEM)
HBM_SPEC = pl.BlockSpec(memory_space=pltpu.HBM)


def call(kernel, name, ins, outs, shift=None, weights=0, back=False, extra=(), limit=32):
    specs = {"v": VMEM_SPEC, "s": SMEM_SPEC, "a": HBM_SPEC}
    c = outs[0][0][-1]
    scratch = []
    if shift:
        scratch.append(pltpu.VMEM(shift, jnp.bfloat16))
    for _ in range(weights):
        taps = (3, c, 3 * c) if back else (3, 3 * c, c)
        scratch += [pltpu.VMEM(taps, jnp.bfloat16), pltpu.SemaphoreType.DMA((TAPS,))]
    scratch += [pltpu.VMEM(e, jnp.float32) for e in extra]
    return pl.pallas_call(
        kernel,
        out_shape=[jax.ShapeDtypeStruct(*o) for o in outs],
        in_specs=[specs[k] for _, k in ins],
        out_specs=[VMEM_SPEC] * len(outs),
        scratch_shapes=scratch,
        compiler_params=pltpu.CompilerParams(vmem_limit_bytes=limit * MIB),
        name=name,
    )(*[a for a, _ in ins])


def body(
    features,
    priors,
    domain,
    shared_w,
    shared_gain,
    shared_bias,
    first_w,
    second_w,
    task_conv,
    task_gain,
    task_bias,
    shared_cot,
    task_cot,
):
    place = Place()
    images, height, breadth, c = features.shape
    wide = breadth * REP
    f32, bf16 = jnp.float32, jnp.bfloat16
    member = (domain[:, None] == jnp.arange(DOMAINS, dtype=jnp.int32)[None, :]).astype(f32)
    named = jnp.sum(member, axis=0)
    number = named * (height * wide)
    counts = number * (place.rows * place.groups)
    scal = jnp.concatenate(
        [
            1.0 / number,
            1.0 / counts,
            (place.row > 0).astype(f32)[None],
            (place.row < place.rows - 1).astype(f32)[None],
        ]
    )

    rows0, rows1, rows2 = wide * images, wide * images + PAD, wide * images + 2 * PAD
    tile0, tile1, tile2 = (
        (height, rows0, c), (height + 2, rows1, c), (height + 4, rows2, c),
    )
    shift1 = ((height + 2) * rows0, 3 * c)
    shift2 = ((height + 4) * rows1, 3 * c)

    def selectors(rows, border):
        r = jnp.arange(rows)
        w, image = r // images - border, r % images
        of = member[image]
        own = ((w >= 0) & (w < wide)).astype(f32)
        col = place.group * wide + w
        seen = (col >= 0) & (col < wide * place.groups) & (w < wide + border)
        table = [of[:, 0], of[:, 0] * own, of[:, 1] * own, seen.astype(f32)]
        return jnp.stack(table + [jnp.zeros_like(own)] * 4, axis=1)

    sel0, sel1 = selectors(rows0, 0), selectors(rows1, 1)
    gains = jnp.stack([shared_gain, shared_bias], axis=1)
    task_gains = jnp.stack([task_gain, task_bias], axis=2)
    gb1 = gains[0][None]
    gb2 = jnp.stack([gains[1], task_gains[0, 0], task_gains[1, 0]])
    gb3 = jnp.stack([gains[2], task_gains[0, 1], task_gains[1, 1]])
    gbr = task_gains[:, 2]
    shared_taps = shared_w.reshape(CONVS * TAPS, c, c)
    task_taps = task_conv.reshape(TASKS * TAPS, c, c)

    features = features.transpose(1, 2, 0, 3).reshape(height, breadth * images, c)
    (features,) = place.halo([place.gather(features, 1)], 2, images)
    priors = priors.transpose(0, 2, 3, 1, 4).reshape(TASKS, height, breadth * images, c)
    priors = place.pieces(priors)
    half_h, half_w = height // 2, breadth // 2

    def spreader(rows, border):
        r = jnp.arange(rows)
        source = (r // images + border) // 2 * images + r % images
        size = (REP * half_w) * images + border * PAD
        return (0.25 * (source[:, None] == jnp.arange(size)[None])).astype(bf16)

    up0, up1 = spreader(rows0, 0), spreader(rows1, 1)

    p1, local = call(
        functools.partial(first_kernel, images, 0), "first",
        [(features, "v"), (shared_taps, "a"), (sel1, "v"), (scal, "s")],
        [(tile1, f32), ((2, 1, DOMAINS, c), f32)],
        shift=shift2, weights=1, limit=46,
    )
    p1, priors = lax.optimization_barrier((p1, priors))
    (priors,) = place.halo([place.join(priors, 2)], 1, images)
    stats1 = total_stats(place, local, number[None, :, None])

    act1, p2, local = call(
        functools.partial(second_kernel, images), "second",
        [
            (p1, "v"), (shared_taps, "a"), (stats1, "v"), (gb1, "v"), (sel1, "v"), (sel0, "v"),
            (scal, "s"),
        ],
        [(tile1, bf16), (tile0, f32), ((2, 1, DOMAINS, c), f32)],
        shift=shift1, weights=1, limit=44,
    )
    h0, h1, local_h = call(
        hidden_kernel, "hidden",
        [(act1, "v"), (priors, "v"), (first_w, "v"), (sel1, "v"), (scal, "s")],
        [(tile1, f32), (tile1, f32), ((2, TASKS, DOMAINS, c), f32)], limit=12,
    )
    local = jnp.concatenate([local, local_h], axis=1)
    stats2 = total_stats(place, local, number[None, :, None])
    stats2, task_cot, shared_cot = lax.optimization_barrier((stats2, task_cot, shared_cot))
    (act2,) = call(
        functools.partial(act_kernel, 0), "act",
        [(p2, "v"), (stats2, "v"), (gb2, "v"), (sel0, "v")],
        [(tile0, bf16)], limit=4,
    )
    (act2,) = place.halo([act2], 2, images)
    act2, task_cot, shared_cot = lax.optimization_barrier((act2, task_cot, shared_cot))
    cots = jnp.concatenate([task_cot, shared_cot[None]]).transpose(0, 2, 3, 1, 4)
    cots = place.pieces(cots.reshape(TASKS + 1, half_h, half_w * images, c))
    hidden0, hidden1, g0, g1, local_g = call(
        gate_kernel, "gate",
        [
            (h0, "v"), (h1, "v"), (second_w, "v"), (stats2, "v"), (gb2, "v"), (sel1, "v"),
            (scal, "s"),
        ],
        [
            (tile1, bf16), (tile1, bf16), (tile1, f32), (tile1, f32),
            ((2, TASKS, DOMAINS, c), f32),
        ],
        limit=10,
    )

    p3, local = call(
        functools.partial(first_kernel, images, 2 * TAPS), "third",
        [(act2, "v"), (shared_taps, "a"), (sel1, "v"), (scal, "s")],
        [(tile1, f32), ((2, 1, DOMAINS, c), f32)],
        shift=shift2, weights=1, limit=46,
    )
    stats3 = total_stats(
        place, jnp.concatenate([local, local_g], axis=1), number[None, :, None]
    )

    m0, m1, r0, r1, local = call(
        functools.partial(fourth_kernel, images), "fourth",
        [
            (p3, "v"), (g0, "v"), (g1, "v"), (task_taps, "a"), (stats3, "v"), (gb3, "v"),
            (sel1, "v"), (sel0, "v"), (scal, "s"),
        ],
        [
            (tile1, bf16), (tile1, bf16), (tile0, f32), (tile0, f32),
            ((2, TASKS, DOMAINS, c), f32),
        ],
        shift=shift1, weights=2, limit=44,
    )
    local, cots = lax.optimization_barrier((local, cots))
    cots = place.join(cots, 2)
    statsr = total_stats(place, local, number[None, :, None])

    local, dy_r = call(
        refined_sums_kernel, "refined_sums",
        [
            (r0, "v"), (r1, "v"), (cots[0], "v"), (cots[1], "v"), (up0, "v"), (statsr, "v"),
            (gbr, "v"), (sel0, "v"),
        ],
        [((TASKS, 2, DOMAINS, c), f32), ((TASKS, *tile0), f32)],
        extra=[(half_h, rows0, c)], limit=6,
    )
    sums_r = total_sums(place, local)
    dv_r = call(
        refined_back_kernel, "refined_back",
        [
            (r0, "v"), (r1, "v"), (dy_r, "v"), (statsr, "v"), (gbr, "v"), (sums_r, "v"),
            (sel0, "v"), (scal, "s"),
        ],
        [(tile0, bf16), (tile0, bf16)], limit=4,
    )
    (shared_low,) = place.halo([cots[TASKS]], 1, images)
    dv_halo = place.halo(dv_r, 2, images)
    part = parts(
        place, ((0, 2, True), (1, 3, True)), images, [m0, m1], dv_r
    )
    dv_halo, part, shared_low = lax.optimization_barrier((dv_halo, part, shared_low))
    part = place.scatter_core(part)
    (grad0,) = call(
        functools.partial(conv_back_kernel, images, 0), "masked_back0",
        [(dv_halo[0], "v"), (task_taps, "a")], [(tile1, f32)],
        shift=shift2, weights=1, back=True, limit=44,
    )
    grad0, part = lax.optimization_barrier((grad0, part))
    task_chunk = place.scatter_chips(part)
    dy3, dyg0, dyg1, local = call(
        functools.partial(masked_back_kernel, images), "masked_back1",
        [
            (dv_halo[1], "v"), (task_taps, "a"), (grad0, "v"), (p3, "v"), (g0, "v"), (g1, "v"),
            (shared_low, "v"), (up1, "v"), (stats3, "v"), (gb3, "v"), (sel1, "v"),
        ],
        [(tile1, f32), (tile1, f32), (tile1, f32), ((3, 2, DOMAINS, c), f32)],
        shift=shift2, weights=1, back=True, extra=[(half_h + 2, rows1, c)], limit=40,
    )
    local, task_chunk = lax.optimization_barrier((local, task_chunk))
    task_rows = gather_rows(place, task_chunk)

    sums3 = total_sums(place, local)
    dv3, dy2, local = call(
        functools.partial(third_back_kernel, images), "third_back",
        [
            (dy3, "v"), (p3, "v"), (p2, "v"), (shared_taps, "a"), (stats3, "v"), (gb3, "v"),
            (sums3, "v"), (stats2, "v"), (gb2, "v"), (sel1, "v"), (sel0, "v"), (scal, "s"),
        ],
        [(tile1, bf16), (tile0, f32), ((1, 2, DOMAINS, c), f32)],
        shift=shift1, weights=1, back=True, limit=40,
    )
    dvg0, dvg1, dyh0, dyh1, local_h = call(
        gate_back_kernel, "gate_back",
        [
            (dyg0, "v"), (dyg1, "v"), (g0, "v"), (g1, "v"), (h0, "v"), (h1, "v"),
            (second_w, "v"), (stats3, "v"), (gb3, "v"), (sums3, "v"), (stats2, "v"), (gb2, "v"),
            (sel1, "v"), (scal, "s"),
        ],
        [
            (tile1, bf16), (tile1, bf16), (tile1, f32), (tile1, f32),
            ((TASKS, 2, DOMAINS, c), f32),
        ],
        limit=10,
    )
    part3 = parts(
        place, ((0, 3, False), (1, 4, False), (2, 5, True)), images,
        [hidden0, hidden1, act2], [dvg0, dvg1, dv3],
    )
    part3 = place.scatter_core(part3)

    sums2 = total_sums(place, jnp.concatenate([local, local_h]))
    (dv2,) = call(
        functools.partial(back_kernel, 0, False), "second_dv",
        [
            (dy2, "v"), (p2, "v"), (stats2, "v"), (gb2, "v"), (sums2, "v"), (sel0, "v"),
            (scal, "s"),
        ],
        [(tile0, bf16)], limit=4,
    )
    (dv2_halo,) = place.halo([dv2], 2, images)
    dv2_halo, part3 = lax.optimization_barrier((dv2_halo, part3))
    chunk3 = place.scatter_chips(part3)
    dvh0, dvh1, grad_hidden = call(
        hidden_back_kernel, "hidden_back",
        [
            (dyh0, "v"), (dyh1, "v"), (h0, "v"), (h1, "v"), (first_w, "v"), (stats2, "v"),
            (gb2, "v"), (sums2, "v"), (sel1, "v"), (scal, "s"),
        ],
        [(tile1, bf16), (tile1, bf16), (tile1, f32)], limit=10,
    )
    dy1, local = call(
        functools.partial(second_back_kernel, images), "second_back",
        [
            (dv2_halo, "v"), (shared_taps, "a"), (grad_hidden, "v"), (p1, "v"), (stats1, "v"),
            (gb1, "v"), (sel1, "v"),
        ],
        [(tile1, f32), ((1, 2, DOMAINS, c), f32)],
        shift=shift2, weights=1, back=True, limit=40,
    )
    part2 = parts(
        place,
        ((0, 3, False), (1, 3, False), (0, 4, False), (2, 4, False), (0, 5, True)),
        images, [act1, priors[0], priors[1]], [dvh0, dvh1, dv2],
    )
    part2 = place.scatter_core(part2)
    local, part2, chunk3 = lax.optimization_barrier((local, part2, chunk3))

    sums1 = total_sums(place, local)
    (dv1,) = call(
        functools.partial(back_kernel, 0, True), "first_dv",
        [
            (dy1, "v"), (p1, "v"), (stats1, "v"), (gb1, "v"), (sums1, "v"), (sel1, "v"),
            (scal, "s"),
        ],
        [(tile1, bf16)], limit=4,
    )
    part1 = place.scatter_core(parts(place, ((0, 1, True),), images, [features], [dv1]))
    chunk1 = place.scatter_chips(jnp.concatenate([part1, part2[2 * TASKS :], part2[: 2 * TASKS]]))
    rest_rows = gather_rows(
        place,
        jnp.concatenate(
            [chunk1[: 2 * TAPS], chunk3[TASKS:], chunk1[2 * TAPS :], chunk3[:TASKS]]
        ),
    )
    chunk1, dv1, p3, r0, r1, dvh0, dvh1 = lax.optimization_barrier(
        (chunk1, dv1, p3, r0, r1, dvh0, dvh1)
    )

    def own(tile, border):
        width = (breadth + 2 * border) * images
        return lax.dynamic_slice_in_dim(tile, place.rep * breadth * images, width, tile.ndim - 2)

    def pooled(value, stat, gb):
        of = jnp.tile(member, (breadth, 1))
        average = jnp.where(of[:, :1] > 0.5, stat[0, :1], stat[0, 1:])
        inverse = lax.rsqrt(jnp.where(of[:, :1] > 0.5, stat[1, :1], stat[1, 1:]) + EPSILON)
        normed = (value - average) * inverse * gb[0] + gb[1]
        out = jax.nn.silu(normed).reshape(half_h, 2, half_w, 2, images, c)
        return jnp.mean(out, axis=(1, 3)).transpose(2, 0, 1, 3).astype(bf16)

    own3 = own(p3[1:-1, images : images + rows0], 0)
    shared_out = pooled(own3, stats3[:, 0], gb3[0])
    task_out = jnp.stack([pooled(own((r0, r1)[t], 0), statsr[:, t], gbr[t]) for t in range(TASKS)])

    near = own(dv1[:, : rows0 + 2 * images], 1).reshape(height + 2, breadth + 2, images, c)
    grad_features = lax.conv_general_dilated(
        near,
        jnp.flip(shared_w[0], (0, 1)),
        (1, 1),
        "VALID",
        dimension_numbers=("HWNC", "HWOI", "HWNC"),
        preferred_element_type=f32,
    ).transpose(2, 0, 1, 3)
    grad_priors = []
    for t, dv in enumerate((dvh0, dvh1)):
        mine = own(dv[1:-1, images : images + rows0], 0)
        value = jnp.einsum("hrd,cd->hrc", mine, first_w[t, c:], preferred_element_type=f32)
        grad_priors.append(value.reshape(height, breadth, images, c).transpose(2, 0, 1, 3))

    (grad_task,) = spread(place, task_rows, 0, [TASKS * TAPS], 9)
    (grad_shared,) = spread(place, rest_rows, 0, [CONVS * TAPS], 9)
    grad_first, grad_second = spread(place, rest_rows, CONVS * TAPS, [2 * TASKS, TASKS], 3)

    shared_sums = jnp.sum(jnp.stack([sums1[0], sums2[0], sums3[0]]), axis=2)
    task_sums = jnp.sum(jnp.stack([sums2[1:], sums3[1:], sums_r], axis=1), axis=3)
    return (
        shared_out,
        task_out,
        grad_features,
        jnp.stack(grad_priors),
        grad_shared.reshape(shared_w.shape),
        shared_sums[:, 1],
        shared_sums[:, 0],
        grad_first.reshape(first_w.shape),
        grad_second.reshape(second_w.shape),
        grad_task.reshape(task_conv.shape),
        task_sums[:, :, 1],
        task_sums[:, :, 0],
    )


def solution(mesh):
    return jax.shard_map(
        body,
        mesh=mesh,
        in_specs=(
            P(None, "row", "col", None),
            P(None, None, "row", "col", None),
            P(),
            P(),
            P(),
            P(),
            P(),
            P(),
            P(),
            P(),
            P(),
            P(None, "row", "col", None),
            P(None, None, "row", "col", None),
        ),
        out_specs=(
            P(None, "row", "col", None),
            P(None, None, "row", "col", None),
            P(None, "row", "col", None),
            P(None, None, "row", "col", None),
            P(),
            P(),
            P(),
            P(),
            P(),
            P(),
            P(),
            P(),
        ),
        check_vma=False,
    )
```

time: 637 us -> 572 us (0.90)
  matrix products: 151 us -> 4.97 us
  Pallas kernels: 35.2 us -> 173 us
  waiting for transfers between devices: 201 us -> 170 us
  other arithmetic: 59.9 us -> 37.5 us
  starting transfers between devices: 114 us -> 95.9 us
  local copies, waits for them, and re-layouts: 54.4 us -> 64.8 us
    pallas_call x4 -> x24, Pallas kernels: 35.2 us -> 173 us  [the longest x17 133 us: call(): pl.pallas_call(kernel, out_shape=[jax.ShapeDtypeStruct(*o) for o in outs]...]
    conv_general_dilated x14 -> x0, matrix products: 111 us -> none  [the longest x4 53.4 us: convolve_back(): lax.conv_general_dilated(padded_grad, jnp.flip(kernel, (0, 1)), (1, 1), '...]
    all_gather x2, waiting for transfers between devices: 110 us -> 66 us  [gather_rows(): whole = lax.all_gather(chunk, BOTH)]
    dot_general x99 -> x2, matrix products: 35.2 us -> 0.67 us  [body(): jnp.einsum('hrd,cd->hrc', mine, first_w[t, c:], preferred_element_type=f32)]
    convert_element_type x22 -> x8, other arithmetic: 24 us -> 1.02 us  [the longest x2 0.77 us: spreader(): return (0.25 * (source[:, None] == jnp.arange(size)[None])).astype(bf16)]
    ppermute x63 -> x69, starting transfers between devices: 95.4 us -> 81.4 us  [swap(): return lax.ppermute(value, BOTH, pairs)]
    ppermute x63 -> x69, waiting for transfers between devices: 89.6 us -> 103 us  [swap(): return lax.ppermute(value, BOTH, pairs)]
    unnamed x285 -> x277, local copies, waits for them, and re-layouts: 27.4 us -> 40.7 us
  transfers between devices with their start and end apart: 75 -> 83, of which waited for: 40 -> 35; matrix products, arithmetic and copies ran while one was open for 20% -> 10% of each run, Pallas kernels for 2% -> 23%
where the time goes in v3:
time: 572 us; the launch traced here: 563 us
  Pallas kernels  173 us (30%)
  waiting for transfers between devices  170 us (30%)
  starting transfers between devices  95.9 us (17%)
  local copies, waits for them, and re-layouts  64.8 us (11%)
  other arithmetic  37.5 us (7%)
  between operations  17.4 us (3%)
    pallas_call x17, Pallas kernels, call(): pl.pallas_call(kernel, out_shape=[jax.ShapeDtypeStruct(*o) for o in outs]...  133 us
    ppermute x69, waiting for transfers between devices, swap(): return lax.ppermute(value, BOTH, pairs)  103 us
    ppermute x69, starting transfers between devices, swap(): return lax.ppermute(value, BOTH, pairs)  81.4 us
    all_gather x2, waiting for transfers between devices, gather_rows(): whole = lax.all_gather(chunk, BOTH)  66 us
    unnamed x277, local copies, waits for them, and re-layouts  40.7 us
    pallas_call x3, Pallas kernels, spread(): pl.pallas_call(functools.partial(spread_kernel, groups, sources), out_sha...  32.5 us
  transfers between devices with their start and end apart: 83, of which 35 were waited for; matrix products, arithmetic and copies ran while one was open for 10% of the time, Pallas kernels for 23%

profile of v3, /device:TPU:0, one launch (start us, length us, event | category | flops | bytes accessed | tf_op | source)
XLA Modules:
  0.0 563.4 jit_solution(2800516351350232312)
XLA Ops:
  8.3 4.0 collective-permute-start
  28.4 12.7 %collective-permute-done.6 = bf16[128,512]{1,0:T(8,128)(2,1)S(1)} collective-permute-done((bf16[128,512]{1,0:T(8,128)(2,1)S(1)}, bf16[128,512]{1,0:T(8,128)(2,1)S(1)}, u32[]{:S(2)}, u32[]{:S(2)}) %collective-permute-start.6) | collective-permute-done | bytes 131104 | tf_op jit(solution)/shard_map/ppermute | solution.py:37
  42.8 10.2 %first.1 = (f32[10,112,512]{2,1,0:T(8,128)S(1)}, f32[2,1,2,512]{3,2,1,0:T(2,128)S(1)}) custom-call(bf16[12,128,512]{2,1,0:T(8,128)(2,1)S(1)} %maximum_maximum_fusion.1.x_ref.refs_0_, bf16[27,512,512]{2,1,0:T(8,128)(2,1)} %bitcast.359, f32[112,8]{1,0:T(8,128)S(1)} %stack.144.sel_ref, f32[6]{0:T(128)S(1)} %pad_maximum_fusion.35.scal_ref), custom_call_target="tpu_custom_call" | custom-call | tf_op jit(solution)/shard_map/first/pallas_call | solution.py:722
  55.3 3.4 collective-permute-start.17
  68.8 8.6 %second.1 = (bf16[10,112,512]{2,1,0:T(8,128)(2,1)S(1)}, f32[8,96,512]{2,1,0:T(8,128)S(1)}, f32[2,1,2,512]{3,2,1,0:T(2,128)S(1)}) custom-call(f32[10,112,512]{2,1,0:T(8,128)S(1)} %get-tuple-element.97.p1_ref.p_ref, bf16[27,512,512]{2,1,0:T(8,128)(2,1)} %bitcast.360, f32[2,1,2,512]{3,2,1,0:T(2,128)S(1)} %pad_maximum_fusion.34.st1_ref.st_ref, ...), custom_call_target="tpu_custom_call" | custom-call | tf_op jit(solution)/shard_map/second/pallas_call | solution.py:722
  79.0 3.4 collective-permute-done.16
  84.1 8.3 %hidden.1 = (f32[10,112,512]{2,1,0:T(8,128)S(1)}, f32[10,112,512]{2,1,0:T(8,128)S(1)}, f32[2,2,2,512]{3,2,1,0:T(2,128)S(1)}) custom-call(bf16[10,112,512]{2,1,0:T(8,128)(2,1)S(1)} %get-tuple-element.101.act_ref.refs_0_, bf16[2,10,112,512]{3,2,1,0:T(8,128)(2,1)S(1)} %maximum_maximum_fusion.pr_ref, bf16[2,1024,512]{2,1,0:T(8,128)(2,1)S(1)} %copy-done.22, ...), custom_call_target="tpu_custom_call" | custom-call | tf_op jit(solution)/shard_map/hidden/pallas_call | solution.py:722
  108.4 10.2 %gate.1 = (bf16[10,112,512]{2,1,0:T(8,128)(2,1)S(1)}, bf16[10,112,512]{2,1,0:T(8,128)(2,1)S(1)}, f32[10,112,512]{2,1,0:T(8,128)S(1)}, f32[10,112,512]{2,1,0:T(8,128)S(1)}, f32[2,2,2,512]{3,2,1,0:T(2,128)S(1)}) custom-call(f32[10,112,512]{2,1,0:T(8,128)S(1)} %get-tuple-element.112.h0_ref, f32[10,112,512]{2,1,0:T(8,128)S(1)} %get-tuple-element.113.h1_ref, ...), custom_call_target="tpu_custom_call" | custom-call | tf_op jit(solution)/shard_map/gate/pallas_call | solution.py:722
  124.2 4.9 collective-permute-done.24
  130.1 10.2 %third.1 = (f32[10,112,512]{2,1,0:T(8,128)S(1)}, f32[2,1,2,512]{3,2,1,0:T(2,128)S(1)}) custom-call(bf16[12,128,512]{2,1,0:T(8,128)(2,1)S(1)} %maximum_maximum_fusion.2.x_ref.refs_2_, bf16[27,512,512]{2,1,0:T(8,128)(2,1)} %bitcast.361, f32[112,8]{1,0:T(8,128)S(1)} %stack.144.sel_ref, f32[6]{0:T(128)S(1)} %copy-done.74), custom_call_target="tpu_custom_call" | custom-call | tf_op jit(solution)/shard_map/third/pallas_call | solution.py:722
  144.4 4.0 collective-permute-start.29
  157.6 17.2 %fourth.1 = (bf16[10,112,512]{2,1,0:T(8,128)(2,1)S(1)}, bf16[10,112,512]{2,1,0:T(8,128)(2,1)S(1)}, f32[8,96,512]{2,1,0:T(8,128)S(1)}, f32[8,96,512]{2,1,0:T(8,128)S(1)}, f32[2,2,2,512]{3,2,1,0:T(2,128)S(1)}) custom-call(f32[10,112,512]{2,1,0:T(8,128)S(1)} %get-tuple-element.170.p3_ref, f32[10,112,512]{2,1,0:T(8,128)S(1)} %copy-done.5, ...), custom_call_target="tpu_custom_call" | custom-call | tf_op jit(solution)/shard_map/fourth/pallas_call | solution.py:722
  185.1 4.1 refined_sums.1
  213.3 7.2 %collective-permute-done.43 = bf16[96,512]{1,0:T(8,128)(2,1)S(1)} collective-permute-done((bf16[96,512]{1,0:T(8,128)(2,1)S(1)}, bf16[96,512]{1,0:T(8,128)(2,1)S(1)}, u32[]{:S(2)}, u32[]{:S(2)}) %collective-permute-start.43) | collective-permute-done | bytes 98336 | tf_op jit(solution)/shard_map/ppermute | solution.py:37
  220.6 3.7 maximum_maximum_fusion.4
  226.9 7.4 %masked_back0.1.grad_ref = f32[10,112,512]{2,1,0:T(8,128)S(1)} custom-call(bf16[12,128,512]{2,1,0:T(8,128)(2,1)S(1)} %copy-done.27, bf16[18,512,512]{2,1,0:T(8,128)(2,1)} %bitcast.365), custom_call_target="tpu_custom_call" | custom-call | tf_op jit(solution)/shard_map/masked_back0/pallas_call | solution.py:722
  237.7 14.8 %masked_back1.1 = (f32[10,112,512]{2,1,0:T(8,128)S(1)}, f32[10,112,512]{2,1,0:T(8,128)S(1)}, f32[10,112,512]{2,1,0:T(8,128)S(1)}, f32[3,2,2,512]{3,2,1,0:T(2,128)S(1)}) custom-call(bf16[12,128,512]{2,1,0:T(8,128)(2,1)S(1)} %copy-done.28, bf16[18,512,512]{2,1,0:T(8,128)(2,1)} %bitcast.366, f32[10,112,512]{2,1,0:T(8,128)S(1)} %masked_back0.1.grad_ref, ...), custom_call_target="tpu_custom_call" | custom-call | tf_op jit(solution)/shard_map/masked_back1/pallas_call | solution.py:722
  259.5 7.9 %collective-permute-done.52 = bf16[12,16,512]{2,1,0:T(8,128)(2,1)S(1)} collective-permute-done((bf16[12,16,512]{2,1,0:T(8,128)(2,1)S(1)}, bf16[12,16,512]{2,1,0:T(8,128)(2,1)S(1)}, u32[]{:S(2)}, u32[]{:S(2)}) %collective-permute-start.52) | collective-permute-done | bytes 196640 | tf_op jit(solution)/shard_map/ppermute | solution.py:37
  271.7 3.3 collective-permute-start.57
  284.0 8.6 %third_back.1 = (bf16[10,112,512]{2,1,0:T(8,128)(2,1)S(1)}, f32[8,96,512]{2,1,0:T(8,128)S(1)}, f32[1,2,2,512]{3,2,1,0:T(2,128)S(1)}) custom-call(f32[10,112,512]{2,1,0:T(8,128)S(1)} %copy-done.39, f32[10,112,512]{2,1,0:T(8,128)S(1)} %get-tuple-element.170.p3_ref, f32[8,96,512]{2,1,0:T(8,128)S(1)} %copy-done.20, bf16[27,512,512]{2,1,0:T(8,128)(2,1)} %bitcast.362, ...), custom_call_target="tpu_custom_call" | custom-call | tf_op jit(solution)/shard_map/third_back/pallas_call | solution.py:722
  298.2 9.8 %gate_back.1 = (bf16[10,112,512]{2,1,0:T(8,128)(2,1)S(1)}, bf16[10,112,512]{2,1,0:T(8,128)(2,1)S(1)}, f32[10,112,512]{2,1,0:T(8,128)S(1)}, f32[10,112,512]{2,1,0:T(8,128)S(1)}, f32[2,2,2,512]{3,2,1,0:T(2,128)S(1)}) custom-call(f32[10,112,512]{2,1,0:T(8,128)S(1)} %copy-done.35, f32[10,112,512]{2,1,0:T(8,128)S(1)} %copy-done.37, ...), custom_call_target="tpu_custom_call" | custom-call | tf_op jit(solution)/shard_map/gate_back/pallas_call | solution.py:722
  333.1 5.4 hidden_back.1
  343.9 7.1 %collective-permute-done.65 = bf16[128,512]{1,0:T(8,128)(2,1)S(1)} collective-permute-done((bf16[128,512]{1,0:T(8,128)(2,1)S(1)}, bf16[128,512]{1,0:T(8,128)(2,1)S(1)}, u32[]{:S(2)}, u32[]{:S(2)}) %collective-permute-start.65) | collective-permute-done | bytes 131104 | tf_op jit(solution)/shard_map/ppermute | solution.py:37
  356.9 9.5 %second_back.1 = (f32[10,112,512]{2,1,0:T(8,128)S(1)}, f32[1,2,2,512]{3,2,1,0:T(2,128)S(1)}) custom-call(bf16[12,128,512]{2,1,0:T(8,128)(2,1)S(1)} %maximum_maximum_fusion.5.dv2_ref, bf16[27,512,512]{2,1,0:T(8,128)(2,1)} %bitcast.363, f32[10,112,512]{2,1,0:T(8,128)S(1)} %get-tuple-element.158.add_ref, f32[10,112,512]{2,1,0:T(8,128)S(1)} %copy-done.10, ...), custom_call_target="tpu_custom_call" | custom-call | tf_op jit(solution)/shard_map/second_back/pallas_call | solution.py:722
  371.3 4.5 collective-permute-done.70
  392.2 11.6 %collective-permute-done.78 = bf16[8,2,16,512]{3,2,0,1:T(8,128)(2,1)S(1)} collective-permute-done((bf16[8,2,16,512]{3,2,0,1:T(8,128)(2,1)S(1)}, bf16[8,2,16,512]{3,2,0,1:T(8,128)(2,1)S(1)}, u32[]{:S(2)}, u32[]{:S(2)}) %collective-permute-start.78) | collective-permute-done | bytes 262176 | tf_op jit(solution)/shard_map/ppermute | solution.py:37
  409.5 8.0 %collective-permute-done.79 = bf16[14,16,512]{2,1,0:T(8,128)(2,1)S(1)} collective-permute-done((bf16[14,16,512]{2,1,0:T(8,128)(2,1)S(1)}, bf16[14,16,512]{2,1,0:T(8,128)(2,1)S(1)}, u32[]{:S(2)}, u32[]{:S(2)}) %collective-permute-start.79) | collective-permute-done | bytes 229408 | tf_op jit(solution)/shard_map/ppermute | solution.py:37
  452.3 4.3 fusion
  457.6 11.4 %spread.5 = f32[18,512,512]{2,1,0:T(8,128)} custom-call(bf16[4,2,4,18,16,512]{5,4,3,2,1,0:T(8,128)(2,1)} %bitcast.367, bf16[4,2,4,18,16,512]{5,4,3,2,1,0:T(8,128)(2,1)} %bitcast.368), custom_call_target="tpu_custom_call" | custom-call | bytes 28311552 | tf_op jit(solution)/shard_map/spread/pallas_call | solution.py:688
  469.0 66.0 %all-gather.5.cloned.1.call-done = bf16[1056,16,512]{2,1,0:T(8,128)(2,1)} async-done(((bf16[33,16,512]{2,1,0:T(8,128)(2,1)}), bf16[1056,16,512]{2,1,0:T(8,128)(2,1)}) %all-gather.5.cloned.1.call-update) | async-done | bytes 17301520 | tf_op jit(solution)/shard_map/all_gather | solution.py:703
  535.1 15.9 %spread.3 = f32[27,512,512]{2,1,0:T(8,128)} custom-call(bf16[4,2,4,33,16,512]{5,4,3,2,1,0:T(8,128)(2,1)} %bitcast.353, bf16[4,2,4,33,16,512]{5,4,3,2,1,0:T(8,128)(2,1)} %bitcast.354), custom_call_target="tpu_custom_call" | custom-call | bytes 42467328 | tf_op jit(solution)/shard_map/spread/pallas_call | solution.py:688
  551.0 5.2 spread.4
  (683 shorter events, 233.2 us)
Async XLA Ops:
  7.2 450.4 %all-gather.7.cloned.1.call-start = ((), (), s32[]{:S(2)}) async-start(), calls=%async_computation.1 | async-start | bytes 9732096 | tf_op jit(solution)/shard_map/all_gather | solution.py:703
  8.3 15.0 %collective-permute-start = (bf16[8,24,512]{2,1,0:T(8,128)(2,1)S(1)}, bf16[8,24,512]{2,1,0:T(8,128)(2,1)S(1)}, u32[]{:S(2)}, u32[]{:S(2)}) collective-permute-start(bf16[8,24,512]{2,1,0:T(8,128)(2,1)S(1)} %copy.191), channel_id=1, source_target_pairs={{0,3},{1,2},{2,1},{3,0},{4,7},{5,6},{6,5},{7,4},{8,11},{9,10},{10,... | collective-permute-start | bytes 589832 | tf_op jit(solution)/shard_map/ppermute | solution.py:37
  14.2 38.9 %collective-permute-start.7 = (bf16[2,8,24,512]{3,2,0,1:T(8,128)(2,1)S(1)}, bf16[2,8,24,512]{3,2,0,1:T(8,128)(2,1)}, u32[]{:S(2)}, u32[]{:S(2)}) collective-permute-start(bf16[2,8,24,512]{3,2,0,1:T(8,128)(2,1)S(1)} %copy.197), channel_id=1, source_target_pairs={{0,1},{1,0},{2,3},{3,2},{4,5},{5,4},{6,7},{7,6},{8,9},{9,8},{10,11... | collective-permute-start | bytes 1179656 | tf_op jit(solution)/shard_map/ppermute | solution.py:37
  16.1 37.0 %collective-permute-start.8 = (bf16[2,8,24,512]{3,2,0,1:T(8,128)(2,1)S(1)}, bf16[2,8,24,512]{3,2,0,1:T(8,128)(2,1)}, u32[]{:S(2)}, u32[]{:S(2)}) collective-permute-start(bf16[2,8,24,512]{3,2,0,1:T(8,128)(2,1)S(1)} %copy.197), channel_id=1, source_target_pairs={{0,2},{1,3},{2,0},{3,1},{4,6},{5,7},{6,4},{7,5},{8,10},{9,11},{10,... | collective-permute-start | bytes 1179656 | tf_op jit(solution)/shard_map/ppermute | solution.py:37
  23.4 29.7 %collective-permute-start.9 = (bf16[2,8,24,512]{3,2,0,1:T(8,128)(2,1)S(1)}, bf16[2,8,24,512]{3,2,0,1:T(8,128)(2,1)S(1)}, u32[]{:S(2)}, u32[]{:S(2)}) collective-permute-start(bf16[2,8,24,512]{3,2,0,1:T(8,128)(2,1)S(1)} %copy.197), channel_id=1, source_target_pairs={{0,3},{1,2},{2,1},{3,0},{4,7},{5,6},{6,5},{7,4},{8,11},{9,10},{10,... | collective-permute-start | bytes 1179656 | tf_op jit(solution)/shard_map/ppermute | solution.py:37
  25.2 15.9 %collective-permute-start.6 = (bf16[128,512]{1,0:T(8,128)(2,1)S(1)}, bf16[128,512]{1,0:T(8,128)(2,1)S(1)}, u32[]{:S(2)}, u32[]{:S(2)}) collective-permute-start(bf16[128,512]{1,0:T(8,128)(2,1)S(1)} %bitcast.404), channel_id=1, source_target_pairs={{0,4},{1,5},{2,6},{3,7},{4,0},{5,1},{6,2},{7,3},{8,12},{9,13},{10,... | collective-permute-start | bytes 393224 | tf_op jit(solution)/shard_map/ppermute | solution.py:37
  28.3 13.5 %collective-permute-start.5 = (bf16[64,512]{1,0:T(8,128)(2,1)S(1)}, bf16[64,512]{1,0:T(8,128)(2,1)S(1)}, u32[]{:S(2)}, u32[]{:S(2)}) collective-permute-start(bf16[64,512]{1,0:T(8,128)(2,1)S(1)} %bitcast.412), channel_id=1, source_target_pairs={{0,4},{1,5},{2,6},{3,7},{4,0},{5,1},{6,2},{7,3},{8,12},{9,13},{10,... | collective-permute-start | bytes 196616 | tf_op jit(solution)/shard_map/ppermute | solution.py:37
  55.3 23.6 %collective-permute-start.17 = (bf16[128,512]{1,0:T(8,128)(2,1)S(1)}, bf16[128,512]{1,0:T(8,128)(2,1)S(1)}, u32[]{:S(2)}, u32[]{:S(2)}) collective-permute-start(bf16[128,512]{1,0:T(8,128)(2,1)S(1)} %bitcast.407), channel_id=1, source_target_pairs={{0,4},{1,5},{2,6},{3,7},{4,0},{5,1},{6,2},{7,3},{8,12},{9,13},{10,... | collective-permute-start | bytes 393224 | tf_op jit(solution)/shard_map/ppermute | solution.py:37
  64.5 12.9 %collective-permute-start.14 = (bf16[1,2,1,96,512]{4,3,1,2,0:T(8,128)(2,1)S(1)}, bf16[1,2,1,96,512]{4,3,1,2,0:T(8,128)(2,1)S(1)}, u32[]{:S(2)}, u32[]{:S(2)}) collective-permute-start(bf16[1,2,1,96,512]{4,3,1,2,0:T(8,128)(2,1)S(1)} %get-tuple-element.264), channel_id=1, source_target_pairs={{8,16},{16,8},{9,17},{17,9},{10,18},{18,10},{11,19},{19,11},{12,20... | collective-permute-start | bytes 589832 | tf_op jit(solution)/shard_map/ppermute | solution.py:80
  65.7 11.7 %collective-permute-start.15 = (bf16[1,2,1,96,512]{4,3,1,2,0:T(8,128)(2,1)S(1)}, bf16[1,2,1,96,512]{4,3,1,2,0:T(8,128)(2,1)S(1)}, u32[]{:S(2)}, u32[]{:S(2)}) collective-permute-start(bf16[1,2,1,96,512]{4,3,1,2,0:T(8,128)(2,1)S(1)} %get-tuple-element.265), channel_id=1, source_target_pairs={{0,8},{8,0},{16,24},{24,16},{1,9},{9,1},{17,25},{25,17},{2,10},{10... | collective-permute-start | bytes 589832 | tf_op jit(solution)/shard_map/ppermute | solution.py:74
  103.0 19.5 %collective-permute-start.22 = (bf16[1,2,96,512]{3,2,1,0:T(8,128)(2,1)S(1)}, bf16[1,2,96,512]{3,2,1,0:T(8,128)(2,1)S(1)}, u32[]{:S(2)}, u32[]{:S(2)}) collective-permute-start(bf16[1,2,96,512]{3,2,1,0:T(8,128)(2,1)S(1)} %get-tuple-element.284), channel_id=1, source_target_pairs={{8,16},{16,8},{9,17},{17,9},{10,18},{18,10},{11,19},{19,11},{12,20... | collective-permute-start | bytes 589832 | tf_op jit(solution)/shard_map/ppermute | solution.py:80
  103.9 18.6 %collective-permute-start.23 = (bf16[1,2,96,512]{3,2,1,0:T(8,128)(2,1)S(1)}, bf16[1,2,96,512]{3,2,1,0:T(8,128)(2,1)S(1)}, u32[]{:S(2)}, u32[]{:S(2)}) collective-permute-start(bf16[1,2,96,512]{3,2,1,0:T(8,128)(2,1)S(1)} %get-tuple-element.285), channel_id=1, source_target_pairs={{0,8},{8,0},{16,24},{24,16},{1,9},{9,1},{17,25},{25,17},{2,10},{10... | collective-permute-start | bytes 589832 | tf_op jit(solution)/shard_map/ppermute | solution.py:74
  106.9 17.3 %collective-permute-start.25 = (bf16[128,512]{1,0:T(8,128)(2,1)S(1)}, bf16[128,512]{1,0:T(8,128)(2,1)S(1)}, u32[]{:S(2)}, u32[]{:S(2)}) collective-permute-start(bf16[128,512]{1,0:T(8,128)(2,1)S(1)} %bitcast.403), channel_id=1, source_target_pairs={{0,4},{1,5},{2,6},{3,7},{4,0},{5,1},{6,2},{7,3},{8,12},{9,13},{10,... | collective-permute-start | bytes 393224 | tf_op jit(solution)/shard_map/ppermute | solution.py:37
  149.7 25.2 %collective-permute-start.30 = (bf16[3,4,12,512]{3,2,1,0:T(8,128)(2,1)S(1)}, bf16[3,4,12,512]{3,2,1,0:T(8,128)(2,1)S(1)}, u32[]{:S(2)}, u32[]{:S(2)}) collective-permute-start(bf16[3,4,12,512]{3,2,1,0:T(8,128)(2,1)S(1)} %copy.209), channel_id=1, source_target_pairs={{0,1},{1,0},{2,3},{3,2},{4,5},{5,4},{6,7},{7,6},{8,9},{9,8},{10,11... | collective-permute-start | bytes 442376 | tf_op jit(solution)/shard_map/ppermute | solution.py:37
  150.2 24.7 %collective-permute-start.31 = (bf16[3,4,12,512]{3,2,1,0:T(8,128)(2,1)S(1)}, bf16[3,4,12,512]{3,2,1,0:T(8,128)(2,1)S(1)}, u32[]{:S(2)}, u32[]{:S(2)}) collective-permute-start(bf16[3,4,12,512]{3,2,1,0:T(8,128)(2,1)S(1)} %copy.209), channel_id=1, source_target_pairs={{0,2},{1,3},{2,0},{3,1},{4,6},{5,7},{6,4},{7,5},{8,10},{9,11},{10,... | collective-permute-start | bytes 442376 | tf_op jit(solution)/shard_map/ppermute | solution.py:37
  150.7 24.2 %collective-permute-start.32 = (bf16[3,4,12,512]{3,2,1,0:T(8,128)(2,1)S(1)}, bf16[3,4,12,512]{3,2,1,0:T(8,128)(2,1)S(1)}, u32[]{:S(2)}, u32[]{:S(2)}) collective-permute-start(bf16[3,4,12,512]{3,2,1,0:T(8,128)(2,1)S(1)} %copy.209), channel_id=1, source_target_pairs={{0,3},{1,2},{2,1},{3,0},{4,7},{5,6},{6,5},{7,4},{8,11},{9,10},{10,... | collective-permute-start | bytes 442376 | tf_op jit(solution)/shard_map/ppermute | solution.py:37
  175.7 13.6 %collective-permute-start.48 = (bf16[32,512]{1,0:T(8,128)(2,1)S(1)}, bf16[32,512]{1,0:T(8,128)(2,1)S(1)}, u32[]{:S(2)}, u32[]{:S(2)}) collective-permute-start(bf16[32,512]{1,0:T(8,128)(2,1)S(1)} %fusion.84), channel_id=1, source_target_pairs={{0,4},{1,5},{2,6},{3,7},{4,0},{5,1},{6,2},{7,3},{8,12},{9,13},{10,... | collective-permute-start | bytes 98312 | tf_op jit(solution)/shard_map/ppermute | solution.py:37
  181.1 13.9 %collective-permute-start.46 = (bf16[1,1,48,512]{3,2,1,0:T(8,128)(2,1)S(1)}, bf16[1,1,48,512]{3,2,1,0:T(8,128)(2,1)S(1)}, u32[]{:S(2)}, u32[]{:S(2)}) collective-permute-start(bf16[1,1,48,512]{3,2,1,0:T(8,128)(2,1)S(1)} %broadcast_select_fusion.42), channel_id=1, source_target_pairs={{0,8},{8,0},{16,24},{24,16},{1,9},{9,1},{17,25},{25,17},{2,10},{10... | collective-permute-start | bytes 147464 | tf_op jit(solution)/shard_map/ppermute | solution.py:74
  181.2 13.8 %collective-permute-start.45 = (bf16[1,1,48,512]{3,2,1,0:T(8,128)(2,1)S(1)}, bf16[1,1,48,512]{3,2,1,0:T(8,128)(2,1)S(1)}, u32[]{:S(2)}, u32[]{:S(2)}) collective-permute-start(bf16[1,1,48,512]{3,2,1,0:T(8,128)(2,1)S(1)} %get-tuple-element.240), channel_id=1, source_target_pairs={{8,16},{16,8},{9,17},{17,9},{10,18},{18,10},{11,19},{19,11},{12,20... | collective-permute-start | bytes 147464 | tf_op jit(solution)/shard_map/ppermute | solution.py:80
  236.6 17.4 %collective-permute-start.51 = (bf16[6,2,16,512]{3,2,0,1:T(8,128)(2,1)S(1)}, bf16[6,2,16,512]{3,2,0,1:T(8,128)(2,1)S(1)}, u32[]{:S(2)}, u32[]{:S(2)}) collective-permute-start(bf16[6,2,16,512]{3,2,0,1:T(8,128)(2,1)S(1)} %fusion.31), channel_id=1, source_target_pairs={{0,4},{1,5},{2,6},{3,7},{4,0},{5,1},{6,2},{7,3},{8,12},{9,13},{10,... | collective-permute-start | bytes 589832 | tf_op jit(solution)/shard_map/ppermute | solution.py:37
  236.7 17.3 %collective-permute-start.50 = (bf16[12,2,16,512]{3,2,0,1:T(8,128)(2,1)S(1)}, bf16[12,2,16,512]{3,2,0,1:T(8,128)(2,1)S(1)}, u32[]{:S(2)}, u32[]{:S(2)}) collective-permute-start(bf16[12,2,16,512]{3,2,0,1:T(8,128)(2,1)S(1)} %fusion.23), channel_id=1, source_target_pairs={{0,16},{1,17},{2,18},{3,19},{4,20},{5,21},{6,22},{7,23},{8,24},{9,... | collective-permute-start | bytes 1179656 | tf_op jit(solution)/shard_map/ppermute | solution.py:37
  255.5 11.9 %collective-permute-start.52 = (bf16[12,16,512]{2,1,0:T(8,128)(2,1)S(1)}, bf16[12,16,512]{2,1,0:T(8,128)(2,1)S(1)}, u32[]{:S(2)}, u32[]{:S(2)}) collective-permute-start(bf16[12,16,512]{2,1,0:T(8,128)(2,1)S(1)} %fusion.32), channel_id=1, source_target_pairs={{0,4},{1,5},{2,6},{3,7},{4,0},{5,1},{6,2},{7,3},{8,12},{9,13},{10,... | collective-permute-start | bytes 589832 | tf_op jit(solution)/shard_map/ppermute | solution.py:37
  268.2 266.8 %all-gather.5.cloned.1.call-start = ((), (), s32[]{:S(2)}) async-start(), calls=%async_computation | async-start | bytes 17842176 | tf_op jit(solution)/shard_map/all_gather | solution.py:703
  321.8 32.9 %collective-permute-start.66 = (bf16[11,2,2,16,512]{4,3,0,1,2:T(8,128)(2,1)S(1)}, bf16[11,2,2,16,512]{4,3,0,1,2:T(8,128)(2,1)S(1)}, u32[]{:S(2)}, u32[]{:S(2)}) collective-permute-start(bf16[11,2,2,16,512]{4,3,0,1,2:T(8,128)(2,1)S(1)} %fusion.10), channel_id=1, source_target_pairs={{0,8},{1,9},{2,10},{3,11},{4,12},{5,13},{6,14},{7,15},{8,0},{9,1},... | collective-permute-start | bytes 2162696 | tf_op jit(solution)/shard_map/ppermute | solution.py:37
  329.8 11.2 %collective-permute-start.62 = (bf16[1,2,96,512]{3,2,1,0:T(8,128)(2,1)S(1)}, bf16[1,2,96,512]{3,2,1,0:T(8,128)(2,1)S(1)}, u32[]{:S(2)}, u32[]{:S(2)}) collective-permute-start(bf16[1,2,96,512]{3,2,1,0:T(8,128)(2,1)S(1)} %get-tuple-element.270), channel_id=1, source_target_pairs={{8,16},{16,8},{9,17},{17,9},{10,18},{18,10},{11,19},{19,11},{12,20... | collective-permute-start | bytes 589832 | tf_op jit(solution)/shard_map/ppermute | solution.py:80
  332.7 18.3 %collective-permute-start.65 = (bf16[128,512]{1,0:T(8,128)(2,1)S(1)}, bf16[128,512]{1,0:T(8,128)(2,1)S(1)}, u32[]{:S(2)}, u32[]{:S(2)}) collective-permute-start(bf16[128,512]{1,0:T(8,128)(2,1)S(1)} %bitcast.402), channel_id=1, source_target_pairs={{0,4},{1,5},{2,6},{3,7},{4,0},{5,1},{6,2},{7,3},{8,12},{9,13},{10,... | collective-permute-start | bytes 393224 | tf_op jit(solution)/shard_map/ppermute | solution.py:37
  341.0 25.4 %collective-permute-start.67 = (bf16[13,2,2,16,512]{4,3,0,1,2:T(8,128)(2,1)S(1)}, bf16[13,2,2,16,512]{4,3,0,1,2:T(8,128)(2,1)S(1)}, u32[]{:S(2)}, u32[]{:S(2)}) collective-permute-start(bf16[13,2,2,16,512]{4,3,0,1,2:T(8,128)(2,1)S(1)} %fusion.9), channel_id=1, source_target_pairs={{0,8},{1,9},{2,10},{3,11},{4,12},{5,13},{6,14},{7,15},{8,0},{9,1},... | collective-permute-start | bytes 2555912 | tf_op jit(solution)/shard_map/ppermute | solution.py:37
  341.2 12.6 %collective-permute-start.64 = (bf16[64,512]{1,0:T(8,128)(2,1)S(1)}, bf16[64,512]{1,0:T(8,128)(2,1)S(1)}, u32[]{:S(2)}, u32[]{:S(2)}) collective-permute-start(bf16[64,512]{1,0:T(8,128)(2,1)S(1)} %bitcast.411), channel_id=1, source_target_pairs={{0,4},{1,5},{2,6},{3,7},{4,0},{5,1},{6,2},{7,3},{8,12},{9,13},{10,... | collective-permute-start | bytes 196616 | tf_op jit(solution)/shard_map/ppermute | solution.py:37
  355.4 11.4 %collective-permute-start.68 = (bf16[7,2,16,512]{3,2,0,1:T(8,128)(2,1)S(1)}, bf16[7,2,16,512]{3,2,0,1:T(8,128)(2,1)S(1)}, u32[]{:S(2)}, u32[]{:S(2)}) collective-permute-start(bf16[7,2,16,512]{3,2,0,1:T(8,128)(2,1)S(1)} %fusion.28), channel_id=1, source_target_pairs={{0,16},{1,17},{2,18},{3,19},{4,20},{5,21},{6,22},{7,23},{8,24},{9,... | collective-permute-start | bytes 688136 | tf_op jit(solution)/shard_map/ppermute | solution.py:37
  388.2 15.5 %collective-permute-start.78 = (bf16[8,2,16,512]{3,2,0,1:T(8,128)(2,1)S(1)}, bf16[8,2,16,512]{3,2,0,1:T(8,128)(2,1)S(1)}, u32[]{:S(2)}, u32[]{:S(2)}) collective-permute-start(bf16[8,2,16,512]{3,2,0,1:T(8,128)(2,1)S(1)} %fusion.26), channel_id=1, source_target_pairs={{0,4},{1,5},{2,6},{3,7},{4,0},{5,1},{6,2},{7,3},{8,12},{9,13},{10,... | collective-permute-start | bytes 786440 | tf_op jit(solution)/shard_map/ppermute | solution.py:37
  391.5 12.7 %collective-permute-start.77 = (bf16[14,2,16,512]{3,2,0,1:T(8,128)(2,1)S(1)}, bf16[14,2,16,512]{3,2,0,1:T(8,128)(2,1)S(1)}, u32[]{:S(2)}, u32[]{:S(2)}) collective-permute-start(bf16[14,2,16,512]{3,2,0,1:T(8,128)(2,1)S(1)} %fusion.21), channel_id=1, source_target_pairs={{0,16},{1,17},{2,18},{3,19},{4,20},{5,21},{6,22},{7,23},{8,24},{9,... | collective-permute-start | bytes 1376264 | tf_op jit(solution)/shard_map/ppermute | solution.py:37
  405.2 12.3 %collective-permute-start.79 = (bf16[14,16,512]{2,1,0:T(8,128)(2,1)S(1)}, bf16[14,16,512]{2,1,0:T(8,128)(2,1)S(1)}, u32[]{:S(2)}, u32[]{:S(2)}) collective-permute-start(bf16[14,16,512]{2,1,0:T(8,128)(2,1)S(1)} %fusion.29), channel_id=1, source_target_pairs={{0,4},{1,5},{2,6},{3,7},{4,0},{5,1},{6,2},{7,3},{8,12},{9,13},{10,... | collective-permute-start | bytes 688136 | tf_op jit(solution)/shard_map/ppermute | solution.py:37
  (187 other events, 1707.9 us)
Sparse Core Ops, SparseCore 0:
  268.4 88.4 all-gather.6
  418.7 116.3 all-gather.4

commit v4 on v3

--- a/solution.py
+++ b/solution.py
@@ -14,7 +14,7 @@
 REP = 4
 TAPS = 9
 LANES = 128
-ROWS, WIDTH = 16, 256
+ROWS = 16
 PAD = 16
 
 EPSILON = 1e-05
@@ -142,7 +142,7 @@
         mine = lax.dynamic_index_in_dim(parts, core, 2, keepdims=False)
         return mine + other.astype(jnp.float32)
 
-    def scatter_chips(self, parts):
+    def scatter_chips(self, parts, beside=()):
         halves = self.rows // CORES
         cut = parts.shape[0] * 2 // 3
 
@@ -165,10 +165,22 @@
                 got.append(piece.astype(jnp.float32))
             return tree_sum(got)
 
-        first, last = along_row(parts[:cut]), along_col(parts[cut:], 2)
-        first, last = lax.optimization_barrier((first, last))
-        first, last = along_col(first, 1), along_row(last)
-        return jnp.concatenate([first, last]).astype(jnp.bfloat16)
+        parts = along_row(parts[:cut]), along_col(parts[cut:], 2)
+        parts, beside = lax.optimization_barrier((parts, beside))
+        parts = along_col(parts[0], 1), along_row(parts[1])
+        return jnp.concatenate(parts).astype(jnp.bfloat16), beside
+
+    def gather_swaps(self, chunk, beside):
+        half = chunk.shape[-1] // 2
+        line = jnp.stack([chunk, self.swap(chunk, 0, 2)])
+        line = jnp.stack([line, self.swap(line, 0, 4)])
+        first, last = line[..., :half], line[..., half:]
+        along_y, along_x = self.swap(first, 2, 0), self.swap(last, 0, 1)
+        first, last = jnp.stack([first, along_y]), jnp.stack([last, along_x])
+        along_x, along_y = self.swap(first, 0, 1), self.swap(last, 2, 0)
+        first, last = jnp.stack([first, along_x]), jnp.stack([last, along_y])
+        first, last, beside = lax.optimization_barrier((first, last, beside))
+        return beside, first, self.swap(first, 1, 0), last, self.swap(last, 1, 0)
 
 
 def tree_sum(values):
@@ -196,12 +208,38 @@
     return value
 
 
-def sweep(rows, c, step):
-    for lane in range(0, c, WIDTH):
+def row_blocks(i):
+    return pl.ds(pl.multiple_of(i * ROWS, ROWS), ROWS)
+
+
+def sweep(rows, c, setup):
+    for lane in range(0, c, LANES):
+        step = setup(slice(lane, lane + LANES))
 
         @pl.loop(0, rows // ROWS)
         def block(i):
-            step(pl.ds(pl.multiple_of(i * ROWS, ROWS), ROWS), slice(lane, lane + WIDTH))
+            step(row_blocks(i))
+
+
+def sweep_sums(sel_ref, rows, c, count, setup, store):
+    for lane in range(0, c, LANES):
+        lanes = slice(lane, lane + LANES)
+        step = setup(lanes)
+
+        def block(i, sums):
+            at = row_blocks(i)
+            added = []
+            for j, value in enumerate(step(at)):
+                for k in range(DOMAINS):
+                    part = value * sel_ref[1 + k, at]
+                    added.append(sums[j * DOMAINS + k] + tree_sum([part[r : r + 8] for r in range(0, ROWS, 8)]))
+            return tuple(added)
+
+        zero = jnp.zeros((8, LANES), jnp.float32)
+        sums = lax.fori_loop(0, rows // ROWS, block, (zero,) * (count * DOMAINS))
+        for j in range(count):
+            for k in range(DOMAINS):
+                store(j, k, lanes, jnp.sum(sums[j * DOMAINS + k], axis=0, keepdims=True))
 
 
 def own_lines(tile_ref):
@@ -210,50 +248,43 @@
     return border, h - border
 
 
-def wide(column):
-    return jnp.broadcast_to(column, (column.shape[0], WIDTH))
-
-
 class Norm:
-    def __init__(self, sel_ref, stat_ref, gb_ref, i, at):
-        rows, self.lanes = at
-        self.first = wide(sel_ref[rows, 0:1]) > 0.5
-        self.average = self.by_row(stat_ref[0, i, :, self.lanes])
-        self.inverse = self.by_row(lax.rsqrt(stat_ref[1, i, :, self.lanes] + EPSILON))
-        self.gain = gb_ref[i, 0:1, self.lanes]
-        self.half_gain, self.half_bias = 0.5 * self.gain, 0.5 * gb_ref[i, 1:2, self.lanes]
-
-    def by_row(self, pair):
-        return jnp.where(self.first, pair[0:1], pair[1:2])
-
-    def form(self, value):
-        return (value - self.average) * self.inverse
+    def __init__(self, stat_ref, gb_ref, i, lanes):
+        self.average = [stat_ref[0, i, k : k + 1, lanes] for k in range(DOMAINS)]
+        self.inverse = [
+            lax.rsqrt(stat_ref[1, i, k : k + 1, lanes] + EPSILON) for k in range(DOMAINS)
+        ]
+        self.gain = gb_ref[i, 0:1, lanes]
+        self.half_gain, self.half_bias = 0.5 * self.gain, 0.5 * gb_ref[i, 1:2, lanes]
+        self.lanes = lanes
 
     def half(self, form):
         return form * self.half_gain + self.half_bias
 
-    def fold(self):
-        self.times = self.inverse * self.half_gain
-        self.plus = self.half_bias - self.average * self.times
-        return self
-
-    def __call__(self, value):
-        return value * self.times + self.plus
-
-    def set_sums(self, sums_ref, scal_ref, i):
+    def forms(self, first):
+        average, inverse = jnp.where(first, *self.average), jnp.where(first, *self.inverse)
+        return lambda value: (value - average) * inverse
+
+    def halves(self, first):
+        times = [inverse * self.half_gain for inverse in self.inverse]
+        plus = [self.half_bias - a * t for a, t in zip(self.average, times)]
+        times, plus = jnp.where(first, *times), jnp.where(first, *plus)
+        return lambda value: value * times + plus
+
+    def backs(self, first, sums_ref, scal_ref, i):
+        scale = [inverse * self.gain for inverse in self.inverse]
         plain, cross = (
-            self.by_row(
-                jnp.concatenate(
-                    [sums_ref[i, j, k : k + 1, self.lanes] * scal_ref[2 + k] for k in range(DOMAINS)]
-                )
-            )
+            [sums_ref[i, j, k : k + 1, self.lanes] * scal_ref[2 + k] for k in range(DOMAINS)]
             for j in range(2)
         )
-        self.scale = self.inverse * self.gain
-        self.plain, self.cross = plain, cross
-
-    def back(self, dy, value):
-        return self.scale * (dy - self.plain - self.form(value) * self.cross)
+        slant = [s * x * inverse for s, x, inverse in zip(scale, cross, self.inverse)]
+        plus = [a * e - s * p for a, e, s, p in zip(self.average, slant, scale, plain)]
+        scale, slant, plus = (jnp.where(first, *pair) for pair in (scale, slant, plus))
+        return lambda dy, value: scale * dy + (plus - slant * value)
+
+
+def is_first(sel_ref, rows):
+    return sel_ref[0, rows] > 0.5
 
 
 def sigmoid(t):
@@ -273,38 +304,36 @@
 
 
 def seen(sel_ref, scal_ref, rows, lines):
-    column = wide(sel_ref[rows, 3:4])
+    column = sel_ref[3, rows]
     return [column * scal_ref[4]] + [column] * (lines - 2) + [column * scal_ref[5]]
-
-
-def add_by_domain(sel_ref, rows, values, out, lanes):
-    for k in range(DOMAINS):
-        out[k : k + 1, lanes] += jnp.sum(
-            values * wide(sel_ref[rows, 1 + k : 2 + k]), axis=0, keepdims=True
-        )
 
 
 def local_stats(tile_ref, sel_ref, scal_ref, out_ref, i):
     _, r, c = tile_ref.shape
     lines = range(*own_lines(tile_ref))
-    out_ref[:, i] = jnp.zeros((2, DOMAINS, c), jnp.float32)
-
-    def total(rows, lanes):
-        value = tree_sum([tile_ref[h, rows, lanes] for h in lines])
-        add_by_domain(sel_ref, rows, value, out_ref.at[0, i], lanes)
-
-    sweep(r, c, total)
-    for k in range(DOMAINS):
-        out_ref[0, i, k : k + 1] = out_ref[0, i, k : k + 1] * scal_ref[k]
-
-    def square(rows, lanes):
-        average = jnp.where(
-            wide(sel_ref[rows, 0:1]) > 0.5, out_ref[0, i, 0:1, lanes], out_ref[0, i, 1:2, lanes]
-        )
-        apart = [tile_ref[h, rows, lanes] - average for h in lines]
-        add_by_domain(sel_ref, rows, tree_sum([a * a for a in apart]), out_ref.at[1, i], lanes)
-
-    sweep(r, c, square)
+
+    def total(lanes):
+        return lambda rows: [tree_sum([tile_ref[h, rows, lanes] for h in lines])]
+
+    def keep_average(_, k, lanes, value):
+        out_ref[0, i, k : k + 1, lanes] = value * scal_ref[k]
+
+    sweep_sums(sel_ref, r, c, 1, total, keep_average)
+
+    def square(lanes):
+        averages = [out_ref[0, i, k : k + 1, lanes] for k in range(DOMAINS)]
+
+        def step(rows):
+            average = jnp.where(is_first(sel_ref, rows), *averages)
+            apart = [tile_ref[h, rows, lanes] - average for h in lines]
+            return [tree_sum([a * a for a in apart])]
+
+        return step
+
+    def keep_square(_, k, lanes, value):
+        out_ref[1, i, k : k + 1, lanes] = value
+
+    sweep_sums(sel_ref, r, c, 1, square, keep_square)
 
 
 def fetch(w_ref, wv_ref, sem, start, back=False):
@@ -365,12 +394,17 @@
     copies = fetch(w_ref, wv_ref, sem, TAPS)
     lines, r, c = p1_ref.shape
 
-    def activate(rows, lanes):
-        norm = Norm(sel_ref, st1_ref, gb_ref, 0, (rows, lanes)).fold()
-        for h, inside in enumerate(seen(sel_ref, scal_ref, rows, lines)):
-            act_ref[h, rows, lanes] = (silu(norm(p1_ref[h, rows, lanes])) * inside).astype(
-                jnp.bfloat16
-            )
+    def activate(lanes):
+        norm = Norm(st1_ref, gb_ref, 0, lanes)
+
+        def step(rows):
+            half = norm.halves(is_first(sel_ref, rows))
+            for h, inside in enumerate(seen(sel_ref, scal_ref, rows, lines)):
+                act_ref[h, rows, lanes] = (silu(half(p1_ref[h, rows, lanes])) * inside).astype(
+                    jnp.bfloat16
+                )
+
+        return step
 
     sweep(r, c, activate)
     convolve(act_ref, xs_ref, wv_ref, copies, p2_ref, images)
@@ -390,10 +424,15 @@
 def act_kernel(which, p_ref, st_ref, gb_ref, sel_ref, act_ref):
     lines, r, c = p_ref.shape
 
-    def activate(rows, lanes):
-        norm = Norm(sel_ref, st_ref, gb_ref, which, (rows, lanes)).fold()
-        for h in range(lines):
-            act_ref[h, rows, lanes] = silu(norm(p_ref[h, rows, lanes])).astype(jnp.bfloat16)
+    def activate(lanes):
+        norm = Norm(st_ref, gb_ref, which, lanes)
+
+        def step(rows):
+            half = norm.halves(is_first(sel_ref, rows))
+            for h in range(lines):
+                act_ref[h, rows, lanes] = silu(half(p_ref[h, rows, lanes])).astype(jnp.bfloat16)
+
+        return step
 
     sweep(r, c, activate)
 
@@ -414,16 +453,19 @@
     copies = [fetch(w_ref, wv_ref, sem, 0), fetch(w_ref, wv2_ref, sem2, TAPS)]
     lines, r, c = p3_ref.shape
 
-    def mask(rows, lanes):
-        norm = Norm(sel_ref, st3_ref, gb_ref, 0, (rows, lanes)).fold()
-        gates = [
-            Norm(sel_ref, st3_ref, gb_ref, 1 + t, (rows, lanes)).fold() for t in range(TASKS)
-        ]
-        for h, inside in enumerate(seen(sel_ref, scal_ref, rows, lines)):
-            last = silu(norm(p3_ref[h, rows, lanes])) * inside
-            for gate, g_ref, m_ref in zip(gates, (g0_ref, g1_ref), (m0_ref, m1_ref)):
-                attention = sigmoid(gate(g_ref[h, rows, lanes]))
-                m_ref[h, rows, lanes] = (attention * last).astype(jnp.bfloat16)
+    def mask(lanes):
+        norms = [Norm(st3_ref, gb_ref, i, lanes) for i in range(1 + TASKS)]
+
+        def step(rows):
+            first = is_first(sel_ref, rows)
+            half, *gates = [norm.halves(first) for norm in norms]
+            for h, inside in enumerate(seen(sel_ref, scal_ref, rows, lines)):
+                last = silu(half(p3_ref[h, rows, lanes])) * inside
+                for gate, g_ref, m_ref in zip(gates, (g0_ref, g1_ref), (m0_ref, m1_ref)):
+                    attention = sigmoid(gate(g_ref[h, rows, lanes]))
+                    m_ref[h, rows, lanes] = (attention * last).astype(jnp.bfloat16)
+
+        return step
 
     sweep(r, c, mask)
     convolve(m0_ref, xs_ref, wv_ref, copies[0], r0_ref, images)
@@ -432,10 +474,15 @@
     local_stats(r1_ref, sel0_ref, scal_ref, st_ref, 1)
 
 
-def store_sums(sel_ref, rows, lanes, out_ref, i, dys, forms):
-    add_by_domain(sel_ref, rows, tree_sum(list(dys)), out_ref.at[i, 0], lanes)
-    cross = tree_sum([dy * form for dy, form in zip(dys, forms)])
-    add_by_domain(sel_ref, rows, cross, out_ref.at[i, 1], lanes)
+def dy_sums(dys, forms):
+    return [tree_sum(list(dys)), tree_sum([dy * form for dy, form in zip(dys, forms)])]
+
+
+def keep_sums(out_ref, at):
+    def store(j, k, lanes, value):
+        out_ref[at + j // 2, j % 2, k : k + 1, lanes] = value
+
+    return store
 
 
 def upsample(up_ref, low_ref, out_ref):
@@ -447,20 +494,24 @@
     r0_ref, r1_ref, c0_ref, c1_ref, up_ref, st_ref, gb_ref, sel_ref, out_ref, dy_ref, low_ref
 ):
     lines, r, c = r0_ref.shape
-    out_ref[...] = jnp.zeros_like(out_ref)
     for t, (r_ref, c_ref) in enumerate(((r0_ref, c0_ref), (r1_ref, c1_ref))):
         upsample(up_ref, c_ref, low_ref)
 
-        def sums(rows, lanes):
-            norm = Norm(sel_ref, st_ref, gb_ref, t, (rows, lanes))
-            dys, forms = [], []
-            for h in range(lines):
-                forms.append(norm.form(r_ref[h, rows, lanes]))
-                dys.append(low_ref[h // 2, rows, lanes] * slope(norm.half(forms[-1])))
-                dy_ref[t, h, rows, lanes] = dys[-1]
-            store_sums(sel_ref, rows, lanes, out_ref, t, dys, forms)
-
-        sweep(r, c, sums)
+        def sums(lanes):
+            norm = Norm(st_ref, gb_ref, t, lanes)
+
+            def step(rows):
+                form_of = norm.forms(is_first(sel_ref, rows))
+                dys, forms = [], []
+                for h in range(lines):
+                    forms.append(form_of(r_ref[h, rows, lanes]))
+                    dys.append(low_ref[h // 2, rows, lanes] * slope(norm.half(forms[-1])))
+                    dy_ref[t, h, rows, lanes] = dys[-1]
+                return dy_sums(dys, forms)
+
+            return step
+
+        sweep_sums(sel_ref, r, c, 2, sums, keep_sums(out_ref, t))
 
 
 def refined_back_kernel(
@@ -486,74 +537,86 @@
     lines, r, c = p3_ref.shape
     own = slice(*own_lines(p3_ref))
     upsample(up_ref, cot_ref, low_ref)
-    sums_ref[...] = jnp.zeros_like(sums_ref)
-
-    def step(rows, lanes):
-        norm = Norm(sel_ref, st3_ref, gb_ref, 0, (rows, lanes))
-        gates = [Norm(sel_ref, st3_ref, gb_ref, 1 + t, (rows, lanes)) for t in range(TASKS)]
-        dys, forms = [[], [], []], [[], [], []]
-        for h in range(lines):
-            form = norm.form(p3_ref[h, rows, lanes])
-            half = norm.half(form)
-            tanh = jnp.tanh(half)
-            last = half + half * tanh
-            grad_last = low_ref[(h + 1) // 2, rows, lanes]
-            for i, (gate, g_ref, from_ref, d_ref) in enumerate(
-                zip(gates, (g0_ref, g1_ref), (grad_ref, dy1_ref), (dy0_ref, dy1_ref))
-            ):
-                gate_form = gate.form(g_ref[h, rows, lanes])
-                attention = sigmoid(gate.half(gate_form))
-                grad = from_ref[h, rows, lanes] * attention
-                grad_last = grad_last + grad
-                dy = grad * last * (1.0 - attention)
-                d_ref[h, rows, lanes] = dy
-                dys[1 + i].append(dy)
-                forms[1 + i].append(gate_form)
-            dy = grad_last * silu_slope(half, tanh)
-            dy3_ref[h, rows, lanes] = dy
-            dys[0].append(dy)
-            forms[0].append(form)
-        for i in range(3):
-            store_sums(sel_ref, rows, lanes, sums_ref, i, dys[i][own], forms[i][own])
-
-    sweep(r, c, step)
+
+    def setup(lanes):
+        norms = [Norm(st3_ref, gb_ref, i, lanes) for i in range(1 + TASKS)]
+
+        def step(rows):
+            first = is_first(sel_ref, rows)
+            form_of = [norm.forms(first) for norm in norms]
+            dys, forms = [[], [], []], [[], [], []]
+            for h in range(lines):
+                form = form_of[0](p3_ref[h, rows, lanes])
+                half = norms[0].half(form)
+                tanh = jnp.tanh(half)
+                last = half + half * tanh
+                grad_last = low_ref[(h + 1) // 2, rows, lanes]
+                for i, (g_ref, from_ref, d_ref) in enumerate(
+                    ((g0_ref, grad_ref, dy0_ref), (g1_ref, dy1_ref, dy1_ref)), 1
+                ):
+                    gate_form = form_of[i](g_ref[h, rows, lanes])
+                    attention = sigmoid(norms[i].half(gate_form))
+                    grad = from_ref[h, rows, lanes] * attention
+                    grad_last = grad_last + grad
+                    dy = grad * last * (1.0 - attention)
+                    d_ref[h, rows, lanes] = dy
+                    dys[i].append(dy)
+                    forms[i].append(gate_form)
+                dy = grad_last * silu_slope(half, tanh)
+                dy3_ref[h, rows, lanes] = dy
+                dys[0].append(dy)
+                forms[0].append(form)
+            return [x for d, f in zip(dys, forms) for x in dy_sums(d[own], f[own])]
+
+        return step
+
+    sweep_sums(sel_ref, r, c, 6, setup, keep_sums(sums_ref, 0))
 
 
 def slope_sums(which, out_at, grad_ref, add_ref, p_ref, st_ref, gb_ref, sel_ref, sums_ref):
     lines, r, c = p_ref.shape
     own = slice(*own_lines(p_ref))
 
-    def step(rows, lanes):
-        norm = Norm(sel_ref, st_ref, gb_ref, which, (rows, lanes))
-        dys, forms = [], []
-        for h in range(lines):
-            form = norm.form(p_ref[h, rows, lanes])
-            grad = grad_ref[h, rows, lanes]
-            if add_ref is not None:
-                grad = grad + add_ref[h, rows, lanes]
-            dy = grad * slope(norm.half(form))
-            grad_ref[h, rows, lanes] = dy
-            dys.append(dy)
-            forms.append(form)
-        store_sums(sel_ref, rows, lanes, sums_ref, out_at, dys[own], forms[own])
-
-    sweep(r, c, step)
+    def setup(lanes):
+        norm = Norm(st_ref, gb_ref, which, lanes)
+
+        def step(rows):
+            form_of = norm.forms(is_first(sel_ref, rows))
+            dys, forms = [], []
+            for h in range(lines):
+                form = form_of(p_ref[h, rows, lanes])
+                grad = grad_ref[h, rows, lanes]
+                if add_ref is not None:
+                    grad = grad + add_ref[h, rows, lanes]
+                dy = grad * slope(norm.half(form))
+                grad_ref[h, rows, lanes] = dy
+                dys.append(dy)
+                forms.append(form)
+            return dy_sums(dys[own], forms[own])
+
+        return step
+
+    sweep_sums(sel_ref, r, c, 2, setup, keep_sums(sums_ref, out_at))
 
 
 def back_kernel(which, masked, dy_ref, p_ref, st_ref, gb_ref, sums_ref, sel_ref, scal_ref, dv_ref):
     lines, r, c = p_ref.shape
 
-    def step(rows, lanes):
-        norm = Norm(sel_ref, st_ref, gb_ref, which, (rows, lanes))
-        norm.set_sums(sums_ref, scal_ref, which)
-        inside = seen(sel_ref, scal_ref, rows, lines)
-        for h in range(lines):
-            dv = norm.back(dy_ref[h, rows, lanes], p_ref[h, rows, lanes])
-            if masked:
-                dv = dv * inside[h]
-            dv_ref[h, rows, lanes] = dv.astype(jnp.bfloat16)
-
-    sweep(r, c, step)
+    def setup(lanes):
+        norm = Norm(st_ref, gb_ref, which, lanes)
+
+        def step(rows):
+            back = norm.backs(is_first(sel_ref, rows), sums_ref, scal_ref, which)
+            inside = seen(sel_ref, scal_ref, rows, lines)
+            for h in range(lines):
+                dv = back(dy_ref[h, rows, lanes], p_ref[h, rows, lanes])
+                if masked:
+                    dv = dv * inside[h]
+                dv_ref[h, rows, lanes] = dv.astype(jnp.bfloat16)
+
+        return step
+
+    sweep(r, c, setup)
 
 
 def third_back_kernel(
@@ -563,7 +626,6 @@
     copies = fetch(w_ref, wv_ref, sem, 2 * TAPS, True)
     back_kernel(0, True, dy3_ref, p3_ref, st3_ref, gb3_ref, sums_ref, sel_ref, scal_ref, dv3_ref)
     convolve(dv3_ref, xs_ref, wv_ref, copies, dy2_ref, images, True)
-    out_ref[...] = jnp.zeros_like(out_ref)
     slope_sums(0, 0, dy2_ref, None, p2_ref, st2_ref, gb2_ref, sel0_ref, out_ref)
 
 
@@ -571,7 +633,6 @@
     dy0_ref, dy1_ref, g0_ref, g1_ref, h0_ref, h1_ref, sw_ref, st3_ref, gb3_ref, sums_ref,
     st2_ref, gb2_ref, sel_ref, scal_ref, dv0_ref, dv1_ref, dh0_ref, dh1_ref, out_ref,
 ):
-    out_ref[...] = jnp.zeros_like(out_ref)
     for t, (dy_ref, g_ref, dv_ref, h_ref, dh_ref) in enumerate(
         (
             (dy0_ref, g0_ref, dv0_ref, h0_ref, dh0_ref),
@@ -604,7 +665,6 @@
 ):
     copies = fetch(w_ref, wv_ref, sem, TAPS, True)
     convolve(dv2_ref, xs_ref, wv_ref, copies, dy_ref, images, True)
-    sums_ref[...] = jnp.zeros_like(sums_ref)
     slope_sums(0, 0, dy_ref, add_ref, p1_ref, st_ref, gb_ref, sel_ref, sums_ref)
 
 
@@ -640,8 +700,6 @@
     def act_spec(x):
         return pl.BlockSpec((*x.shape[:2], LANES), lambda i, b: (0, 0, b[0]))
 
-    def grad_spec(x):
-        return pl.BlockSpec(x.shape, lambda i, b: (0, 0, 0))
 
     return pl.pallas_call(
         functools.partial(parts_kernel, plan, images),
@@ -649,17 +707,17 @@
         grid_spec=pltpu.PrefetchScalarGridSpec(
             num_scalar_prefetch=1,
             grid=(1,),
-            in_specs=[act_spec(x) for x in acts] + [grad_spec(x) for x in grads],
-            out_specs=pl.BlockSpec((count, LANES, c), lambda i, b: (0, 0, 0)),
+            in_specs=[act_spec(x) for x in acts] + [VMEM_SPEC] * len(grads),
+            out_specs=VMEM_SPEC,
             scratch_shapes=[pltpu.VMEM((8 * 16 * images, TAPS * LANES), jnp.bfloat16)],
         ),
-        compiler_params=pltpu.CompilerParams(vmem_limit_bytes=32 * MIB),
+        compiler_params=pltpu.CompilerParams(vmem_limit_bytes=12 * MIB),
         name="parts",
     )(place.rep.astype(jnp.int32)[None], *acts, *grads)
 
 
-def spread_kernel(groups, sources_per, *refs):
-    sources, targets = refs[: groups * sources_per], refs[groups * sources_per :]
+def spread_kernel(groups, sources_per, skip, *refs):
+    sources, targets = refs[: groups * sources_per], refs[groups * sources_per + skip :]
     at = 0
     places = [(target, i) for target in targets for i in range(target.shape[0])]
     for s in range(sources_per):
@@ -673,7 +731,7 @@
                     target[m, at : at + per, :] = source[r, 0, 0, i].astype(jnp.float32)
 
 
-def spread(place, gathered, start, counts, step):
+def spread(place, gathered, start, counts, step, into=None):
     rows, groups, _, _, per, c = gathered.shape
     block = rows * groups * per
     sources = 1 if len(counts) == 1 else sum(counts) // step
@@ -685,18 +743,65 @@
         )
 
     takes = [step] if len(counts) == 1 else counts
+    old = [] if into is None else [into]
+    at = into.shape[0] - counts[0] if old else 0
     return pl.pallas_call(
-        functools.partial(spread_kernel, groups, sources),
-        out_shape=[jax.ShapeDtypeStruct((n, REP * block, c), jnp.float32) for n in counts],
+        functools.partial(spread_kernel, groups, sources, len(old)),
+        out_shape=[jax.ShapeDtypeStruct((n + at, REP * block, c), jnp.float32) for n in counts],
         grid=(sum(counts) // (step * sources), REP),
-        in_specs=[source(s, g) for s in range(sources) for g in range(groups)],
-        out_specs=[pl.BlockSpec((n, block, c), lambda i, b: (i, b, 0)) for n in takes],
+        in_specs=[source(s, g) for s in range(sources) for g in range(groups)]
+        + [pl.BlockSpec(memory_space=pl.ANY)] * len(old),
+        out_specs=[pl.BlockSpec((n, block, c), lambda i, b: (at // step + i, b, 0)) for n in takes],
+        input_output_aliases={groups * sources: 0} if old else {},
         compiler_params=pltpu.CompilerParams(vmem_limit_bytes=58 * MIB),
         cost_estimate=pl.CostEstimate(
             flops=0, bytes_accessed=6 * sum(counts) * REP * block * c, transcendentals=0
         ),
         name="spread",
-    )(*([gathered] * (groups * sources)))
+    )(*([gathered] * (groups * sources)), *old)
+
+
+def place_kernel(place_ref, *refs):
+    *sources, target = refs
+    per, half = sources[0].shape[-2:]
+    row, col = place_ref[0], place_ref[1]
+    for r in range(4):
+        for q in range(8):
+            apart_r, apart_q = r ^ row, q ^ col
+            y, x, high, low = apart_r // 2, apart_q % 2, apart_q // 4, apart_q // 2 % 2
+            same = apart_r % 2 == 0
+            at = ((q % REP) * 8 + r * 2 + q // REP) * per
+            first = jnp.where(same, sources[0][x, y, high, low], sources[1][x, y, high, low])
+            last = jnp.where(same, sources[2][y, x, high, low], sources[3][y, x, high, low])
+            target[:, at : at + per, :half] = first.astype(jnp.float32)
+            target[:, at : at + per, half:] = last.astype(jnp.float32)
+
+
+def place_swapped(place, swapped, total, step):
+    m, per, half = swapped[0].shape[-3:]
+    rows = place.rows * place.cols * per
+    here = jnp.stack([place.row, place.col]).astype(jnp.int32)
+
+    def source(part):
+        return pl.BlockSpec(
+            (*part.shape[:4], step, per, half), lambda i, here: (0, 0, 0, 0, i, 0, 0)
+        )
+
+    return pl.pallas_call(
+        place_kernel,
+        out_shape=jax.ShapeDtypeStruct((total, rows, 2 * half), jnp.float32),
+        grid_spec=pltpu.PrefetchScalarGridSpec(
+            num_scalar_prefetch=1,
+            grid=(m // step,),
+            in_specs=[source(p) for p in swapped],
+            out_specs=pl.BlockSpec((step, rows, 2 * half), lambda i, here: (i, 0, 0)),
+        ),
+        compiler_params=pltpu.CompilerParams(vmem_limit_bytes=32 * MIB),
+        cost_estimate=pl.CostEstimate(
+            flops=0, bytes_accessed=12 * m * rows * half, transcendentals=0
+        ),
+        name="place",
+    )(here, *swapped)
 
 
 def gather_rows(place, chunk):
@@ -776,8 +881,8 @@
         own = ((w >= 0) & (w < wide)).astype(f32)
         col = place.group * wide + w
         seen = (col >= 0) & (col < wide * place.groups) & (w < wide + border)
-        table = [of[:, 0], of[:, 0] * own, of[:, 1] * own, seen.astype(f32)]
-        return jnp.stack(table + [jnp.zeros_like(own)] * 4, axis=1)
+        table = jnp.stack([of[:, 0], of[:, 0] * own, of[:, 1] * own, seen.astype(f32)])
+        return jnp.broadcast_to(table[:, :, None], (4, rows, LANES))
 
     sel0, sel1 = selectors(rows0, 0), selectors(rows1, 1)
     gains = jnp.stack([shared_gain, shared_bias], axis=1)
@@ -901,15 +1006,14 @@
     part = parts(
         place, ((0, 2, True), (1, 3, True)), images, [m0, m1], dv_r
     )
+    part = place.scatter_core(part)
     dv_halo, part, shared_low = lax.optimization_barrier((dv_halo, part, shared_low))
-    part = place.scatter_core(part)
     (grad0,) = call(
         functools.partial(conv_back_kernel, images, 0), "masked_back0",
         [(dv_halo[0], "v"), (task_taps, "a")], [(tile1, f32)],
         shift=shift2, weights=1, back=True, limit=44,
     )
-    grad0, part = lax.optimization_barrier((grad0, part))
-    task_chunk = place.scatter_chips(part)
+    task_chunk, grad0 = place.scatter_chips(part, grad0)
     dy3, dyg0, dyg1, local = call(
         functools.partial(masked_back_kernel, images), "masked_back1",
         [
@@ -961,8 +1065,6 @@
         [(tile0, bf16)], limit=4,
     )
     (dv2_halo,) = place.halo([dv2], 2, images)
-    dv2_halo, part3 = lax.optimization_barrier((dv2_halo, part3))
-    chunk3 = place.scatter_chips(part3)
     dvh0, dvh1, grad_hidden = call(
         hidden_back_kernel, "hidden_back",
         [
@@ -971,6 +1073,17 @@
         ],
         [(tile1, bf16), (tile1, bf16), (tile1, f32)], limit=10,
     )
+    part2 = parts(
+        place,
+        ((0, 5, True), (0, 3, False), (1, 3, False), (0, 4, False), (2, 4, False)),
+        images, [act1, priors[0], priors[1]], [dvh0, dvh1, dv2],
+    )
+    part2 = place.scatter_core(part2)
+    dv2_halo, grad_hidden, part2, part3 = lax.optimization_barrier(
+        (dv2_halo, grad_hidden, part2, part3)
+    )
+    part = jnp.concatenate([part2[:TAPS], part3[TASKS:], part2[TAPS:], part3[:TASKS]])
+    part, _ = place.scatter_chips(part)
     dy1, local = call(
         functools.partial(second_back_kernel, images), "second_back",
         [
@@ -980,15 +1093,10 @@
         [(tile1, f32), ((1, 2, DOMAINS, c), f32)],
         shift=shift2, weights=1, back=True, limit=40,
     )
-    part2 = parts(
-        place,
-        ((0, 3, False), (1, 3, False), (0, 4, False), (2, 4, False), (0, 5, True)),
-        images, [act1, priors[0], priors[1]], [dvh0, dvh1, dv2],
-    )
-    part2 = place.scatter_core(part2)
-    local, part2, chunk3 = lax.optimization_barrier((local, part2, chunk3))
 
     sums1 = total_sums(place, local)
+    sums1, part = lax.optimization_barrier((sums1, part))
+    rest_rows = gather_rows(place, part)
     (dv1,) = call(
         functools.partial(back_kernel, 0, True), "first_dv",
         [
@@ -998,13 +1106,7 @@
         [(tile1, bf16)], limit=4,
     )
     part1 = place.scatter_core(parts(place, ((0, 1, True),), images, [features], [dv1]))
-    chunk1 = place.scatter_chips(jnp.concatenate([part1, part2[2 * TASKS :], part2[: 2 * TASKS]]))
-    rest_rows = gather_rows(
-        place,
-        jnp.concatenate(
-            [chunk1[: 2 * TAPS], chunk3[TASKS:], chunk1[2 * TAPS :], chunk3[:TASKS]]
-        ),
-    )
+    chunk1, _ = place.scatter_chips(part1)
     chunk1, dv1, p3, r0, r1, dvh0, dvh1 = lax.optimization_barrier(
         (chunk1, dv1, p3, r0, r1, dvh0, dvh1)
     )
@@ -1041,8 +1143,17 @@
         grad_priors.append(value.reshape(height, breadth, images, c).transpose(2, 0, 1, 3))
 
     (grad_task,) = spread(place, task_rows, 0, [TASKS * TAPS], 9)
-    (grad_shared,) = spread(place, rest_rows, 0, [CONVS * TAPS], 9)
-    grad_first, grad_second = spread(place, rest_rows, CONVS * TAPS, [2 * TASKS, TASKS], 3)
+    beside = (grad_task, shared_out, task_out, grad_features, grad_priors)
+    late = (CONVS - 1) * TAPS
+    if place.rows == 4 and place.cols == 8:
+        beside, *swapped = place.gather_swaps(chunk1, beside)
+        grad_task, shared_out, task_out, grad_features, grad_priors = beside
+        grad_shared = place_swapped(place, swapped, CONVS * TAPS, 3)
+    else:
+        (grad_shared,) = spread(place, gather_rows(place, chunk1), 0, [TAPS], 9)
+        grad_shared = jnp.pad(grad_shared, ((0, late), (0, 0), (0, 0)))
+    (grad_shared,) = spread(place, rest_rows, 0, [late], 9, grad_shared)
+    grad_first, grad_second = spread(place, rest_rows, late, [2 * TASKS, TASKS], 3)
 
     shared_sums = jnp.sum(jnp.stack([sums1[0], sums2[0], sums3[0]]), axis=2)
     task_sums = jnp.sum(jnp.stack([sums2[1:], sums3[1:], sums_r], axis=1), axis=3)

time: 572 us -> 509 us (0.89)
  Pallas kernels: 173 us -> 147 us
  local copies, waits for them, and re-layouts: 64.8 us -> 42.2 us
  other arithmetic: 37.5 us -> 24.7 us
  waiting for transfers between devices: 170 us -> 160 us
  starting transfers between devices: 95.9 us -> 104 us
    all_gather x2, waiting for transfers between devices: 66 us -> 0.02 us  [gather_rows(): whole = lax.all_gather(chunk, BOTH)]
    ppermute x69 -> x77, waiting for transfers between devices: 103 us -> 160 us  [swap(): return lax.ppermute(value, BOTH, pairs)]
    pallas_call x17, Pallas kernels: 133 us -> 106 us  [call(): pl.pallas_call(kernel, out_shape=[jax.ShapeDtypeStruct(*o) for o in outs]...]
    unnamed x277 -> x145, local copies, waits for them, and re-layouts: 40.7 us -> 31.1 us
    ppermute x6, starting transfers between devices: 9.67 us -> 16.4 us  [halo_rows(): lax.ppermute(jnp.where(even, high, low), 'row', [(i, i ^ 1) for i in rang...]
    ppermute x69 -> x77, starting transfers between devices: 81.4 us -> 82.9 us  [swap(): return lax.ppermute(value, BOTH, pairs)]
    pallas_call x3 -> x4, Pallas kernels: 32.5 us -> 32.9 us  [the longest x3 28.1 us: spread(): pl.pallas_call(functools.partial(spread_kernel, groups, sources, len(old)...]
  transfers between devices with their start and end apart: 83 -> 91, of which waited for: 35 -> 39; matrix products, arithmetic and copies ran while one was open for 10% -> 9% of each run, Pallas kernels for 23% -> 23%
where the time goes in v4:
time: 509 us; the launch traced here: 502 us
  waiting for transfers between devices  160 us (31%)
  Pallas kernels  147 us (29%)
  starting transfers between devices  104 us (20%)
  local copies, waits for them, and re-layouts  42.2 us (8%)
  other arithmetic  24.7 us (5%)
  between operations  16.8 us (3%)
  matrix products  7.24 us (1%)
    ppermute x77, waiting for transfers between devices, swap(): return lax.ppermute(value, BOTH, pairs)  160 us
    pallas_call x17, Pallas kernels, call(): pl.pallas_call(kernel, out_shape=[jax.ShapeDtypeStruct(*o) for o in outs]...  106 us
    ppermute x77, starting transfers between devices, swap(): return lax.ppermute(value, BOTH, pairs)  82.9 us
    unnamed x145, local copies, waits for them, and re-layouts  31.1 us
    pallas_call x3, Pallas kernels, spread(): pl.pallas_call(functools.partial(spread_kernel, groups, sources, len(old)...  28.1 us
    ppermute x6, starting transfers between devices, halo_rows(): lax.ppermute(jnp.where(even, high, low), 'row', [(i, i ^ 1) for i in rang...  16.4 us
  transfers between devices with their start and end apart: 91, of which 39 were waited for; matrix products, arithmetic and copies ran while one was open for 9% of the time, Pallas kernels for 23%

profile of v4, /device:TPU:0, one launch (start us, length us, event | category | flops | bytes accessed | tf_op | source)
XLA Modules:
  0.0 501.8 jit_solution(71425628498536189)
XLA Ops:
  8.3 4.0 collective-permute-start
  30.5 10.6 %collective-permute-done.6 = bf16[128,512]{1,0:T(8,128)(2,1)S(1)} collective-permute-done((bf16[128,512]{1,0:T(8,128)(2,1)S(1)}, bf16[128,512]{1,0:T(8,128)(2,1)S(1)}, u32[]{:S(2)}, u32[]{:S(2)}) %collective-permute-start.6) | collective-permute-done | bytes 131104 | tf_op jit(solution)/shard_map/ppermute | solution.py:37
  42.9 8.7 %first.1 = (f32[10,112,512]{2,1,0:T(8,128)S(1)}, f32[2,1,2,512]{3,2,1,0:T(2,128)S(1)}) custom-call(bf16[12,128,512]{2,1,0:T(8,128)(2,1)S(1)} %maximum_maximum_fusion.1.x_ref.refs_0_, bf16[27,512,512]{2,1,0:T(8,128)(2,1)} %bitcast.384, f32[4,112,128]{2,1,0:T(8,128)S(1)} %broadcast_in_dim.183.sel_ref, f32[6]{0:T(128)S(1)} %pad_maximum_fusion.44.scal_ref), custom_call_target="tpu_custom_call" | custom-call | tf_op jit(solution)/shard_map/first/pallas_call | solution.py:827
  67.2 6.8 %second.1 = (bf16[10,112,512]{2,1,0:T(8,128)(2,1)S(1)}, f32[8,96,512]{2,1,0:T(8,128)S(1)}, f32[2,1,2,512]{3,2,1,0:T(2,128)S(1)}) custom-call(f32[10,112,512]{2,1,0:T(8,128)S(1)} %get-tuple-element.106.p1_ref.p_ref, bf16[27,512,512]{2,1,0:T(8,128)(2,1)} %bitcast.385, f32[2,1,2,512]{3,2,1,0:T(2,128)S(1)} %pad_maximum_fusion.41.st1_ref.st_ref, ...), custom_call_target="tpu_custom_call" | custom-call | tf_op jit(solution)/shard_map/second/pallas_call | solution.py:827
  80.7 5.4 %hidden.1 = (f32[10,112,512]{2,1,0:T(8,128)S(1)}, f32[10,112,512]{2,1,0:T(8,128)S(1)}, f32[2,2,2,512]{3,2,1,0:T(2,128)S(1)}) custom-call(bf16[10,112,512]{2,1,0:T(8,128)(2,1)S(1)} %get-tuple-element.110.act_ref.refs_0_, bf16[2,10,112,512]{3,2,1,0:T(8,128)(2,1)S(1)} %maximum_maximum_fusion.pr_ref, bf16[2,1024,512]{2,1,0:T(8,128)(2,1)S(1)} %copy-done.19, ...), custom_call_target="tpu_custom_call" | custom-call | tf_op jit(solution)/shard_map/hidden/pallas_call | solution.py:827
  99.9 6.2 %gate.1 = (bf16[10,112,512]{2,1,0:T(8,128)(2,1)S(1)}, bf16[10,112,512]{2,1,0:T(8,128)(2,1)S(1)}, f32[10,112,512]{2,1,0:T(8,128)S(1)}, f32[10,112,512]{2,1,0:T(8,128)S(1)}, f32[2,2,2,512]{3,2,1,0:T(2,128)S(1)}) custom-call(f32[10,112,512]{2,1,0:T(8,128)S(1)} %get-tuple-element.121.h0_ref, f32[10,112,512]{2,1,0:T(8,128)S(1)} %get-tuple-element.122.h1_ref, ...), custom_call_target="tpu_custom_call" | custom-call | tf_op jit(solution)/shard_map/gate/pallas_call | solution.py:827
  112.0 4.0 collective-permute-done.24
  117.0 8.7 %third.1 = (f32[10,112,512]{2,1,0:T(8,128)S(1)}, f32[2,1,2,512]{3,2,1,0:T(2,128)S(1)}) custom-call(bf16[12,128,512]{2,1,0:T(8,128)(2,1)S(1)} %maximum_maximum_fusion.2.x_ref.refs_2_, bf16[27,512,512]{2,1,0:T(8,128)(2,1)} %bitcast.386, f32[4,112,128]{2,1,0:T(8,128)S(1)} %broadcast_in_dim.183.sel_ref, f32[6]{0:T(128)S(1)} %pad_maximum_fusion.44.scal_ref), custom_call_target="tpu_custom_call" | custom-call | tf_op jit(solution)/shard_map/third/pallas_call | solution.py:827
  135.5 14.6 %fourth.1 = (bf16[10,112,512]{2,1,0:T(8,128)(2,1)S(1)}, bf16[10,112,512]{2,1,0:T(8,128)(2,1)S(1)}, f32[8,96,512]{2,1,0:T(8,128)S(1)}, f32[8,96,512]{2,1,0:T(8,128)S(1)}, f32[2,2,2,512]{3,2,1,0:T(2,128)S(1)}) custom-call(f32[10,112,512]{2,1,0:T(8,128)S(1)} %get-tuple-element.181.p3_ref, f32[10,112,512]{2,1,0:T(8,128)} %copy-done.5, ...), custom_call_target="tpu_custom_call" | custom-call | tf_op jit(solution)/shard_map/fourth/pallas_call | solution.py:827
  182.0 7.8 %collective-permute-done.44 = bf16[192,512]{1,0:T(8,128)(2,1)S(1)} collective-permute-done((bf16[192,512]{1,0:T(8,128)(2,1)S(1)}, bf16[192,512]{1,0:T(8,128)(2,1)S(1)}, u32[]{:S(2)}, u32[]{:S(2)}) %collective-permute-start.44) | collective-permute-done | bytes 196640 | tf_op jit(solution)/shard_map/ppermute | solution.py:37
  190.2 6.9 %collective-permute-done.43 = bf16[96,512]{1,0:T(8,128)(2,1)S(1)} collective-permute-done((bf16[96,512]{1,0:T(8,128)(2,1)S(1)}, bf16[96,512]{1,0:T(8,128)(2,1)S(1)}, u32[]{:S(2)}, u32[]{:S(2)}) %collective-permute-start.43) | collective-permute-done | bytes 98336 | tf_op jit(solution)/shard_map/ppermute | solution.py:37
  200.6 7.2 %masked_back0.1.grad_ref = f32[10,112,512]{2,1,0:T(8,128)S(1)} custom-call(bf16[12,128,512]{2,1,0:T(8,128)(2,1)S(1)} %get-tuple-element.145.x_ref, bf16[18,512,512]{2,1,0:T(8,128)(2,1)} %bitcast.391), custom_call_target="tpu_custom_call" | custom-call | tf_op jit(solution)/shard_map/masked_back0/pallas_call | solution.py:827
  212.8 13.7 %masked_back1.1 = (f32[10,112,512]{2,1,0:T(8,128)S(1)}, f32[10,112,512]{2,1,0:T(8,128)S(1)}, f32[10,112,512]{2,1,0:T(8,128)S(1)}, f32[3,2,2,512]{3,2,1,0:T(2,128)S(1)}) custom-call(bf16[12,128,512]{2,1,0:T(8,128)(2,1)S(1)} %get-tuple-element.143.dv_ref, bf16[18,512,512]{2,1,0:T(8,128)(2,1)} %bitcast.392, f32[10,112,512]{2,1,0:T(8,128)S(1)} %masked_back0.1.grad_ref, ...), custom_call_target="tpu_custom_call" | custom-call | tf_op jit(solution)/shard_map/masked_back1/pallas_call | solution.py:827
  244.6 7.5 %third_back.1 = (bf16[10,112,512]{2,1,0:T(8,128)(2,1)S(1)}, f32[8,96,512]{2,1,0:T(8,128)S(1)}, f32[1,2,2,512]{3,2,1,0:T(2,128)S(1)}) custom-call(f32[10,112,512]{2,1,0:T(8,128)S(1)} %copy-done.33, f32[10,112,512]{2,1,0:T(8,128)S(1)} %get-tuple-element.181.p3_ref, f32[8,96,512]{2,1,0:T(8,128)S(1)} %copy-done.14, bf16[27,512,512]{2,1,0:T(8,128)(2,1)} %bitcast.387, ...), custom_call_target="tpu_custom_call" | custom-call | tf_op jit(solution)/shard_map/third_back/pallas_call | solution.py:827
  256.1 6.7 %gate_back.1 = (bf16[10,112,512]{2,1,0:T(8,128)(2,1)S(1)}, bf16[10,112,512]{2,1,0:T(8,128)(2,1)S(1)}, f32[10,112,512]{2,1,0:T(8,128)S(1)}, f32[10,112,512]{2,1,0:T(8,128)S(1)}, f32[2,2,2,512]{3,2,1,0:T(2,128)S(1)}) custom-call(f32[10,112,512]{2,1,0:T(8,128)S(1)} %copy-done.37, f32[10,112,512]{2,1,0:T(8,128)S(1)} %copy-done.39, ...), custom_call_target="tpu_custom_call" | custom-call | tf_op jit(solution)/shard_map/gate_back/pallas_call | solution.py:827
  280.2 4.1 hidden_back.1
  289.9 9.9 %collective-permute-done.65 = bf16[128,512]{1,0:T(8,128)(2,1)S(1)} collective-permute-done((bf16[128,512]{1,0:T(8,128)(2,1)S(1)}, bf16[128,512]{1,0:T(8,128)(2,1)S(1)}, u32[]{:S(2)}, u32[]{:S(2)}) %collective-permute-start.65) | collective-permute-done | bytes 131104 | tf_op jit(solution)/shard_map/ppermute | solution.py:37
  299.8 3.8 collective-permute-done.64
  308.5 8.8 %second_back.1 = (f32[10,112,512]{2,1,0:T(8,128)S(1)}, f32[1,2,2,512]{3,2,1,0:T(2,128)S(1)}) custom-call(bf16[12,128,512]{2,1,0:T(8,128)(2,1)S(1)} %maximum_maximum_fusion.5.dv2_ref, bf16[27,512,512]{2,1,0:T(8,128)(2,1)} %bitcast.388, f32[10,112,512]{2,1,0:T(8,128)S(1)} %get-tuple-element.169.add_ref, f32[10,112,512]{2,1,0:T(8,128)S(1)} %copy-done.1, ...), custom_call_target="tpu_custom_call" | custom-call | tf_op jit(solution)/shard_map/second_back/pallas_call | solution.py:827
  322.9 6.1 %collective-permute-done.73 = bf16[8,2,16,512]{3,2,0,1:T(8,128)(2,1)S(1)} collective-permute-done((bf16[8,2,16,512]{3,2,0,1:T(8,128)(2,1)S(1)}, bf16[8,2,16,512]{3,2,0,1:T(8,128)(2,1)S(1)}, u32[]{:S(2)}, u32[]{:S(2)}) %collective-permute-start.73) | collective-permute-done | bytes 262176 | tf_op jit(solution)/shard_map/ppermute | solution.py:37
  330.0 4.7 collective-permute-done.75
  334.7 8.3 %collective-permute-done.74 = bf16[16,16,512]{2,1,0:T(8,128)(2,1)S(1)} collective-permute-done((bf16[16,16,512]{2,1,0:T(8,128)(2,1)S(1)}, bf16[16,16,512]{2,1,0:T(8,128)(2,1)S(1)}, u32[]{:S(2)}, u32[]{:S(2)}) %collective-permute-start.74) | collective-permute-done | bytes 262176 | tf_op jit(solution)/shard_map/ppermute | solution.py:37
  354.8 10.6 %collective-permute-done.78 = bf16[3,2,16,512]{3,2,0,1:T(8,128)(2,1)S(1)} collective-permute-done((bf16[3,2,16,512]{3,2,0,1:T(8,128)(2,1)S(1)}, bf16[3,2,16,512]{3,2,0,1:T(8,128)(2,1)S(1)}, u32[]{:S(2)}, u32[]{:S(2)}) %collective-permute-start.78) | collective-permute-done | bytes 98336 | tf_op jit(solution)/shard_map/ppermute | solution.py:37
  369.7 4.0 collective-permute-done.79
  389.8 19.6 %collective-permute-done.82 = bf16[2,9,16,512]{3,2,1,0:T(8,128)(2,1)} collective-permute-done((bf16[2,9,16,512]{3,2,1,0:T(8,128)(2,1)}, bf16[2,9,16,512]{3,2,1,0:T(8,128)(2,1)}, u32[]{:S(2)}, u32[]{:S(2)}) %collective-permute-start.82) | collective-permute-done | bytes 294944 | tf_op jit(solution)/shard_map/ppermute | solution.py:37
  415.6 10.0 %collective-permute-done.83 = bf16[2,2,9,16,256]{4,3,2,1,0:T(8,128)(2,1)S(1)} collective-permute-done((bf16[2,2,9,16,256]{4,3,2,1,0:T(8,128)(2,1)S(1)}, bf16[2,2,9,16,256]{4,3,2,1,0:T(8,128)(2,1)S(1)}, u32[]{:S(2)}, u32[]{:S(2)}) %collective-permute-start.83) | collective-permute-done | bytes 294944 | tf_op jit(solution)/shard_map/ppermute | solution.py:37
  428.9 5.1 %fusion = f32[6,8,4,512]{3,0,2,1:T(8,128)} fusion(bf16[10,6,6,512]{3,2,1,0:T(8,128)(2,1)S(1)} %copy-done.51, bf16[3,3,3,512,512]{4,3,2,1,0:T(8,128)(2,1)} %param.16), kind=kOutput, calls=%fused_computation.2 | convolution fusion | flops 905969664 | bytes 5480448 | tf_op jit(solution)/shard_map/transpose | solution.py:1138
  433.9 19.9 %collective-permute-done.84 = bf16[2,2,2,9,16,256]{5,4,3,2,1,0:T(8,128)(2,1)S(1)} collective-permute-done((bf16[2,2,2,9,16,256]{5,4,3,2,1,0:T(8,128)(2,1)S(1)}, bf16[2,2,2,9,16,256]{5,4,3,2,1,0:T(8,128)(2,1)S(1)}, u32[]{:S(2)}, u32[]{:S(2)}) %collective-permute-start.84) | collective-permute-done | bytes 589856 | tf_op jit(solution)/shard_map/ppermute | solution.py:37
  454.8 11.5 %spread.3 = f32[18,512,512]{2,1,0:T(8,128)} custom-call(bf16[4,2,4,18,16,512]{5,4,3,2,1,0:T(8,128)(2,1)} %bitcast.393, bf16[4,2,4,18,16,512]{5,4,3,2,1,0:T(8,128)(2,1)} %bitcast.394), custom_call_target="tpu_custom_call" | custom-call | bytes 28311552 | tf_op jit(solution)/shard_map/spread/pallas_call | solution.py:748
  473.4 4.9 place.1.refs_2_
  478.2 5.2 %spread.5 = (f32[4,512,512]{2,1,0:T(8,128)}, f32[2,512,512]{2,1,0:T(8,128)}) custom-call(bf16[4,2,4,24,16,512]{5,4,3,2,1,0:T(8,128)(2,1)} %bitcast.378, bf16[4,2,4,24,16,512]{5,4,3,2,1,0:T(8,128)(2,1)} %bitcast.379, bf16[4,2,4,24,16,512]{5,4,3,2,1,0:T(8,128)(2,1)} %bitcast.380, bf16[4,2,4,24,16,512]{5,4,3,2,1,0:T(8,128)(2,1)} %bitcast.381), custom_call_target="tpu_custom_call" | custom-call | bytes 9437184 | tf_op jit(solution)/shard_map/spread/pallas_call | solution.py:748
  483.4 11.4 %spread.4 = f32[27,512,512]{2,1,0:T(8,128)} custom-call(bf16[4,2,4,24,16,512]{5,4,3,2,1,0:T(8,128)(2,1)} %bitcast.382, bf16[4,2,4,24,16,512]{5,4,3,2,1,0:T(8,128)(2,1)} %bitcast.383, f32[27,512,512]{2,1,0:T(8,128)} %place.1.refs_2_), custom_call_target="tpu_custom_call", output_to_operand_aliasing={{}: (2, {})} | custom-call | bytes 28311552 | tf_op jit(solution)/shard_map/spread/pallas_call | solution.py:748
  (575 shorter events, 218.3 us)
Async XLA Ops:
  7.2 447.5 %all-gather.5.cloned.1.call-start = ((), (), s32[]{:S(2)}) async-start(), calls=%async_computation | async-start | bytes 9732096 | tf_op jit(solution)/shard_map/all_gather | solution.py:808
  14.2 37.5 %collective-permute-start.7 = (bf16[2,8,24,512]{3,2,0,1:T(8,128)(2,1)S(1)}, bf16[2,8,24,512]{3,2,0,1:T(8,128)(2,1)S(1)}, u32[]{:S(2)}, u32[]{:S(2)}) collective-permute-start(bf16[2,8,24,512]{3,2,0,1:T(8,128)(2,1)S(1)} %copy.127), channel_id=1, source_target_pairs={{0,1},{1,0},{2,3},{3,2},{4,5},{5,4},{6,7},{7,6},{8,9},{9,8},{10,11... | collective-permute-start | bytes 1179656 | tf_op jit(solution)/shard_map/ppermute | solution.py:37
  16.1 35.6 %collective-permute-start.8 = (bf16[2,8,24,512]{3,2,0,1:T(8,128)(2,1)S(1)}, bf16[2,8,24,512]{3,2,0,1:T(8,128)(2,1)S(1)}, u32[]{:S(2)}, u32[]{:S(2)}) collective-permute-start(bf16[2,8,24,512]{3,2,0,1:T(8,128)(2,1)S(1)} %copy.127), channel_id=1, source_target_pairs={{0,2},{1,3},{2,0},{3,1},{4,6},{5,7},{6,4},{7,5},{8,10},{9,11},{10,... | collective-permute-start | bytes 1179656 | tf_op jit(solution)/shard_map/ppermute | solution.py:37
  20.2 31.6 %collective-permute-start.9 = (bf16[2,8,24,512]{3,2,0,1:T(8,128)(2,1)S(1)}, bf16[2,8,24,512]{3,2,0,1:T(8,128)(2,1)S(1)}, u32[]{:S(2)}, u32[]{:S(2)}) collective-permute-start(bf16[2,8,24,512]{3,2,0,1:T(8,128)(2,1)S(1)} %copy.127), channel_id=1, source_target_pairs={{0,3},{1,2},{2,1},{3,0},{4,7},{5,6},{6,5},{7,4},{8,11},{9,10},{10,... | collective-permute-start | bytes 1179656 | tf_op jit(solution)/shard_map/ppermute | solution.py:37
  26.8 14.3 %collective-permute-start.6 = (bf16[128,512]{1,0:T(8,128)(2,1)S(1)}, bf16[128,512]{1,0:T(8,128)(2,1)S(1)}, u32[]{:S(2)}, u32[]{:S(2)}) collective-permute-start(bf16[128,512]{1,0:T(8,128)(2,1)S(1)} %bitcast.438), channel_id=1, source_target_pairs={{0,4},{1,5},{2,6},{3,7},{4,0},{5,1},{6,2},{7,3},{8,12},{9,13},{10,... | collective-permute-start | bytes 393224 | tf_op jit(solution)/shard_map/ppermute | solution.py:37
  54.1 20.0 %collective-permute-start.14 = (bf16[1,2,1,96,512]{4,3,1,2,0:T(8,128)(2,1)S(1)}, bf16[1,2,1,96,512]{4,3,1,2,0:T(8,128)(2,1)S(1)}, u32[]{:S(2)}, u32[]{:S(2)}) collective-permute-start(bf16[1,2,1,96,512]{4,3,1,2,0:T(8,128)(2,1)S(1)} %get-tuple-element.274), channel_id=1, source_target_pairs={{8,16},{16,8},{9,17},{17,9},{10,18},{18,10},{11,19},{19,11},{12,20... | collective-permute-start | bytes 589832 | tf_op jit(solution)/shard_map/ppermute | solution.py:80
  55.0 19.1 %collective-permute-start.15 = (bf16[1,2,1,96,512]{4,3,1,2,0:T(8,128)(2,1)S(1)}, bf16[1,2,1,96,512]{4,3,1,2,0:T(8,128)(2,1)S(1)}, u32[]{:S(2)}, u32[]{:S(2)}) collective-permute-start(bf16[1,2,1,96,512]{4,3,1,2,0:T(8,128)(2,1)S(1)} %get-tuple-element.275), channel_id=1, source_target_pairs={{0,8},{8,0},{16,24},{24,16},{1,9},{9,1},{17,25},{25,17},{2,10},{10... | collective-permute-start | bytes 589832 | tf_op jit(solution)/shard_map/ppermute | solution.py:74
  95.1 14.8 %collective-permute-start.22 = (bf16[1,2,96,512]{3,2,1,0:T(8,128)(2,1)S(1)}, bf16[1,2,96,512]{3,2,1,0:T(8,128)(2,1)S(1)}, u32[]{:S(2)}, u32[]{:S(2)}) collective-permute-start(bf16[1,2,96,512]{3,2,1,0:T(8,128)(2,1)S(1)} %get-tuple-element.294), channel_id=1, source_target_pairs={{8,16},{16,8},{9,17},{17,9},{10,18},{18,10},{11,19},{19,11},{12,20... | collective-permute-start | bytes 589832 | tf_op jit(solution)/shard_map/ppermute | solution.py:80
  95.8 14.1 %collective-permute-start.23 = (bf16[1,2,96,512]{3,2,1,0:T(8,128)(2,1)S(1)}, bf16[1,2,96,512]{3,2,1,0:T(8,128)(2,1)S(1)}, u32[]{:S(2)}, u32[]{:S(2)}) collective-permute-start(bf16[1,2,96,512]{3,2,1,0:T(8,128)(2,1)S(1)} %get-tuple-element.295), channel_id=1, source_target_pairs={{0,8},{8,0},{16,24},{24,16},{1,9},{9,1},{17,25},{25,17},{2,10},{10... | collective-permute-start | bytes 589832 | tf_op jit(solution)/shard_map/ppermute | solution.py:74
  98.8 13.2 %collective-permute-start.25 = (bf16[128,512]{1,0:T(8,128)(2,1)S(1)}, bf16[128,512]{1,0:T(8,128)(2,1)S(1)}, u32[]{:S(2)}, u32[]{:S(2)}) collective-permute-start(bf16[128,512]{1,0:T(8,128)(2,1)S(1)} %bitcast.437), channel_id=1, source_target_pairs={{0,4},{1,5},{2,6},{3,7},{4,0},{5,1},{6,2},{7,3},{8,12},{9,13},{10,... | collective-permute-start | bytes 393224 | tf_op jit(solution)/shard_map/ppermute | solution.py:37
  131.9 18.3 %collective-permute-start.30 = (bf16[3,4,12,512]{3,2,1,0:T(8,128)(2,1)S(1)}, bf16[3,4,12,512]{3,2,1,0:T(8,128)(2,1)S(1)}, u32[]{:S(2)}, u32[]{:S(2)}) collective-permute-start(bf16[3,4,12,512]{3,2,1,0:T(8,128)(2,1)S(1)} %copy.139), channel_id=1, source_target_pairs={{0,1},{1,0},{2,3},{3,2},{4,5},{5,4},{6,7},{7,6},{8,9},{9,8},{10,11... | collective-permute-start | bytes 442376 | tf_op jit(solution)/shard_map/ppermute | solution.py:37
  132.4 17.8 %collective-permute-start.31 = (bf16[3,4,12,512]{3,2,1,0:T(8,128)(2,1)S(1)}, bf16[3,4,12,512]{3,2,1,0:T(8,128)(2,1)S(1)}, u32[]{:S(2)}, u32[]{:S(2)}) collective-permute-start(bf16[3,4,12,512]{3,2,1,0:T(8,128)(2,1)S(1)} %copy.139), channel_id=1, source_target_pairs={{0,2},{1,3},{2,0},{3,1},{4,6},{5,7},{6,4},{7,5},{8,10},{9,11},{10,... | collective-permute-start | bytes 442376 | tf_op jit(solution)/shard_map/ppermute | solution.py:37
  133.7 16.5 %collective-permute-start.32 = (bf16[3,4,12,512]{3,2,1,0:T(8,128)(2,1)S(1)}, bf16[3,4,12,512]{3,2,1,0:T(8,128)(2,1)S(1)}, u32[]{:S(2)}, u32[]{:S(2)}) collective-permute-start(bf16[3,4,12,512]{3,2,1,0:T(8,128)(2,1)S(1)} %copy.139), channel_id=1, source_target_pairs={{0,3},{1,2},{2,1},{3,0},{4,7},{5,6},{6,5},{7,4},{8,11},{9,10},{10,... | collective-permute-start | bytes 442376 | tf_op jit(solution)/shard_map/ppermute | solution.py:37
  150.7 19.1 %collective-permute-start.46 = (bf16[1,1,48,512]{3,2,1,0:T(8,128)(2,1)S(1)}, bf16[1,1,48,512]{3,2,1,0:T(8,128)(2,1)S(1)}, u32[]{:S(2)}, u32[]{:S(2)}) collective-permute-start(bf16[1,1,48,512]{3,2,1,0:T(8,128)(2,1)S(1)} %get-tuple-element.250), channel_id=1, source_target_pairs={{8,16},{16,8},{9,17},{17,9},{10,18},{18,10},{11,19},{19,11},{12,20... | collective-permute-start | bytes 147464 | tf_op jit(solution)/shard_map/ppermute | solution.py:80
  151.4 18.4 %collective-permute-start.47 = (bf16[1,1,48,512]{3,2,1,0:T(8,128)(2,1)S(1)}, bf16[1,1,48,512]{3,2,1,0:T(8,128)(2,1)S(1)}, u32[]{:S(2)}, u32[]{:S(2)}) collective-permute-start(bf16[1,1,48,512]{3,2,1,0:T(8,128)(2,1)S(1)} %broadcast_select_fusion.42), channel_id=1, source_target_pairs={{0,8},{8,0},{16,24},{24,16},{1,9},{9,1},{17,25},{25,17},{2,10},{10... | collective-permute-start | bytes 147464 | tf_op jit(solution)/shard_map/ppermute | solution.py:74
  174.3 15.5 %collective-permute-start.41 = (bf16[2,2,96,512]{3,2,1,0:T(8,128)(2,1)S(1)}, bf16[2,2,96,512]{3,2,1,0:T(8,128)(2,1)S(1)}, u32[]{:S(2)}, u32[]{:S(2)}) collective-permute-start(bf16[2,2,96,512]{3,2,1,0:T(8,128)(2,1)S(1)} %get-tuple-element.288), channel_id=1, source_target_pairs={{8,16},{16,8},{9,17},{17,9},{10,18},{18,10},{11,19},{19,11},{12,20... | collective-permute-start | bytes 1179656 | tf_op jit(solution)/shard_map/ppermute | solution.py:80
  175.0 14.8 %collective-permute-start.42 = (bf16[2,2,96,512]{3,2,1,0:T(8,128)(2,1)S(1)}, bf16[2,2,96,512]{3,2,1,0:T(8,128)(2,1)S(1)}, u32[]{:S(2)}, u32[]{:S(2)}) collective-permute-start(bf16[2,2,96,512]{3,2,1,0:T(8,128)(2,1)S(1)} %get-tuple-element.289), channel_id=1, source_target_pairs={{0,8},{8,0},{16,24},{24,16},{1,9},{9,1},{17,25},{25,17},{2,10},{10... | collective-permute-start | bytes 1179656 | tf_op jit(solution)/shard_map/ppermute | solution.py:74
  181.7 17.4 %collective-permute-start.45 = (bf16[18,2,2,16,512]{4,3,0,1,2:T(8,128)(2,1)S(1)}, bf16[18,2,2,16,512]{4,3,0,1,2:T(8,128)(2,1)S(1)}, u32[]{:S(2)}, u32[]{:S(2)}) collective-permute-start(bf16[18,2,2,16,512]{4,3,0,1,2:T(8,128)(2,1)S(1)} %fusion.3), channel_id=1, source_target_pairs={{0,8},{1,9},{2,10},{3,11},{4,12},{5,13},{6,14},{7,15},{8,0},{9,1},... | collective-permute-start | bytes 3538952 | tf_op jit(solution)/shard_map/ppermute | solution.py:37
  211.1 19.5 %collective-permute-start.53 = (bf16[6,16,512]{2,1,0:T(8,128)(2,1)S(1)}, bf16[6,16,512]{2,1,0:T(8,128)(2,1)S(1)}, u32[]{:S(2)}, u32[]{:S(2)}) collective-permute-start(bf16[6,16,512]{2,1,0:T(8,128)(2,1)S(1)} %fusion.43), channel_id=1, source_target_pairs={{0,16},{1,17},{2,18},{3,19},{4,20},{5,21},{6,22},{7,23},{8,24},{9,... | collective-permute-start | bytes 294920 | tf_op jit(solution)/shard_map/ppermute | solution.py:37
  212.7 18.0 %collective-permute-start.52 = (bf16[12,16,512]{2,1,0:T(8,128)(2,1)S(1)}, bf16[12,16,512]{2,1,0:T(8,128)(2,1)S(1)}, u32[]{:S(2)}, u32[]{:S(2)}) collective-permute-start(bf16[12,16,512]{2,1,0:T(8,128)(2,1)S(1)} %fusion.25), channel_id=1, source_target_pairs={{0,4},{1,5},{2,6},{3,7},{4,0},{5,1},{6,2},{7,3},{8,12},{9,13},{10,... | collective-permute-start | bytes 589832 | tf_op jit(solution)/shard_map/ppermute | solution.py:37
  231.5 246.7 %all-gather.7.cloned.1.call-start = ((), (), s32[]{:S(2)}) async-start(), calls=%async_computation.1 | async-start | bytes 12976128 | tf_op jit(solution)/shard_map/all_gather | solution.py:808
  271.4 33.1 %collective-permute-start.67 = (bf16[11,2,2,16,512]{4,3,0,1,2:T(8,128)(2,1)S(1)}, bf16[11,2,2,16,512]{4,3,0,1,2:T(8,128)(2,1)S(1)}, u32[]{:S(2)}, u32[]{:S(2)}) collective-permute-start(bf16[11,2,2,16,512]{4,3,0,1,2:T(8,128)(2,1)S(1)} %fusion.10), channel_id=1, source_target_pairs={{0,8},{1,9},{2,10},{3,11},{4,12},{5,13},{6,14},{7,15},{8,0},{9,1},... | collective-permute-start | bytes 2162696 | tf_op jit(solution)/shard_map/ppermute | solution.py:37
  280.1 19.7 %collective-permute-start.65 = (bf16[128,512]{1,0:T(8,128)(2,1)S(1)}, bf16[128,512]{1,0:T(8,128)(2,1)S(1)}, u32[]{:S(2)}, u32[]{:S(2)}) collective-permute-start(bf16[128,512]{1,0:T(8,128)(2,1)S(1)} %bitcast.436), channel_id=1, source_target_pairs={{0,4},{1,5},{2,6},{3,7},{4,0},{5,1},{6,2},{7,3},{8,12},{9,13},{10,... | collective-permute-start | bytes 393224 | tf_op jit(solution)/shard_map/ppermute | solution.py:37
  286.7 18.2 %collective-permute-start.66 = (bf16[13,2,2,16,512]{4,3,0,1,2:T(8,128)(2,1)S(1)}, bf16[13,2,2,16,512]{4,3,0,1,2:T(8,128)(2,1)S(1)}, u32[]{:S(2)}, u32[]{:S(2)}) collective-permute-start(bf16[13,2,2,16,512]{4,3,0,1,2:T(8,128)(2,1)S(1)} %fusion.9), channel_id=1, source_target_pairs={{0,8},{1,9},{2,10},{3,11},{4,12},{5,13},{6,14},{7,15},{8,0},{9,1},... | collective-permute-start | bytes 2555912 | tf_op jit(solution)/shard_map/ppermute | solution.py:37
  286.9 16.7 %collective-permute-start.64 = (bf16[64,512]{1,0:T(8,128)(2,1)S(1)}, bf16[64,512]{1,0:T(8,128)(2,1)S(1)}, u32[]{:S(2)}, u32[]{:S(2)}) collective-permute-start(bf16[64,512]{1,0:T(8,128)(2,1)S(1)} %bitcast.445), channel_id=1, source_target_pairs={{0,4},{1,5},{2,6},{3,7},{4,0},{5,1},{6,2},{7,3},{8,12},{9,13},{10,... | collective-permute-start | bytes 196616 | tf_op jit(solution)/shard_map/ppermute | solution.py:37
  306.6 22.5 %collective-permute-start.72 = (bf16[16,2,16,512]{3,2,0,1:T(8,128)(2,1)S(1)}, bf16[16,2,16,512]{3,2,0,1:T(8,128)(2,1)S(1)}, u32[]{:S(2)}, u32[]{:S(2)}) collective-permute-start(bf16[16,2,16,512]{3,2,0,1:T(8,128)(2,1)S(1)} %fusion.12), channel_id=1, source_target_pairs={{0,16},{1,17},{2,18},{3,19},{4,20},{5,21},{6,22},{7,23},{8,24},{9,... | collective-permute-start | bytes 1572872 | tf_op jit(solution)/shard_map/ppermute | solution.py:37
  307.8 21.2 %collective-permute-start.73 = (bf16[8,2,16,512]{3,2,0,1:T(8,128)(2,1)S(1)}, bf16[8,2,16,512]{3,2,0,1:T(8,128)(2,1)S(1)}, u32[]{:S(2)}, u32[]{:S(2)}) collective-permute-start(bf16[8,2,16,512]{3,2,0,1:T(8,128)(2,1)S(1)} %fusion.21), channel_id=1, source_target_pairs={{0,4},{1,5},{2,6},{3,7},{4,0},{5,1},{6,2},{7,3},{8,12},{9,13},{10,... | collective-permute-start | bytes 786440 | tf_op jit(solution)/shard_map/ppermute | solution.py:37
  384.7 24.7 %collective-permute-start.82 = (bf16[2,9,16,512]{3,2,1,0:T(8,128)(2,1)}, bf16[2,9,16,512]{3,2,1,0:T(8,128)(2,1)}, u32[]{:S(2)}, u32[]{:S(2)}) collective-permute-start(bf16[2,9,16,512]{3,2,1,0:T(8,128)(2,1)} %get-tuple-element.327), channel_id=1, source_target_pairs={{0,4},{1,5},{2,6},{3,7},{4,0},{5,1},{6,2},{7,3},{8,12},{9,13},{10,... | collective-permute-start | bytes 884744 | tf_op jit(solution)/shard_map/ppermute | solution.py:37
  410.5 15.0 %collective-permute-start.83 = (bf16[2,2,9,16,256]{4,3,2,1,0:T(8,128)(2,1)S(1)}, bf16[2,2,9,16,256]{4,3,2,1,0:T(8,128)(2,1)S(1)}, u32[]{:S(2)}, u32[]{:S(2)}) collective-permute-start(bf16[2,2,9,16,256]{4,3,2,1,0:T(8,128)(2,1)S(1)} %get-tuple-element.307), channel_id=1, source_target_pairs={{0,16},{1,17},{2,18},{3,19},{4,20},{5,21},{6,22},{7,23},{8,24},{9,... | collective-permute-start | bytes 884744 | tf_op jit(solution)/shard_map/ppermute | solution.py:37
  412.1 15.8 %collective-permute-start.85 = (bf16[2,2,9,16,256]{4,3,2,1,0:T(8,128)(2,1)S(1)}, bf16[2,2,9,16,256]{4,3,2,1,0:T(8,128)(2,1)S(1)}, u32[]{:S(2)}, u32[]{:S(2)}) collective-permute-start(bf16[2,2,9,16,256]{4,3,2,1,0:T(8,128)(2,1)S(1)} %get-tuple-element.306), channel_id=1, source_target_pairs={{0,1},{1,0},{2,3},{3,2},{4,5},{5,4},{6,7},{7,6},{8,9},{9,8},{10,11... | collective-permute-start | bytes 884744 | tf_op jit(solution)/shard_map/ppermute | solution.py:37
  425.7 28.2 %collective-permute-start.84 = (bf16[2,2,2,9,16,256]{5,4,3,2,1,0:T(8,128)(2,1)S(1)}, bf16[2,2,2,9,16,256]{5,4,3,2,1,0:T(8,128)(2,1)S(1)}, u32[]{:S(2)}, u32[]{:S(2)}) collective-permute-start(bf16[2,2,2,9,16,256]{5,4,3,2,1,0:T(8,128)(2,1)S(1)} %get-tuple-element.309), channel_id=1, source_target_pairs={{0,1},{1,0},{2,3},{3,2},{4,5},{5,4},{6,7},{7,6},{8,9},{9,8},{10,11... | collective-permute-start | bytes 1769480 | tf_op jit(solution)/shard_map/ppermute | solution.py:37
  428.0 26.6 %collective-permute-start.86 = (bf16[2,2,2,9,16,256]{5,4,3,2,1,0:T(8,128)(2,1)S(1)}, bf16[2,2,2,9,16,256]{5,4,3,2,1,0:T(8,128)(2,1)S(1)}, u32[]{:S(2)}, u32[]{:S(2)}) collective-permute-start(bf16[2,2,2,9,16,256]{5,4,3,2,1,0:T(8,128)(2,1)S(1)} %get-tuple-element.305), channel_id=1, source_target_pairs={{0,16},{1,17},{2,18},{3,19},{4,20},{5,21},{6,22},{7,23},{8,24},{9,... | collective-permute-start | bytes 1769480 | tf_op jit(solution)/shard_map/ppermute | solution.py:37
  (127 other events, 883.5 us)
Sparse Core Ops, SparseCore 0:
  231.7 97.9 all-gather.4
  344.0 126.9 all-gather.6
